TPU v7x, 32 devices: a whole 2x2x4 slice. The times are simulated.
32 devices in a mesh: dp: 4 (over z), expert: 8 (over y, x, core).
Axes of the slice: x: 2, y: 2, z: 4, core: 2. Of those that a mesh axis runs over, the one named last changes fastest.
Arguments:
- tokens: bfloat16 [4096, 1280], P(('dp', 'expert')), may hold values from -6 to 6
- cotangent: bfloat16 [4096, 1280], P(('dp', 'expert')), may hold values from -6 to 6
- routes: int32 [4096, 7], P(('dp', 'expert')), may hold values from 0 to 31, all different within a row; in each aligned block of 128 rows (0 to 127, 128 to 255, ...) at most 48 rows name the same one
- doc_ids: int32 [32, 128], P(('dp', 'expert')), may hold values from 0 to 3, never falling along the last dimension, each value on 1 to 64 neighbouring positions
- attn_weight: float32 [4, 1280, 1280], P(None, ('dp', 'expert')), may hold values from -0.15625 to 0.15625
- attn_momentum: float32 [4, 1280, 1280], P(None, ('dp', 'expert')), may hold values from -384 to 384
- attn_average: float32 [4, 1280, 1280], P(None, ('dp', 'expert')), may hold values from -0.15625 to 0.15625
- shared_weight: float32 [3, 1280, 896], P(None, ('dp', 'expert')), may hold values from -0.15625 to 0.15625
- shared_momentum: float32 [3, 1280, 896], P(None, ('dp', 'expert')), may hold values from -192 to 192
- shared_average: float32 [3, 1280, 896], P(None, ('dp', 'expert')), may hold values from -0.15625 to 0.15625
- router_weight: float32 [1280, 32], P(('dp', 'expert')), may hold values from -0.078125 to 0.078125
- router_momentum: float32 [1280, 32], P(('dp', 'expert')), may hold values from -512 to 512
- router_average: float32 [1280, 32], P(('dp', 'expert')), may hold values from -0.078125 to 0.078125
- gain_weight: float32 [2, 1280], P(None, ('dp', 'expert')), may hold values from 0.5 to 1.5
- gain_momentum: float32 [2, 1280], P(None, ('dp', 'expert')), may hold values from -384 to 384
- gain_average: float32 [2, 1280], P(None, ('dp', 'expert')), may hold values from 0.1 to 1.9
- expert_weight: float32 [32, 3, 1280, 896], P('expert', None, 'dp'), may hold values from -0.15625 to 0.15625
- expert_momentum: float32 [32, 3, 1280, 896], P('expert', None, 'dp'), may hold values from -16 to 16
- expert_average: float32 [32, 3, 1280, 896], P('expert', None, 'dp'), may hold values from -0.15625 to 0.15625
Outputs:
- layer_out: bfloat16 [4096, 1280], P(('dp', 'expert'))
- input_grad: float32 [4096, 1280], P(('dp', 'expert'))
- attn_new: float32 [4, 1280, 1280], P(None, ('dp', 'expert'))
- attn_moment: float32 [4, 1280, 1280], P(None, ('dp', 'expert'))
- attn_mean: float32 [4, 1280, 1280], P(None, ('dp', 'expert'))
- shared_new: float32 [3, 1280, 896], P(None, ('dp', 'expert'))
- shared_moment: float32 [3, 1280, 896], P(None, ('dp', 'expert'))
- shared_mean: float32 [3, 1280, 896], P(None, ('dp', 'expert'))
- router_new: float32 [1280, 32], P(('dp', 'expert'))
- router_moment: float32 [1280, 32], P(('dp', 'expert'))
- router_mean: float32 [1280, 32], P(('dp', 'expert'))
- gain_new: float32 [2, 1280], P(None, ('dp', 'expert'))
- gain_moment: float32 [2, 1280], P(None, ('dp', 'expert'))
- gain_mean: float32 [2, 1280], P(None, ('dp', 'expert'))
- expert_new: float32 [32, 3, 1280, 896], P('expert', None, 'dp')
- expert_moment: float32 [32, 3, 1280, 896], P('expert', None, 'dp')
- expert_mean: float32 [32, 3, 1280, 896], P('expert', None, 'dp')
- sublayer_rms: float32 [32, 2], P(('dp', 'expert'))
Inputs may be any that keep to these rules, and one draw needn't show every extreme that they name: `routes`: each row names 7 different experts; in each aligned block of 128 rows (one sequence) no expert is named more than 48 times, a bound that some block reaches. `doc_ids`: never falls along a sequence; each of the 4 documents holds 1 to 64 positions.
All inputs are finite; a program needn't handle non-finite values.
Results may differ from a plain program's by a relative error of at most 0.012.
Values may be sent and summed in bfloat16 or wider, within the bound.
No kernel may reach another device: no remote copies, remote signals or barrier semaphores. Data moves between devices by JAX's collectives and lax.ppermute only.
A program may use at most 384 MiB of HBM per device.

v0:
```python
import math

import jax
import jax.numpy as jnp
from jax import lax
from jax.sharding import PartitionSpec as P

HEADS = 10
HD = 128
TOPK = 7
STEP = 3


epsilon = 1e-06
momentum_decay = 0.9
masked_score = -1e30
highest = lax.Precision.HIGHEST
rate_attn = 5e-05
rate_output = 0.0002
rate_shared = 0.0001
rate_router = 3e-05
rate_gain = 0.002
rate_expert = 0.0015


def swish(value_in):
    return value_in * jax.nn.sigmoid(value_in)


def swish_back(pair, hidden_grad):
    gate_in = pair[0]
    up_in = pair[1]
    sigmoid_g = jax.nn.sigmoid(gate_in)
    gate_grad = hidden_grad * up_in * sigmoid_g * (1.0 + gate_in * (1.0 - sigmoid_g))
    up_grad = hidden_grad * gate_in * sigmoid_g
    return jnp.stack([gate_grad, up_grad])


def rope_tables(length, size):
    half = size // 2
    freq = jnp.exp(jnp.arange(half, dtype=jnp.float32) * (-2.0 * math.log(10000.0) / size))
    angle = jnp.arange(length, dtype=jnp.float32)[:, None] * freq[None, :]
    cosine = jnp.concatenate([jnp.cos(angle), jnp.cos(angle)], -1)
    sine = jnp.concatenate([jnp.sin(angle), jnp.sin(angle)], -1)
    return (cosine, sine)


def rotate(heads_in, cosine, sine):
    half = heads_in.shape[-1] // 2
    turned = jnp.concatenate([-heads_in[..., half:], heads_in[..., :half]], -1)
    return heads_in * cosine[:, None, :] + turned * sine[:, None, :]


def rotate_back(grads_in, cosine, sine):
    half = grads_in.shape[-1] // 2
    scaled = grads_in * sine[:, None, :]
    turned = jnp.concatenate([scaled[..., half:], -scaled[..., :half]], -1)
    return grads_in * cosine[:, None, :] + turned


def destinations(routes_in, capacity, experts):
    flat = routes_in.reshape(-1)
    onehot = (flat[:, None] == jnp.arange(experts, dtype=jnp.int32)[None, :]).astype(jnp.int32)
    before = jnp.cumsum(onehot, 0) - onehot
    slot = jnp.sum(before * onehot, 1)
    return flat * capacity + slot


def update(weight, moment, average, grad, rate):
    moment_new = momentum_decay * moment + grad
    weight_new = weight - rate * (grad + momentum_decay * moment_new)
    average_new = average + (weight_new - average) / (STEP + 1.0)
    return (weight_new, moment_new, average_new)


def expert_front(rows, weights):
    pair = jnp.einsum("erd,emdf->merf", rows, weights[:, :2], preferred_element_type=jnp.float32)
    hidden = (swish(pair[0]) * pair[1]).astype(jnp.bfloat16)
    return (pair, hidden)


def body(
    tokens,
    cotangent,
    routes,
    doc_ids,
    attn_weight,
    attn_momentum,
    attn_average,
    shared_weight,
    shared_momentum,
    shared_average,
    router_weight,
    router_momentum,
    router_average,
    gain_weight,
    gain_momentum,
    gain_average,
    expert_weight,
    expert_momentum,
    expert_average,
):
    attn_w, shared_w, router_w, gain_w = (
        lax.all_gather(attn_weight.astype(jnp.bfloat16), ("dp", "expert"), axis=1, tiled=True),
        lax.all_gather(shared_weight.astype(jnp.bfloat16), ("dp", "expert"), axis=1, tiled=True),
        lax.all_gather(router_weight.astype(jnp.bfloat16), ("dp", "expert"), axis=0, tiled=True),
        lax.all_gather(gain_weight.astype(jnp.bfloat16), ("dp", "expert"), axis=1, tiled=True),
    )
    gain_vals = gain_w.astype(jnp.float32)
    inputs = tokens.astype(jnp.float32)
    length = inputs.shape[0]
    model_width = inputs.shape[1]
    experts = router_w.shape[1]
    capacity = min(length, (length * TOPK * 3 // (2 * experts) + 7) // 8 * 8)
    dp_count = lax.axis_size("dp")
    local_experts = expert_weight.shape[0]
    documents = doc_ids[0]
    cosine, sine = rope_tables(length, HD)
    score_scale = HD ** (-0.5)
    position = jnp.arange(length)
    allowed = (
        (position[None, :] <= position[:, None]) & (documents[None, :] == documents[:, None])
    )[None]
    work_w = lax.all_gather(expert_weight.astype(jnp.bfloat16), "dp", axis=2, tiled=True)
    inv_first = lax.rsqrt(jnp.mean(inputs * inputs, -1, keepdims=True) + epsilon)
    unit_first = inputs * inv_first
    normed = (unit_first * gain_vals[0]).astype(jnp.bfloat16)
    projected = jnp.einsum("ld,mde->mle", normed, attn_w[:3], preferred_element_type=jnp.float32)
    query = rotate(projected[0].reshape(length, HEADS, HD), cosine, sine).astype(jnp.bfloat16)
    key_rot = rotate(projected[1].reshape(length, HEADS, HD), cosine, sine).astype(jnp.bfloat16)
    values = projected[2].astype(jnp.bfloat16).reshape(length, HEADS, HD)

    def scores_of(query_in, keys_in):
        raw = (
            jnp.einsum("ihd,jhd->hij", query_in, keys_in, preferred_element_type=jnp.float32)
            * score_scale
        )
        return jnp.where(allowed, raw, masked_score)

    scores = scores_of(query, key_rot)
    row_max = jnp.max(scores, -1, keepdims=True)
    exponent = jnp.exp(scores - row_max)
    row_total = jnp.sum(exponent, -1, keepdims=True)
    attn_probs = exponent / row_total
    log_total = row_max + jnp.log(row_total)
    heads_out = jnp.einsum(
        "hij,jhd->ihd", attn_probs.astype(jnp.bfloat16), values, preferred_element_type=jnp.float32
    )
    heads_out = heads_out.reshape(length, model_width).astype(jnp.bfloat16)
    attn_out = jnp.dot(heads_out, attn_w[3], preferred_element_type=jnp.float32)
    middle = inputs + attn_out
    inv_second = lax.rsqrt(jnp.mean(middle * middle, -1, keepdims=True) + epsilon)
    unit_second = middle * inv_second
    inner = (unit_second * gain_vals[1]).astype(jnp.bfloat16)
    logits = jnp.dot(inner, router_w, preferred_element_type=jnp.float32)
    route_hot = (routes[:, :, None] == jnp.arange(experts, dtype=jnp.int32)[None, None, :]).astype(
        jnp.float32
    )
    chosen = jnp.sum(route_hot * logits[:, None, :], -1)
    gate_probs = jax.nn.softmax(chosen, axis=-1)
    shared_pair = jnp.einsum("ld,mdf->mlf", inner, shared_w[:2], preferred_element_type=jnp.float32)
    shared_hidden = (swish(shared_pair[0]) * shared_pair[1]).astype(jnp.bfloat16)
    shared_out = jnp.einsum(
        "lf,df->ld", shared_hidden, shared_w[2], preferred_element_type=jnp.float32
    )
    target = destinations(routes, capacity, experts)
    source = jnp.arange(length * TOPK) // TOPK
    outbound = (
        jnp.zeros((experts * capacity, model_width), jnp.bfloat16).at[target].set(inner[source])
    )
    received = lax.all_to_all(
        outbound.reshape(experts, capacity, model_width),
        "expert",
        split_axis=0,
        concat_axis=1,
        tiled=True,
    )
    expert_pair, expert_hidden = expert_front(received, work_w)
    expert_out = jnp.einsum(
        "erf,edf->erd", expert_hidden, work_w[:, 2], preferred_element_type=jnp.float32
    ).astype(jnp.bfloat16)
    returned = lax.all_to_all(
        expert_out, "expert", split_axis=1, concat_axis=0, tiled=True
    ).reshape(experts * capacity, model_width)
    picked = returned[target].reshape(length, TOPK, model_width).astype(jnp.float32)
    routed = jnp.sum(gate_probs[:, :, None] * picked, 1)
    branch = shared_out + routed
    layer_out = (middle + branch).astype(jnp.bfloat16)
    first_mask = jnp.concatenate([jnp.ones((1,), bool), documents[1:] != documents[:-1]])
    kept_mask = 1.0 - first_mask.astype(jnp.float32)
    kept_count = jnp.sum(kept_mask)
    attn_rms = jnp.sqrt(
        jnp.sum(kept_mask[:, None] * attn_out * attn_out) / (kept_count * model_width)
    )
    branch_rms = jnp.sqrt(
        jnp.sum(kept_mask[:, None] * branch * branch) / (kept_count * model_width)
    )
    sublayer_rms = jnp.stack([attn_rms, branch_rms])[None, :]
    upstream = cotangent.astype(jnp.float32)
    gate_grad = jnp.sum(picked * upstream[:, None, :], -1)
    slot_grad = (
        (gate_probs[:, :, None] * upstream[:, None, :])
        .astype(jnp.bfloat16)
        .reshape(length * TOPK, model_width)
    )
    inbound = jnp.zeros((experts * capacity, model_width), jnp.bfloat16).at[target].set(slot_grad)
    out_grad = lax.all_to_all(
        inbound.reshape(experts, capacity, model_width),
        "expert",
        split_axis=0,
        concat_axis=1,
        tiled=True,
    )
    back_pair, back_hidden = (expert_pair, expert_hidden)
    hidden_grad = jnp.einsum(
        "erd,edf->erf", out_grad, work_w[:, 2], preferred_element_type=jnp.float32
    )
    down_grad = jnp.einsum(
        "erf,erd->edf", back_hidden, out_grad, preferred_element_type=jnp.float32
    )
    pair_grad = swish_back(back_pair, hidden_grad).astype(jnp.bfloat16)
    front_grad = jnp.einsum(
        "erd,merf->emdf", received, pair_grad, preferred_element_type=jnp.float32
    )
    rows_grad = jnp.einsum(
        "merf,emdf->erd", pair_grad, work_w[:, :2], preferred_element_type=jnp.float32
    ).astype(jnp.bfloat16)
    sent_grad = lax.all_to_all(
        rows_grad, "expert", split_axis=1, concat_axis=0, tiled=True
    ).reshape(experts * capacity, model_width)
    routed_grad = jnp.sum(
        sent_grad[target].reshape(length, TOPK, model_width).astype(jnp.float32), 1
    )
    chosen_grad = gate_probs * (gate_grad - jnp.sum(gate_probs * gate_grad, -1, keepdims=True))
    logit_grad = jnp.sum(route_hot * chosen_grad[:, :, None], 1)
    inner_wide = inner.astype(jnp.float32)
    router_grad = jnp.dot(inner_wide.T, logit_grad, precision=highest)
    router_back = jnp.dot(logit_grad, router_w.astype(jnp.float32).T, precision=highest)
    shared_hidden_grad = jnp.dot(cotangent, shared_w[2], preferred_element_type=jnp.float32)
    shared_down_grad = jnp.einsum(
        "ld,lf->df", cotangent, shared_hidden, preferred_element_type=jnp.float32
    )
    shared_pair_grad = swish_back(shared_pair, shared_hidden_grad).astype(jnp.bfloat16)
    shared_front_grad = jnp.einsum(
        "ld,mlf->mdf", inner, shared_pair_grad, preferred_element_type=jnp.float32
    )
    shared_back = jnp.einsum(
        "mlf,mdf->ld", shared_pair_grad, shared_w[:2], preferred_element_type=jnp.float32
    )
    inner_grad = routed_grad + router_back + shared_back
    scaled_second = inner_grad * gain_vals[1]
    second_gain_grad = jnp.sum(inner_grad * unit_second, 0)
    middle_grad = upstream + inv_second * (
        scaled_second - unit_second * jnp.mean(scaled_second * unit_second, -1, keepdims=True)
    )
    attn_grad = middle_grad.astype(jnp.bfloat16)
    output_grad = jnp.einsum("li,lo->io", heads_out, attn_grad, preferred_element_type=jnp.float32)
    heads_grad = jnp.einsum("lo,io->li", attn_grad, attn_w[3], preferred_element_type=jnp.float32)
    heads_grad = heads_grad.astype(jnp.bfloat16).reshape(length, HEADS, HD)
    probs_again = jnp.exp(scores_of(query, key_rot) - log_total)
    value_grad = jnp.einsum(
        "hij,ihd->jhd",
        probs_again.astype(jnp.bfloat16),
        heads_grad,
        preferred_element_type=jnp.float32,
    ).astype(jnp.bfloat16)
    prob_grad = jnp.einsum("ihd,jhd->hij", heads_grad, values, preferred_element_type=jnp.float32)
    score_grad = (
        probs_again * (prob_grad - jnp.sum(probs_again * prob_grad, -1, keepdims=True))
    ).astype(jnp.bfloat16)
    query_grad = (
        jnp.einsum("hij,jhd->ihd", score_grad, key_rot, preferred_element_type=jnp.float32)
        * score_scale
    )
    query_grad = rotate_back(query_grad, cosine, sine).astype(jnp.bfloat16)
    key_grad = (
        jnp.einsum("hij,ihd->jhd", score_grad, query, preferred_element_type=jnp.float32)
        * score_scale
    )
    key_grad = rotate_back(key_grad, cosine, sine).astype(jnp.bfloat16)
    proj_grad = jnp.stack(
        [
            query_grad.reshape(length, model_width),
            key_grad.reshape(length, model_width),
            value_grad.reshape(length, model_width),
        ]
    )
    qkv_grad = jnp.einsum("ld,mle->mde", normed, proj_grad, preferred_element_type=jnp.float32)
    normed_grad = jnp.einsum(
        "mle,mde->ld", proj_grad, attn_w[:3], preferred_element_type=jnp.float32
    )
    scaled_first = normed_grad * gain_vals[0]
    first_gain_grad = jnp.sum(normed_grad * unit_first, 0)
    input_grad = middle_grad + inv_first * (
        scaled_first - unit_first * jnp.mean(scaled_first * unit_first, -1, keepdims=True)
    )
    expert_all = jnp.concatenate([front_grad, down_grad[:, None]], 1)
    split_view = expert_all.reshape(
        local_experts, 3, dp_count, model_width // dp_count, expert_all.shape[3]
    )
    from_sources = lax.all_to_all(
        split_view.astype(jnp.bfloat16), "dp", split_axis=2, concat_axis=2, tiled=True
    ).astype(split_view.dtype)
    expert_sum = jnp.sum(from_sources, 2)
    attn_all = jnp.concatenate([qkv_grad, output_grad[None]], 0)
    shared_all = jnp.concatenate([shared_front_grad, shared_down_grad[None]], 0)
    gain_all = jnp.stack([first_gain_grad, second_gain_grad])
    attn_sum, shared_sum, router_sum, gain_sum = (
        lax.psum_scatter(attn_all, ("dp", "expert"), scatter_dimension=1, tiled=True),
        lax.psum_scatter(shared_all, ("dp", "expert"), scatter_dimension=1, tiled=True),
        lax.psum_scatter(router_grad, ("dp", "expert"), scatter_dimension=0, tiled=True),
        lax.psum_scatter(gain_all, ("dp", "expert"), scatter_dimension=1, tiled=True),
    )
    attn_rates = jnp.array([rate_attn, rate_attn, rate_attn, rate_output], jnp.float32).reshape(
        4, 1, 1
    )
    attn_new, attn_moment, attn_mean = update(
        attn_weight, attn_momentum, attn_average, attn_sum, attn_rates
    )
    shared_new, shared_moment, shared_mean = update(
        shared_weight, shared_momentum, shared_average, shared_sum, rate_shared
    )
    router_new, router_moment, router_mean = update(
        router_weight, router_momentum, router_average, router_sum, rate_router
    )
    gain_new, gain_moment, gain_mean = update(
        gain_weight, gain_momentum, gain_average, gain_sum, rate_gain
    )
    expert_new, expert_moment, expert_mean = update(
        expert_weight, expert_momentum, expert_average, expert_sum, rate_expert
    )
    return (
        layer_out,
        input_grad,
        attn_new,
        attn_moment,
        attn_mean,
        shared_new,
        shared_moment,
        shared_mean,
        router_new,
        router_moment,
        router_mean,
        gain_new,
        gain_moment,
        gain_mean,
        expert_new,
        expert_moment,
        expert_mean,
        sublayer_rms,
    )


def solution(mesh):
    return jax.shard_map(
        body,
        mesh=mesh,
        in_specs=(
            P(("dp", "expert"), None),
            P(("dp", "expert"), None),
            P(("dp", "expert"), None),
            P(("dp", "expert"), None),
            P(None, ("dp", "expert"), None),
            P(None, ("dp", "expert"), None),
            P(None, ("dp", "expert"), None),
            P(None, ("dp", "expert"), None),
            P(None, ("dp", "expert"), None),
            P(None, ("dp", "expert"), None),
            P(("dp", "expert"), None),
            P(("dp", "expert"), None),
            P(("dp", "expert"), None),
            P(None, ("dp", "expert")),
            P(None, ("dp", "expert")),
            P(None, ("dp", "expert")),
            P("expert", None, "dp", None),
            P("expert", None, "dp", None),
            P("expert", None, "dp", None),
        ),
        out_specs=(
            P(("dp", "expert"), None),
            P(("dp", "expert"), None),
            P(None, ("dp", "expert"), None),
            P(None, ("dp", "expert"), None),
            P(None, ("dp", "expert"), None),
            P(None, ("dp", "expert"), None),
            P(None, ("dp", "expert"), None),
            P(None, ("dp", "expert"), None),
            P(("dp", "expert"), None),
            P(("dp", "expert"), None),
            P(("dp", "expert"), None),
            P(None, ("dp", "expert")),
            P(None, ("dp", "expert")),
            P(None, ("dp", "expert")),
            P("expert", None, "dp", None),
            P("expert", None, "dp", None),
            P("expert", None, "dp", None),
            P(("dp", "expert"), None),
        ),
        check_vma=False,
    )
```

profile of v0, /device:TPU:16, one launch (start us, length us, event | category | flops | bytes accessed | tf_op | source)
XLA Modules:
  0.0 2095.3 jit_solution(14882631195140708919)
XLA Ops:
  7.2 1.9 convert_element_type.146
  9.2 8.8 convert_element_type.161
  19.3 31.8 %all-gather = bf16[32,40,2]{1,2,0:T(2,128)(2,1)S(1)} all-gather(bf16[1,40,2]{1,2,0:T(2,128)(2,1)S(1)} %convert_bitcast_fusion.1), channel_id=1, replica_groups=mesh['dp'=4,'expert'=8] {'dp','expert'}, dimensions={0}, use_global_device_ids=true | all-gather | bytes 5280 | tf_op jit(solution)/shard_map/all_gather | solution.py:107
  51.5 2.0 reduce-window.6
  55.3 54.7 %all-gather.6.cloned.1.call-done = bf16[4,1280,1280]{2,1,0:T(8,128)(2,1)} async-done(((bf16[4,40,1280]{2,1,0:T(8,128)(2,1)}), bf16[4,1280,1280]{2,1,0:T(8,128)(2,1)}) %all-gather.6.cloned.1.call-update) | async-done | bytes 13107216 | tf_op jit(solution)/shard_map/all_gather | solution.py:104
  110.0 5.3 fusion.17
  118.0 4.2 multiply_reduce_fusion.5
  123.2 17.5 scatter_custom_fusion
  140.7 4.5 all-to-all-start
  145.3 84.8 %all-gather.1 = bf16[32,40,32]{1,2,0:T(8,128)(2,1)S(1)} all-gather(bf16[1,40,32]{1,2,0:T(8,128)(2,1)S(1)} %convert_bitcast_fusion), channel_id=1, replica_groups=mesh['dp'=4,'expert'=8] {'dp','expert'}, dimensions={0}, use_global_device_ids=true | all-gather | bytes 84480 | tf_op jit(solution)/shard_map/all_gather | solution.py:106
  230.6 2.7 mul.471
  233.3 5.5 mul.472
  239.9 12.9 scatter_custom_fusion.1
  252.9 5.0 all-to-all-start.2
  257.9 4.4 copy.313
  262.2 42.0 %all-to-all-done.2 = bf16[32,48,1280]{2,1,0:T(8,128)(2,1)} async-done(((bf16[32,48,1280]{2,1,0:T(8,128)(2,1)}), bf16[32,48,1280]{2,1,0:T(8,128)(2,1)}, u32[]{:S(2)}, u32[]{:S(2)}) %all-to-all-start.2) | async-done | bytes 3932192 | tf_op jit(solution)/shard_map/all_to_all | solution.py:207
  304.2 4.4 copy.318
  308.6 265.3 %all-gather.10.cloned.1.call-done = bf16[4,3,1280,896]{3,2,1,0:T(8,128)(2,1)} async-done(((bf16[4,3,320,896]{3,2,1,0:T(8,128)(2,1)}), bf16[4,3,1280,896]{3,2,1,0:T(8,128)(2,1)}) %all-gather.10.cloned.1.call-update) | async-done | bytes 27525136 | tf_op jit(solution)/shard_map/all_gather | solution.py:124
  573.9 16.9 convolution_bitcast_fusion.4
  590.8 12.8 fusion.23
  603.7 15.6 bitcast_convert_fusion
  619.3 7.1 copy.320
  626.4 4.6 all-to-all-start.3
  631.8 8.7 fusion.12
  640.6 5.0 copy.315
  645.5 39.0 %all-to-all-done.3 = bf16[4,384,1280]{2,0,1:T(4,128)(2,1)} async-done(((bf16[4,384,1280]{2,0,1:T(4,128)(2,1)}), bf16[4,384,1280]{2,0,1:T(4,128)(2,1)}, u32[]{:S(2)}, u32[]{:S(2)}) %all-to-all-start.3) | async-done | bytes 3932192 | tf_op jit(solution)/shard_map/all_to_all | solution.py:228
  684.5 4.7 all-to-all-start.1
  689.3 15.9 fusion.2
  705.2 24.3 %copy.343 = bf16[4,2,1280,896]{3,2,1,0:T(8,128)(2,1)} copy(bf16[4,2,1280,896]{2,3,1,0:T(8,128)(2,1)} %fusion.2) | data formatting | bytes 36700160 | tf_op jit(solution)/shard_map/erd,merf->emdf/transpose | solution.py:222
  729.4 10.0 convolution_convert_fusion.1
  739.5 19.6 pad_maximum_fusion
  759.0 19.3 copy.346
  778.4 11.5 all-to-all-start.4
  792.0 3.1 fusion.39
  795.0 3.0 convolution_bitcast_fusion.3
  798.0 2.2 fusion.86
  800.3 5.1 convolution_bitcast_fusion.2
  805.3 11.1 pad_maximum_fusion.2
  816.4 22.6 %copy.339 = f32[3,1280,896]{2,0,1:T(4,128)} copy(f32[3,1280,896]{1,2,0:T(8,128)} %pad_maximum_fusion.2) | data formatting | bytes 27525120 | tf_op jit(solution)/shard_map/concatenate | solution.py:306
  839.0 4.8 fusion.25
  843.8 4.6 copy.321
  848.4 4.6 copy.316
  853.0 8.5 gather_fusion.1
  861.5 9.0 gather_fusion
  870.5 4.7 reshape.383
  875.2 4.9 multiply_reduce_fusion
  880.2 3.0 reshape.384
  883.3 4.2 reduce_sum.190
  888.3 4.2 fusion.54
  892.6 3.4 fusion.31
  899.3 2.1 convolution_bitcast_fusion.1
  901.5 2.8 convolution_bitcast_fusion
  904.3 9.1 pad_maximum_fusion.1
  913.5 31.1 %copy.335 = f32[4,1280,1280]{2,0,1:T(4,128)} copy(f32[4,1280,1280]{1,2,0:T(8,128)} %pad_maximum_fusion.1) | data formatting | bytes 52428800 | tf_op jit(solution)/shard_map/concatenate | solution.py:305
  947.6 8.5 fusion.52
  956.1 601.8 %all-reduce.3 = f32[2,1280]{1,0:T(2,128)S(1)} all-reduce(f32[2,1280]{1,0:T(2,128)S(1)} %pad_maximum_fusion.12), channel_id=5, replica_groups=mesh['dp'=4,'expert'=8] {'dp','expert'}, use_global_device_ids=true, to_apply=%region_25.26.clone | all-reduce | flops 2560 | bytes 20480
  1559.1 1.4 multiply_add_fusion.9
  1560.4 2.2 fusion.51
  1562.6 468.7 %all-reduce.7.cloned.1.call-done = (f32[4,1280,1280]{2,0,1:T(4,128)}, f32[3,1280,896]{2,0,1:T(4,128)}, f32[1280,32]{0,1:T(8,128)}) async-done(((f32[4,1280,1280]{2,0,1:T(4,128)}, f32[3,1280,896]{2,0,1:T(4,128)}, f32[1280,32]{0,1:T(8,128)}), (f32[4,1280,1280]{2,0,1:T(4,128)}, f32[3,1280,896]{2,0,1:T(4,128)}, f32[1280,32]{0,1:T(8,128)})) %all-reduce.7.cloned.1.call-update) | async-done | bytes 40140816
  2032.6 1.5 multiply_add_fusion.7
  2035.3 2.2 multiply_add_fusion.5
  2037.5 2.4 multiply_add_fusion.2
  2039.9 15.8 convert_reduce_fusion
  2055.7 32.9 %multiply_add_fusion = (f32[4,3,320,896]{3,2,1,0:T(8,128)}, f32[4,3,320,896]{3,2,1,0:T(8,128)}, f32[4,3,320,896]{3,2,1,0:T(8,128)}) fusion(f32[4,3,320,896]{3,2,1,0:T(8,128)} %param.38, f32[4,3,320,896]{3,2,1,0:T(8,128)} %param.36, f32[4,3,320,896]{3,2,1,0:T(8,128)} %convert_reduce_fusion, f32[4,3,320,896]{3,2,1,0:T(8,128)} %param.37), kind=kLoop, calls=%fused_computation.14 | loop fusion | flops 30965760 | bytes 96337920 | tf_op jit(solution)/shard_map/add | solution.py:72
  (213 shorter events, 20.1 us)
Async XLA Ops:
  7.2 102.8 %all-gather.6.cloned.1.call-start = ((), (), s32[]{:S(2)}) async-start(), calls=%async_computation.5 | async-start | bytes 13516800 | tf_op jit(solution)/shard_map/all_gather | solution.py:104
  9.2 564.7 %all-gather.10.cloned.1.call-start = ((), (), s32[]{:S(2)}) async-start(), calls=%async_computation.7 | async-start | bytes 34406400 | tf_op jit(solution)/shard_map/all_gather | solution.py:124
  18.1 37.0 %copy-start.4 = (bf16[128,1280]{1,0:T(8,128)(2,1)S(1)}, bf16[128,1280]{1,0:T(8,128)(2,1)}, u32[]{:S(2)}) copy-start(bf16[128,1280]{1,0:T(8,128)(2,1)} %param.20) | copy-start | bytes 983044
  18.1 37.1 %copy-start.57 = (s32[1,128]{1,0:T(1,128)S(1)}, s32[1,128]{1,0:T(1,128)}, u32[]{:S(2)}) copy-start(s32[1,128]{1,0:T(1,128)} %param.23) | copy-start | bytes 1540
  54.1 61.2 %copy-start.40 = (f32[1280]{0:T(1024)}, f32[1280]{0:T(1024)S(1)}, u32[]{:S(2)}) copy-start(f32[1280]{0:T(1024)S(1)} %get-tuple-element.115) | copy-start | bytes 15364
  54.1 68.1 %copy-start.42 = (f32[1280]{0:T(1024)}, f32[1280]{0:T(1024)S(1)}, u32[]{:S(2)}) copy-start(f32[1280]{0:T(1024)S(1)} %get-tuple-element.114) | copy-start | bytes 15364
  55.2 60.1 %copy-start.59 = (f32[128]{0:T(128)}, f32[128]{0:T(128)S(1)}, u32[]{:S(2)}) copy-start(f32[128]{0:T(128)S(1)} %add_rsqrt_fusion.1) | copy-start | bytes 1540
  115.9 2.1 copy-start.21
  116.6 1.4 copy-start.8
  116.6 1.4 copy-start.10
  116.9 23.8 %copy-start.38 = (f32[10,128]{1,0:T(8,128)}, f32[10,128]{1,0:T(8,128)S(1)}, u32[]{:S(2)}) copy-start(f32[10,128]{1,0:T(8,128)S(1)} %get-tuple-element.169) | copy-start | bytes 15364
  117.0 5.2 copy-start.48
  118.0 4.2 copy-start.17
  122.2 18.5 copy-start.55
  123.2 22.1 %copy-start.44 = (f32[40,32]{0,1:T(8,128)S(1)}, f32[40,32]{0,1:T(8,128)}, u32[]{:S(2)}) copy-start(f32[40,32]{0,1:T(8,128)} %param.30) | copy-start | bytes 15364
  123.2 107.3 %copy-start.12 = (bf16[128,1280]{1,0:T(8,128)(2,1)S(1)}, bf16[128,1280]{1,0:T(8,128)(2,1)}, u32[]{:S(2)}) copy-start(bf16[128,1280]{1,0:T(8,128)(2,1)} %param.21) | copy-start | bytes 983044
  140.7 112.2 %all-to-all-start = ((bf16[32,48,1280]{2,1,0:T(8,128)(2,1)}), bf16[32,48,1280]{2,1,0:T(8,128)(2,1)}, u32[]{:S(2)}, u32[]{:S(2)}) async-start(bf16[32,48,1280]{2,1,0:T(8,128)(2,1)} %bitcast.253), calls=%async_computation | async-start | bytes 7864320 | tf_op jit(solution)/shard_map/all_to_all | solution.py:171
  230.5 8.2 copy-start.26
  239.0 13.9 copy-start.51
  239.6 13.3 copy-start.53
  239.7 13.2 copy-start.30
  252.9 51.3 %all-to-all-start.2 = ((bf16[32,48,1280]{2,1,0:T(8,128)(2,1)}), bf16[32,48,1280]{2,1,0:T(8,128)(2,1)}, u32[]{:S(2)}, u32[]{:S(2)}) async-start(bf16[32,48,1280]{2,1,0:T(8,128)(2,1)} %bitcast.254), calls=%async_computation.2 | async-start | bytes 7864320 | tf_op jit(solution)/shard_map/all_to_all | solution.py:207
  573.9 16.9 copy-start.6
  626.4 4.7 copy-start.19
  626.4 58.1 %all-to-all-start.3 = ((bf16[4,384,1280]{2,0,1:T(4,128)(2,1)}), bf16[4,384,1280]{2,0,1:T(4,128)(2,1)}, u32[]{:S(2)}, u32[]{:S(2)}) async-start(bf16[4,384,1280]{2,0,1:T(4,128)(2,1)} %copy.320), calls=%async_computation.3 | async-start | bytes 7864320 | tf_op jit(solution)/shard_map/all_to_all | solution.py:228
  631.1 160.9 %all-gather.8.cloned.1.call-start = ((), (), s32[]{:S(2)}) async-start(), calls=%async_computation.6 | async-start | bytes 7096320 | tf_op jit(solution)/shard_map/all_gather | solution.py:105
  684.5 93.9 %all-to-all-start.1 = ((bf16[4,384,1280]{2,0,1:T(4,128)(2,1)}), bf16[4,384,1280]{2,0,1:T(4,128)(2,1)}, u32[]{:S(2)}, u32[]{:S(2)}) async-start(bf16[4,384,1280]{2,0,1:T(4,128)(2,1)} %copy.315), calls=%async_computation.1 | async-start | bytes 7864320 | tf_op jit(solution)/shard_map/all_to_all | solution.py:182
  778.4 12.8 copy-start.58
  778.4 1261.5 %all-to-all-start.4 = ((bf16[4,3,4,320,896]{4,3,1,0,2:T(8,128)(2,1)}), bf16[4,3,4,320,896]{4,3,1,0,2:T(8,128)(2,1)}, u32[]{:S(2)}, u32[]{:S(2)}) async-start(bf16[4,3,4,320,896]{4,3,1,0,2:T(8,128)(2,1)} %copy.346), calls=%async_computation.4 | async-start | bytes 55050240 | tf_op jit(solution)/shard_map/all_to_all | solution.py:301
  789.9 1241.5 %all-reduce.7.cloned.1.call-start = ((), (), s32[]{:S(2)}) async-start(), calls=%async_computation.8 | async-start | bytes 89456640
  795.0 5.2 copy-start.35
  816.4 22.6 %copy-start.39 = (f32[10,128]{1,0:T(8,128)S(1)}, f32[10,128]{1,0:T(8,128)}, u32[]{:S(2)}) copy-start(f32[10,128]{1,0:T(8,128)} %copy-done.38) | copy-start | bytes 15364
  816.4 22.6 %copy-start.49 = (f32[10,128]{1,0:T(8,128)S(1)}, f32[10,128]{1,0:T(8,128)}, u32[]{:S(2)}) copy-start(f32[10,128]{1,0:T(8,128)} %copy-done.48) | copy-start | bytes 15364
  870.5 4.7 copy-start.14
  870.5 4.7 copy-start.31
  880.1 7.3 copy-start.37
  880.1 7.3 copy-start.52
  880.1 7.3 copy-start.54
  880.1 7.3 copy-start.47
  880.2 7.4 copy-start.3
  880.2 7.4 copy-start.27
  880.2 7.4 copy-start.43
  880.2 7.4 copy-start.56
  883.2 4.3 copy-start.29
  883.2 5.0 copy-start.13
  883.3 5.0 copy-start.28
  888.3 7.9 copy-start.1
  892.6 4.0 copy-start.15
  892.6 4.9 copy-start.22
  892.6 5.4 copy-start.11
  892.6 5.7 copy-start.9
  892.6 5.7 copy-start.34
  898.7 2.8 copy-start.5
  898.7 2.8 copy-start.41
  898.7 2.8 copy-start.60
  899.0 2.6 copy-start.23
  947.5 612.9 %copy-start.16 = (f32[128,1280]{1,0:T(8,128)S(1)}, f32[128,1280]{1,0:T(8,128)}, u32[]{:S(2)}) copy-start(f32[128,1280]{1,0:T(8,128)} %copy-done.15) | copy-start | bytes 1966084
  947.6 1085.0 %copy-start.45 = (f32[40,32]{0,1:T(8,128)S(1)}, f32[40,32]{0,1:T(8,128)}, u32[]{:S(2)}) copy-start(f32[40,32]{0,1:T(8,128)} %param.30) | copy-start | bytes 15364
  947.6 1085.0 %copy-start.50 = (f32[40,32]{0,1:T(8,128)S(1)}, f32[40,32]{0,1:T(8,128)}, u32[]{:S(2)}) copy-start(f32[40,32]{0,1:T(8,128)} %param.32) | copy-start | bytes 15364
  956.0 1079.2 %copy-start.20 = (f32[3,40,896]{2,1,0:T(8,128)S(1)}, f32[3,40,896]{2,1,0:T(8,128)}, u32[]{:S(2)}) copy-start(f32[3,40,896]{2,1,0:T(8,128)} %param.27) | copy-start | bytes 1290244
  956.0 1079.3 %copy-start.32 = (f32[3,40,896]{2,1,0:T(8,128)S(1)}, f32[3,40,896]{2,1,0:T(8,128)}, u32[]{:S(2)}) copy-start(f32[3,40,896]{2,1,0:T(8,128)} %param.29) | copy-start | bytes 1290244
  956.0 1081.4 %copy-start.7 = (f32[4,40,1280]{2,1,0:T(8,128)S(1)}, f32[4,40,1280]{2,1,0:T(8,128)}, u32[]{:S(2)}) copy-start(f32[4,40,1280]{2,1,0:T(8,128)} %param.24) | copy-start | bytes 2457604
  956.0 1081.4 %copy-start.24 = (f32[4,40,1280]{2,1,0:T(8,128)S(1)}, f32[4,40,1280]{2,1,0:T(8,128)}, u32[]{:S(2)}) copy-start(f32[4,40,1280]{2,1,0:T(8,128)} %param.26) | copy-start | bytes 2457604
  2031.4 6.1 copy-start.25
  (7 other events, 6.4 us)
Sparse Core Ops, SparseCore 0:
  11.5 98.4 all-gather.5
  112.2 461.7 all-gather.9
  635.3 107.5 all-gather.7
  945.6 1085.7 all-reduce.6
where the time goes:
time: 2110 us; the launch traced here: 2100 us
  waiting for transfers between devices  870 us (41%)
  blocking collectives  718 us (34%)
  local copies, waits for them, and re-layouts  188 us (9%)
  other arithmetic  139 us (7%)
  matrix products  132 us (6%)
  starting transfers between devices  30.9 us (1%)
    unnamed x1, blocking collectives  602 us
    unnamed x5, waiting for transfers between devices  469 us
    all_gather x1, waiting for transfers between devices, body(): lax.all_gather(expert_weight.astype(jnp.bfloat16), 'dp', axis=2, tiled=True)  265 us
    all_gather x1, blocking collectives, body(): lax.all_gather(router_weight.astype(jnp.bfloat16), ('dp', 'expert'), axis...  84.8 us
    all_gather x1, waiting for transfers between devices, body(): lax.all_gather(attn_weight.astype(jnp.bfloat16), ('dp', 'expert'), axis=1...  54.7 us
  transfers between devices with their start and end apart: 9, of which 5 were waited for; matrix products, arithmetic and copies ran while one was open for 17% of the time, Pallas kernels for 0%

commit v1 on v0

v1 whole, which is shorter than its diff:
```python
import math

import jax
import jax.numpy as jnp
from jax import lax
from jax.sharding import PartitionSpec as P

HEADS = 10
HD = 128
TOPK = 7
STEP = 3
BF = jnp.bfloat16
F32 = jnp.float32

epsilon = 1e-06
momentum_decay = 0.9
masked_score = -1e30
rate_attn = 5e-05
rate_output = 0.0002
rate_shared = 0.0001
rate_router = 3e-05
rate_gain = 0.002
rate_expert = 0.0015
ALL = ("dp", "expert")


def rope_tables(length, size):
    half = size // 2
    freq = jnp.exp(jnp.arange(half, dtype=F32) * (-2.0 * math.log(10000.0) / size))
    angle = jnp.arange(length, dtype=F32)[:, None] * freq[None, :]
    cosine = jnp.concatenate([jnp.cos(angle), jnp.cos(angle)], -1)
    sine = jnp.concatenate([jnp.sin(angle), jnp.sin(angle)], -1)
    return (cosine, sine)


def rotate(heads_in, cosine, sine):
    half = heads_in.shape[-1] // 2
    turned = jnp.concatenate([-heads_in[..., half:], heads_in[..., :half]], -1)
    return heads_in * cosine[:, None, :] + turned * sine[:, None, :]


def rotate_back(grads_in, cosine, sine):
    half = grads_in.shape[-1] // 2
    scaled = grads_in * sine[:, None, :]
    turned = jnp.concatenate([scaled[..., half:], -scaled[..., :half]], -1)
    return grads_in * cosine[:, None, :] + turned


def update(weight, moment, average, grad, rate):
    moment_new = momentum_decay * moment + grad
    weight_new = weight - rate * (grad + momentum_decay * moment_new)
    average_new = average + (weight_new - average) / (STEP + 1.0)
    return (weight_new, moment_new, average_new)


def mm(a, b):
    return jnp.dot(a, b, preferred_element_type=F32)


def mm_nt(a, b):
    return lax.dot_general(a, b, (((1,), (1,)), ((), ())), preferred_element_type=F32)


def mm_tn(a, b):
    return lax.dot_general(a, b, (((0,), (0,)), ((), ())), preferred_element_type=F32)


def body(
    tokens,
    cotangent,
    routes,
    doc_ids,
    attn_weight,
    attn_momentum,
    attn_average,
    shared_weight,
    shared_momentum,
    shared_average,
    router_weight,
    router_momentum,
    router_average,
    gain_weight,
    gain_momentum,
    gain_average,
    expert_weight,
    expert_momentum,
    expert_average,
):
    Z = lax.axis_size("dp")
    E = lax.axis_size("expert")
    L, D = tokens.shape
    rows_own = attn_weight.shape[1]
    local, _, deep, FF = expert_weight.shape
    experts = router_weight.shape[1]
    parts = Z // local
    FP = FF // parts
    FS = shared_weight.shape[2] // Z
    cap = min(L, (L * TOPK * 3 // (2 * experts) + 7) // 8 * 8)
    zi = lax.axis_index("dp")

    def swap_z(pieces):
        out = [pieces[0]]
        for k in range(1, Z):
            out.append(lax.ppermute(pieces[k], "dp", [(i, i ^ k) for i in range(Z)]))
        return out

    def gather_z(x):
        return swap_z([x] * Z)

    attn_rows = jnp.swapaxes(attn_weight, 0, 1).reshape(rows_own, 4 * D).astype(BF)
    extra = jnp.concatenate([router_weight, gain_weight.T], 1).astype(BF)
    extra = jnp.pad(extra, ((0, 0), (0, 128 - extra.shape[1])))
    packed = lax.all_gather(jnp.concatenate([attn_rows, extra], 1), ALL, axis=0, tiled=True)
    w_qkv = packed[:, : 3 * D]
    w_o = packed[:, 3 * D : 4 * D]
    router_w = packed[:, 4 * D : 4 * D + experts]
    gain_vals = packed[:, 4 * D + experts : 4 * D + experts + 2].astype(F32).T

    grad_in = jnp.stack(gather_z(cotangent))
    routes_z = jnp.stack(gather_z(routes))

    ew = expert_weight.astype(BF)
    expert_full = []
    for m in (0, 1, 2):
        w = ew[:, m].reshape(local, deep, parts, FP).transpose(0, 2, 1, 3).reshape(Z, deep, FP)
        expert_full.append(
            lax.all_to_all(w, "dp", split_axis=0, concat_axis=0, tiled=True).reshape(Z * deep, FP)
        )
    wg, wu, wd = expert_full

    sw = shared_weight.astype(BF).reshape(3, rows_own, Z, FS).transpose(2, 0, 1, 3)
    sw = lax.all_to_all(sw, "dp", split_axis=0, concat_axis=0, tiled=True)
    sw = lax.all_gather(sw, "expert", axis=0, tiled=False)
    shared_w = sw.transpose(2, 1, 0, 3, 4).reshape(3, D, FS)

    inputs = tokens.astype(F32)
    cosine, sine = rope_tables(L, HD)
    score_scale = HD ** (-0.5)
    documents = doc_ids[0]
    position = jnp.arange(L)
    allowed = (
        (position[None, :] <= position[:, None]) & (documents[None, :] == documents[:, None])
    )[None]
    inv_first = lax.rsqrt(jnp.mean(inputs * inputs, -1, keepdims=True) + epsilon)
    unit_first = inputs * inv_first
    normed = (unit_first * gain_vals[0]).astype(BF)
    projected = mm(normed, w_qkv)
    query = rotate(projected[:, :D].reshape(L, HEADS, HD), cosine, sine).astype(BF)
    key_rot = rotate(projected[:, D : 2 * D].reshape(L, HEADS, HD), cosine, sine).astype(BF)
    values = projected[:, 2 * D :].astype(BF).reshape(L, HEADS, HD)
    raw = jnp.einsum("ihd,jhd->hij", query, key_rot, preferred_element_type=F32) * score_scale
    scores = jnp.where(allowed, raw, masked_score)
    row_max = jnp.max(scores, -1, keepdims=True)
    exponent = jnp.exp(scores - row_max)
    attn_probs = exponent / jnp.sum(exponent, -1, keepdims=True)
    probs_low = attn_probs.astype(BF)
    heads_out = jnp.einsum("hij,jhd->ihd", probs_low, values, preferred_element_type=F32)
    heads_out = heads_out.reshape(L, D).astype(BF)
    attn_out = mm(heads_out, w_o)
    middle = inputs + attn_out
    inv_second = lax.rsqrt(jnp.mean(middle * middle, -1, keepdims=True) + epsilon)
    unit_second = middle * inv_second
    inner = (unit_second * gain_vals[1]).astype(BF)

    inner_z = jnp.stack(gather_z(inner))
    hot = jnp.sum(
        (routes_z[:, :, :, None] == jnp.arange(experts, dtype=jnp.int32)).astype(F32), 2
    )
    before = (position[None, :] < position[:, None]).astype(BF)
    rank = jnp.einsum("tu,sux->stx", before, hot.astype(BF), preferred_element_type=F32)
    first = zi // parts
    mine = jnp.arange(E) * local + first
    pick = (jnp.arange(experts)[:, None] == mine[None, :]).astype(F32)
    hot_mine = jnp.einsum("stx,xe->est", hot, pick)
    rank_mine = jnp.einsum("stx,xe->est", rank, pick, precision=lax.Precision.HIGHEST)
    place = (
        (rank_mine[:, :, None, :] == jnp.arange(cap, dtype=F32)[None, None, :, None])
        & (hot_mine[:, :, None, :] > 0.5)
    ).astype(BF)

    logits = jnp.einsum("std,dx->stx", inner_z, router_w, preferred_element_type=F32)
    chosen = jnp.where(hot > 0.5, logits, masked_score)
    chosen_max = jnp.max(chosen, -1, keepdims=True)
    chosen_exp = jnp.where(hot > 0.5, jnp.exp(chosen - chosen_max), 0.0)
    gates = chosen_exp / jnp.sum(chosen_exp, -1, keepdims=True)
    gates_mine = jnp.einsum("stx,xe->est", gates, pick, precision=lax.Precision.HIGHEST)
    gate_rows = jnp.sum(place.astype(F32) * gates_mine[:, :, None, :], -1)

    def dispatch(x):
        rows = jnp.einsum("esct,std->escd", place, x, preferred_element_type=F32).astype(BF)
        return lax.all_to_all(rows, "expert", split_axis=0, concat_axis=0, tiled=True).reshape(
            E * Z * cap, D
        )

    def collect(rows, add):
        back = lax.all_to_all(
            rows.reshape(E, Z, cap, D), "expert", split_axis=0, concat_axis=0, tiled=True
        )
        total = jnp.einsum("esct,escd->std", place, back, preferred_element_type=F32) + add
        total = total.astype(BF)
        got = swap_z([total[k] for k in range(Z)])
        return sum(g.astype(F32) for g in got)

    grad_rows = dispatch(grad_in)
    rows = dispatch(inner_z)
    gate_col = lax.all_to_all(gate_rows, "expert", split_axis=0, concat_axis=0, tiled=True)
    gate_col = gate_col.reshape(E * Z * cap, 1)

    eg = mm(rows, wg)
    eu = mm(rows, wu)
    sig = jax.nn.sigmoid(eg)
    silu = eg * sig
    hidden = silu * eu
    gated = (gate_col * hidden).astype(BF)
    plain_grad = mm(grad_rows, wd)
    gate_grad = jnp.sum(hidden * plain_grad, -1)
    hidden_grad = gate_col * plain_grad
    eg_grad = (hidden_grad * eu * sig * (1.0 + eg * (1.0 - sig))).astype(BF)
    eu_grad = (hidden_grad * silu).astype(BF)
    rows_grad = (mm_nt(eg_grad, wg) + mm_nt(eu_grad, wu)).astype(BF)
    routed_rows = mm_nt(gated, wd).astype(BF)

    flat_inner = inner_z.reshape(Z * L, D)
    flat_grad = grad_in.reshape(Z * L, D)
    sg = mm(flat_inner, shared_w[0])
    su = mm(flat_inner, shared_w[1])
    ssig = jax.nn.sigmoid(sg)
    ssilu = sg * ssig
    shared_hidden = (ssilu * su).astype(BF)
    shared_out = mm_nt(shared_hidden, shared_w[2])
    shared_hidden_grad = mm(flat_grad, shared_w[2])
    sg_grad = (shared_hidden_grad * su * ssig * (1.0 + sg * (1.0 - ssig))).astype(BF)
    su_grad = (shared_hidden_grad * ssilu).astype(BF)
    shared_back = mm_nt(sg_grad, shared_w[0]) + mm_nt(su_grad, shared_w[1])
    shared_grads = jnp.stack(
        [mm_tn(flat_inner, sg_grad), mm_tn(flat_inner, su_grad), mm_tn(flat_grad, shared_hidden)]
    ).astype(BF)

    inner_grad = collect(rows_grad, shared_back.reshape(Z, L, D))
    branch = collect(routed_rows, shared_out.reshape(Z, L, D))

    gate_grad_back = lax.all_to_all(
        gate_grad.reshape(E, Z, cap), "expert", split_axis=0, concat_axis=0, tiled=True
    )
    gate_grad_mine = jnp.sum(place.astype(F32) * gate_grad_back[:, :, :, None], 2)
    gate_grad_z = jnp.einsum(
        "est,xe->stx", gate_grad_mine, pick, precision=lax.Precision.HIGHEST
    )
    got = swap_z([gate_grad_z[k] for k in range(Z)])
    gate_grad_own = sum(got)
    gates_own = gates[0]
    logit_grad = gates_own * (
        gate_grad_own - jnp.sum(gates_own * gate_grad_own, -1, keepdims=True)
    )
    router_grad = mm_tn(inner.astype(F32), logit_grad)
    router_back = mm_nt(logit_grad, router_w.astype(F32))
    inner_grad = inner_grad + router_back

    layer_out = (middle + branch).astype(BF)
    first_mask = jnp.concatenate([jnp.ones((1,), bool), documents[1:] != documents[:-1]])
    kept_mask = 1.0 - first_mask.astype(F32)
    kept_total = jnp.sum(kept_mask) * D
    attn_rms = jnp.sqrt(jnp.sum(kept_mask[:, None] * attn_out * attn_out) / kept_total)
    branch_rms = jnp.sqrt(jnp.sum(kept_mask[:, None] * branch * branch) / kept_total)
    sublayer_rms = jnp.stack([attn_rms, branch_rms])[None, :]

    upstream = cotangent.astype(F32)
    scaled_second = inner_grad * gain_vals[1]
    second_gain_grad = jnp.sum(inner_grad * unit_second, 0)
    middle_grad = upstream + inv_second * (
        scaled_second - unit_second * jnp.mean(scaled_second * unit_second, -1, keepdims=True)
    )
    attn_grad = middle_grad.astype(BF)
    output_grad = mm_tn(heads_out, attn_grad)
    heads_grad = mm_nt(attn_grad, w_o).astype(BF).reshape(L, HEADS, HD)
    value_grad = jnp.einsum(
        "hij,ihd->jhd", probs_low, heads_grad, preferred_element_type=F32
    ).astype(BF)
    prob_grad = jnp.einsum("ihd,jhd->hij", heads_grad, values, preferred_element_type=F32)
    score_grad = (
        attn_probs * (prob_grad - jnp.sum(attn_probs * prob_grad, -1, keepdims=True))
    ).astype(BF)
    query_grad = (
        jnp.einsum("hij,jhd->ihd", score_grad, key_rot, preferred_element_type=F32) * score_scale
    )
    query_grad = rotate_back(query_grad, cosine, sine).astype(BF)
    key_grad = (
        jnp.einsum("hij,ihd->jhd", score_grad, query, preferred_element_type=F32) * score_scale
    )
    key_grad = rotate_back(key_grad, cosine, sine).astype(BF)
    proj_grad = jnp.concatenate(
        [query_grad.reshape(L, D), key_grad.reshape(L, D), value_grad.reshape(L, D)], 1
    )
    qkv_grad = mm_tn(normed, proj_grad)
    normed_grad = mm_nt(proj_grad, w_qkv)
    scaled_first = normed_grad * gain_vals[0]
    first_gain_grad = jnp.sum(normed_grad * unit_first, 0)
    input_grad = middle_grad + inv_first * (
        scaled_first - unit_first * jnp.mean(scaled_first * unit_first, -1, keepdims=True)
    )

    down_grad = mm_tn(grad_rows, gated).astype(BF)
    gate_w_grad = mm_tn(rows, eg_grad).astype(BF)
    up_w_grad = mm_tn(rows, eu_grad).astype(BF)
    sums = []
    for g in (gate_w_grad, up_w_grad, down_grad):
        g = lax.all_to_all(g.reshape(Z, deep, FP), "dp", split_axis=0, concat_axis=0, tiled=True)
        g = g.reshape(local, parts, deep, FP).transpose(0, 2, 1, 3).reshape(local, deep, FF)
        sums.append(g.astype(F32))
    expert_sum = jnp.stack(sums, 1)

    gain_all = jnp.stack([first_gain_grad, second_gain_grad], 1)
    pad = jnp.zeros((D, 128 - experts - 2), F32)
    attn_all = jnp.concatenate([qkv_grad, output_grad, router_grad, gain_all, pad], 1).astype(BF)
    attn_own = lax.psum_scatter(attn_all, ALL, scatter_dimension=0, tiled=True).astype(F32)
    attn_sum = jnp.swapaxes(attn_own[:, : 4 * D].reshape(rows_own, 4, D), 0, 1)
    router_sum = attn_own[:, 4 * D : 4 * D + experts]
    gain_sum = attn_own[:, 4 * D + experts : 4 * D + experts + 2].T

    sgr = shared_grads.reshape(3, Z, E, rows_own, FS).transpose(2, 1, 0, 3, 4)
    sgr = lax.psum_scatter(sgr, "expert", scatter_dimension=0, tiled=False)
    sgr = lax.all_to_all(sgr, "dp", split_axis=0, concat_axis=0, tiled=True)
    shared_sum = sgr.transpose(1, 2, 0, 3).reshape(3, rows_own, Z * FS).astype(F32)

    attn_rates = jnp.array([rate_attn, rate_attn, rate_attn, rate_output], F32).reshape(4, 1, 1)
    return (
        layer_out,
        input_grad,
        *update(attn_weight, attn_momentum, attn_average, attn_sum, attn_rates),
        *update(shared_weight, shared_momentum, shared_average, shared_sum, rate_shared),
        *update(router_weight, router_momentum, router_average, router_sum, rate_router),
        *update(gain_weight, gain_momentum, gain_average, gain_sum, rate_gain),
        *update(expert_weight, expert_momentum, expert_average, expert_sum, rate_expert),
        sublayer_rms,
    )


def solution(mesh):
    rows = P(ALL, None)
    middle = P(None, ALL, None)
    gains = P(None, ALL)
    routed = P("expert", None, "dp", None)
    weights = (middle,) * 6 + (rows,) * 3 + (gains,) * 3 + (routed,) * 3
    return jax.shard_map(
        body,
        mesh=mesh,
        in_specs=(rows,) * 4 + weights,
        out_specs=(rows,) * 2 + weights + (rows,),
        check_vma=False,
    )
```

time: 2110 us -> 967 us (0.46)
  blocking collectives: 718 us -> 0 us
  waiting for transfers between devices: 870 us -> 532 us
  local copies, waits for them, and re-layouts: 188 us -> 56.1 us
  starting transfers between devices: 30.9 us -> 136 us
  other arithmetic: 139 us -> 75.5 us
    unnamed x1 -> x0, blocking collectives: 602 us -> none
    unnamed x5 -> x6, waiting for transfers between devices: 469 us -> 30.5 us
    all_gather x3 -> x2, waiting for transfers between devices: 320 us -> 72.9 us  [the longest x1 72.9 us: body(): lax.all_gather(jnp.concatenate([attn_rows, extra], 1), ALL, axis=0, tiled...]
    all_to_all x5 -> x14, waiting for transfers between devices: 81 us -> 316 us  [the longest x3 145 us: body(): lax.all_to_all(g.reshape(Z, deep, FP), 'dp', split_axis=0, concat_axis=0,...]
    all_gather x2 -> x0, blocking collectives: 117 us -> none  [the longest x1 84.8 us: body(): lax.all_gather(router_weight.astype(jnp.bfloat16), ('dp', 'expert'), axis...]
    ppermute x0 -> x18, waiting for transfers between devices: none -> 113 us  [swap_z(): out.append(lax.ppermute(pieces[k], 'dp', [(i, i ^ k) for i in range(Z)]))]
    all_to_all x5 -> x14, starting transfers between devices: 30.4 us -> 109 us  [the longest x3 46.4 us: body(): lax.all_to_all(g.reshape(Z, deep, FP), 'dp', split_axis=0, concat_axis=0,...]
    concatenate x3 -> x1, local copies, waits for them, and re-layouts: 73 us -> 19.2 us  [body(): jnp.concatenate([qkv_grad, output_grad, router_grad, gain_all, pad], 1)]
  transfers between devices with their start and end apart: 9 -> 36, of which waited for: 5 -> 20; matrix products, arithmetic and copies ran while one was open for 17% -> 25% of each run, Pallas kernels for 0% -> 0%
where the time goes in v1:
time: 967 us; the launch traced here: 957 us
  waiting for transfers between devices  532 us (55%)
  matrix products  138 us (14%)
  starting transfers between devices  136 us (14%)
  other arithmetic  75.5 us (8%)
  local copies, waits for them, and re-layouts  56.1 us (6%)
  between operations  19.2 us (2%)
    all_to_all x3, waiting for transfers between devices, body(): lax.all_to_all(g.reshape(Z, deep, FP), 'dp', split_axis=0, concat_axis=0,...  145 us
    ppermute x18, waiting for transfers between devices, swap_z(): out.append(lax.ppermute(pieces[k], 'dp', [(i, i ^ k) for i in range(Z)]))  113 us
    all_gather x1, waiting for transfers between devices, body(): lax.all_gather(jnp.concatenate([attn_rows, extra], 1), ALL, axis=0, tiled...  72.9 us
    all_to_all x3, waiting for transfers between devices, body(): lax.all_to_all(w, 'dp', split_axis=0, concat_axis=0, tiled=True)  64.5 us
    all_to_all x2, waiting for transfers between devices, collect(): lax.all_to_all(rows.reshape(E, Z, cap, D), 'expert', split_axis=0, concat...  55.9 us
    all_to_all x3, starting transfers between devices, body(): lax.all_to_all(g.reshape(Z, deep, FP), 'dp', split_axis=0, concat_axis=0,...  46.4 us
    dot_general x8, matrix products, mm(): return jnp.dot(a, b, preferred_element_type=F32)  46.2 us
    all_to_all x2, waiting for transfers between devices, dispatch(): lax.all_to_all(rows, 'expert', split_axis=0, concat_axis=0, tiled=True)  39.2 us
  transfers between devices with their start and end apart: 36, of which 20 were waited for; matrix products, arithmetic and copies ran while one was open for 25% of the time, Pallas kernels for 0%

profile of v1, /device:TPU:16, one launch (start us, length us, event | category | flops | bytes accessed | tf_op | source)
XLA Modules:
  0.0 956.8 jit_solution(14509111457688888036)
XLA Ops:
  11.6 8.8 convert_element_type.215
  20.4 6.4 slice_bitcast_fusion.2
  26.9 5.3 all-to-all-start.3
  32.8 3.3 collective-permute-start.1
  36.4 64.5 %all-to-all-done.3 = bf16[4,320,896]{2,1,0:T(8,128)(2,1)} async-done(((bf16[4,320,896]{2,1,0:T(8,128)(2,1)}), bf16[4,320,896]{2,1,0:T(8,128)(2,1)}, u32[]{:S(2)}, u32[]{:S(2)}) %all-to-all-start.3) | async-done | bytes 2293792 | tf_op jit(solution)/shard_map/all_to_all | solution.py:127
  100.9 8.0 all-to-all-start.2
  110.4 72.9 %all-gather.4.cloned.1.call-done = bf16[1280,5248]{1,0:T(8,128)(2,1)} async-done(((bf16[40,5248]{1,0:T(8,128)(2,1)}), bf16[1280,5248]{1,0:T(8,128)(2,1)}) %all-gather.4.cloned.1.call-update) | async-done | bytes 13434896 | tf_op jit(solution)/shard_map/all_gather | solution.py:113
  185.0 5.3 fusion.6
  193.9 10.0 %all-to-all-start.4 = ((bf16[4,320,896]{2,1,0:T(8,128)(2,1)}), bf16[4,320,896]{2,1,0:T(8,128)(2,1)}, u32[]{:S(2)}, u32[]{:S(2)}) async-start(bf16[4,320,896]{2,1,0:T(8,128)(2,1)} %get-tuple-element.179), calls=%async_computation.4 | async-start | bytes 4587520 | tf_op jit(solution)/shard_map/all_to_all | solution.py:127
  206.7 3.5 multiply_reduce_fusion.4
  211.1 3.3 collective-permute-start.4
  214.5 62.0 %collective-permute-done.5 = bf16[128,1280]{1,0:T(8,128)(2,1)S(1)} collective-permute-done((bf16[128,1280]{1,0:T(8,128)(2,1)S(1)}, bf16[128,1280]{1,0:T(8,128)(2,1)S(1)}, u32[]{:S(2)}, u32[]{:S(2)}) %collective-permute-start.5) | collective-permute-done | bytes 327712 | tf_op jit(solution)/shard_map/ppermute | solution.py:104
  276.4 5.3 collective-permute-done.4
  283.1 2.3 copy.394
  285.4 4.7 all-to-all-start.1
  290.7 4.3 collective-permute-start.10
  295.0 19.7 %collective-permute-done.11 = bf16[128,1280]{1,0:T(8,128)(2,1)S(1)} collective-permute-done((bf16[128,1280]{1,0:T(8,128)(2,1)S(1)}, bf16[128,1280]{1,0:T(8,128)(2,1)S(1)}, u32[]{:S(2)}, u32[]{:S(2)}) %collective-permute-start.11) | collective-permute-done | bytes 327712 | tf_op jit(solution)/shard_map/ppermute | solution.py:104
  314.7 4.5 collective-permute-done.10
  320.4 2.3 copy.402
  322.7 13.7 %all-to-all-done.1 = bf16[8,4,48,1280]{3,2,1,0:T(8,128)(2,1)} async-done(((bf16[8,4,48,1280]{3,2,1,0:T(8,128)(2,1)}), bf16[8,4,48,1280]{3,2,1,0:T(8,128)(2,1)}, u32[]{:S(2)}, u32[]{:S(2)}) %all-to-all-start.1) | async-done | bytes 3932192 | tf_op jit(solution)/shard_map/all_to_all | solution.py:191
  336.4 4.7 all-to-all-start.7
  343.6 9.1 fusion.147
  352.7 9.1 fusion.146
  361.7 25.5 %all-to-all-done.7 = bf16[8,4,48,1280]{3,2,1,0:T(8,128)(2,1)} async-done(((bf16[8,4,48,1280]{3,2,1,0:T(8,128)(2,1)}), bf16[8,4,48,1280]{3,2,1,0:T(8,128)(2,1)}, u32[]{:S(2)}, u32[]{:S(2)}) %all-to-all-start.7) | async-done | bytes 3932192 | tf_op jit(solution)/shard_map/all_to_all | solution.py:191
  387.3 13.6 %multiply_reduce_fusion = (f32[1536]{0:T(1024)S(1)}, f32[1536,896]{0,1:T(8,128)}) fusion(f32[1536,896]{0,1:T(8,128)} %fusion.147, f32[1536,896]{0,1:T(8,128)} %fusion.146, bf16[1536,1280]{1,0:T(8,128)(2,1)} %bitcast.54, bf16[1280,896]{1,0:T(8,128)(2,1)} %bitcast.30), kind=kOutput, calls=%fused_computation.17 | convolution fusion | flops 3532847616 | bytes 22747136 | tf_op jit(solution)/shard_map/dot_general | solution.py:57
  401.6 3.3 all-to-all-start.9
  405.0 4.6 all-to-all-done.9
  409.6 6.7 all-to-all-start.6
  419.5 2.6 all-to-all-done.6
  422.1 3.3 all-to-all-start
  426.0 4.1 all-to-all-done
  430.9 8.7 multiply_convert_fusion
  439.6 7.7 fusion.150
  447.3 7.5 fusion.8
  454.9 5.1 all-to-all-start.8
  469.5 7.5 convolution_convert_fusion.2
  477.0 29.3 %all-to-all-done.8 = bf16[8,4,48,1280]{3,2,1,0:T(8,128)(2,1)} async-done(((bf16[8,4,48,1280]{3,2,1,0:T(8,128)(2,1)}), bf16[8,4,48,1280]{3,2,1,0:T(8,128)(2,1)}, u32[]{:S(2)}, u32[]{:S(2)}) %all-to-all-start.8) | async-done | bytes 3932192 | tf_op jit(solution)/shard_map/all_to_all | solution.py:196
  506.3 4.5 all-to-all-start.5
  510.9 2.8 multiply_convert_fusion.5
  523.0 2.9 collective-permute-start.16
  530.1 3.8 fusion.25
  538.4 26.6 %all-to-all-done.5 = bf16[8,4,48,1280]{3,2,1,0:T(8,128)(2,1)} async-done(((bf16[8,4,48,1280]{3,2,1,0:T(8,128)(2,1)}), bf16[8,4,48,1280]{3,2,1,0:T(8,128)(2,1)}, u32[]{:S(2)}, u32[]{:S(2)}) %all-to-all-start.5) | async-done | bytes 3932192 | tf_op jit(solution)/shard_map/all_to_all | solution.py:196
  565.0 3.0 fusion.16
  570.7 2.9 collective-permute-start.7
  575.7 16.6 %collective-permute-done.8 = bf16[128,1280]{1,0:T(8,128)(2,1)S(1)} collective-permute-done((bf16[128,1280]{1,0:T(8,128)(2,1)S(1)}, bf16[128,1280]{1,0:T(8,128)(2,1)S(1)}, u32[]{:S(2)}, u32[]{:S(2)}) %collective-permute-start.8) | collective-permute-done | bytes 327712 | tf_op jit(solution)/shard_map/ppermute | solution.py:104
  592.3 3.4 collective-permute-done.7
  597.6 3.2 fusion.33
  605.4 8.0 fusion.67
  614.0 2.7 convolution_convert_fusion.1
  616.7 5.4 convolution_convert_fusion
  622.2 19.2 %concatenate.50 = bf16[1280,5248]{1,0:T(8,128)(2,1)} concatenate(bf16[1280,3840]{1,0:T(8,128)(2,1)} %convolution_convert_fusion, bf16[1280,1280]{1,0:T(8,128)(2,1)} %convolution_convert_fusion.1, bf16[1280,32]{1,0:T(8,128)(2,1)S(1)} %copy.412, bf16[1280,1]{1,0:T(8,128)(2,1)S(1)} %stack.112, bf16[1280,1]{1,0:T(8,128)(2,1)S(1)} %stack.113, bf16[1280,94]{1,0:T(8,128)(2,1)S(1)} %broadcast_in_dim.26), dimensions={1} | concatenate | bytes 26869760 | tf_op jit(solution)/shard_map/concatenate | solution.py:314
  644.9 7.0 all-to-all-start.10
  651.9 8.6 convolution_convert_fusion.5
  660.5 5.1 all-to-all-start.13
  665.6 8.7 convolution_convert_fusion.6
  674.3 47.2 %all-to-all-done.13 = bf16[4,320,896]{2,1,0:T(8,128)(2,1)} async-done(((bf16[4,320,896]{2,1,0:T(8,128)(2,1)}), bf16[4,320,896]{2,1,0:T(8,128)(2,1)}, u32[]{:S(2)}, u32[]{:S(2)}) %all-to-all-start.13) | async-done | bytes 2293792 | tf_op jit(solution)/shard_map/all_to_all | solution.py:307
  721.5 21.1 %all-to-all-start.12 = ((bf16[4,320,896]{2,1,0:T(8,128)(2,1)}), bf16[4,320,896]{2,1,0:T(8,128)(2,1)}, u32[]{:S(2)}, u32[]{:S(2)}) async-start(bf16[4,320,896]{2,1,0:T(8,128)(2,1)} %bitcast.307), calls=%async_computation.12 | async-start | bytes 4587520 | tf_op jit(solution)/shard_map/all_to_all | solution.py:307
  742.6 8.6 convolution_convert_fusion.7
  751.3 47.0 %all-to-all-done.12 = bf16[4,320,896]{2,1,0:T(8,128)(2,1)} async-done(((bf16[4,320,896]{2,1,0:T(8,128)(2,1)}), bf16[4,320,896]{2,1,0:T(8,128)(2,1)}, u32[]{:S(2)}, u32[]{:S(2)}) %all-to-all-start.12) | async-done | bytes 2293792 | tf_op jit(solution)/shard_map/all_to_all | solution.py:307
  798.2 20.2 %all-to-all-start.11 = ((bf16[4,320,896]{2,1,0:T(8,128)(2,1)}), bf16[4,320,896]{2,1,0:T(8,128)(2,1)}, u32[]{:S(2)}, u32[]{:S(2)}) async-start(bf16[4,320,896]{2,1,0:T(8,128)(2,1)} %bitcast.305), calls=%async_computation.11 | async-start | bytes 4587520 | tf_op jit(solution)/shard_map/all_to_all | solution.py:307
  821.9 50.6 %all-to-all-done.11 = bf16[4,320,896]{2,1,0:T(8,128)(2,1)} async-done(((bf16[4,320,896]{2,1,0:T(8,128)(2,1)}), bf16[4,320,896]{2,1,0:T(8,128)(2,1)}, u32[]{:S(2)}, u32[]{:S(2)}) %all-to-all-start.11) | async-done | bytes 2293792 | tf_op jit(solution)/shard_map/all_to_all | solution.py:307
  872.5 30.5 %multiply_add_fusion = (f32[4,3,320,896]{3,2,1,0:T(8,128)}, f32[4,3,320,896]{3,2,1,0:T(8,128)}, f32[4,3,320,896]{3,2,1,0:T(8,128)}) fusion(f32[4,3,320,896]{3,2,1,0:T(8,128)} %param.38, f32[4,3,320,896]{3,2,1,0:T(8,128)} %param.36, bf16[4,1,320,896]{3,2,1,0:T(8,128)(2,1)} %bitcast.101, bf16[4,1,320,896]{3,2,1,0:T(8,128)(2,1)} %bitcast.99, ...), kind=kLoop, calls=%fused_computation.7 | loop fusion | flops 41287680 | bytes 89456640 | tf_op jit(solution)/shard_map/add | solution.py:52
  906.1 30.0 %reduce-scatter.6.cloned.1.call-done = bf16[40,5248]{1,0:T(8,128)(2,1)} async-done(((bf16[1280,5248]{1,0:T(8,128)(2,1)}), bf16[40,5248]{1,0:T(8,128)(2,1)}) %reduce-scatter.6.cloned.1.call-update) | async-done | bytes 419856
  946.2 2.8 multiply_add_fusion.1
  (285 shorter events, 82.5 us)
Async XLA Ops:
  8.0 175.3 %all-gather.4.cloned.1.call-start = ((), (), s32[]{:S(2)}) async-start(), calls=%async_computation.15 | async-start | bytes 13854720 | tf_op jit(solution)/shard_map/all_gather | solution.py:113
  26.9 5.4 copy-start.59
  26.9 9.2 copy-start.4
  26.9 74.1 %all-to-all-start.3 = ((bf16[4,320,896]{2,1,0:T(8,128)(2,1)}), bf16[4,320,896]{2,1,0:T(8,128)(2,1)}, u32[]{:S(2)}, u32[]{:S(2)}) async-start(bf16[4,320,896]{2,1,0:T(8,128)(2,1)} %get-tuple-element.180), calls=%async_computation.3 | async-start | bytes 4587520 | tf_op jit(solution)/shard_map/all_to_all | solution.py:127
  32.2 77.4 %copy-start.61 = (s32[1,128]{1,0:T(1,128)S(1)}, s32[1,128]{1,0:T(1,128)}, u32[]{:S(2)}) copy-start(s32[1,128]{1,0:T(1,128)} %param.23) | copy-start | bytes 1540
  32.2 77.5 %collective-permute-start.2 = (s32[128,7]{0,1:T(8,128)S(1)}, s32[128,7]{0,1:T(8,128)S(1)}, u32[]{:S(2)}, u32[]{:S(2)}) collective-permute-start(s32[128,7]{0,1:T(8,128)S(1)} %copy-done.59), channel_id=1, source_target_pairs={{0,24},{8,16},{16,8},{24,0},{1,25},{9,17},{17,9},{25,1},{2,26},{10... | collective-permute-start | bytes 10760 | tf_op jit(solution)/shard_map/ppermute | solution.py:104
  32.8 77.0 %collective-permute-start.1 = (s32[128,7]{0,1:T(8,128)S(1)}, s32[128,7]{0,1:T(8,128)S(1)}, u32[]{:S(2)}, u32[]{:S(2)}) collective-permute-start(s32[128,7]{0,1:T(8,128)S(1)} %copy-done.59), channel_id=1, source_target_pairs={{0,16},{8,24},{16,0},{24,8},{1,17},{9,25},{17,1},{25,9},{2,18},{10... | collective-permute-start | bytes 10760 | tf_op jit(solution)/shard_map/ppermute | solution.py:104
  36.1 73.7 %collective-permute-start = (s32[128,7]{0,1:T(8,128)S(1)}, s32[128,7]{0,1:T(8,128)S(1)}, u32[]{:S(2)}, u32[]{:S(2)}) collective-permute-start(s32[128,7]{0,1:T(8,128)S(1)} %copy-done.59), channel_id=1, source_target_pairs={{0,8},{8,0},{16,24},{24,16},{1,9},{9,1},{17,25},{25,17},{2,10},{10... | collective-permute-start | bytes 10760 | tf_op jit(solution)/shard_map/ppermute | solution.py:104
  100.9 92.9 %all-to-all-start.2 = ((bf16[4,320,896]{2,1,0:T(8,128)(2,1)}), bf16[4,320,896]{2,1,0:T(8,128)(2,1)}, u32[]{:S(2)}, u32[]{:S(2)}) async-start(bf16[4,320,896]{2,1,0:T(8,128)(2,1)} %get-tuple-element.178), calls=%async_computation.2 | async-start | bytes 4587520 | tf_op jit(solution)/shard_map/all_to_all | solution.py:127
  109.6 80.7 %copy-start.57 = (f32[128]{0:T(128)}, f32[128]{0:T(128)S(1)}, u32[]{:S(2)}) copy-start(f32[128]{0:T(128)S(1)} %add_rsqrt_fusion.1) | copy-start | bytes 1540
  109.7 80.6 %copy-start.54 = (s32[8]{0:T(128)}, s32[8]{0:T(128)S(1)}, u32[]{:S(2)}) copy-start(s32[8]{0:T(128)S(1)} %multiply_add_fusion.9) | copy-start | bytes 100
  110.0 209.2 %copy-start.43 = (pred[8,4,128]{2,0,1:T(8,128)(4,1)}, pred[8,4,128]{2,0,1:T(8,128)(4,1)S(1)}, u32[]{:S(2)}) copy-start(pred[8,4,128]{2,0,1:T(8,128)(4,1)S(1)} %convolution_compare_fusion) | copy-start | bytes 12292
  191.9 14.5 %copy-start.39 = (bf16[128,1280]{0,1:T(8,128)(2,1)}, bf16[128,1280]{0,1:T(8,128)(2,1)S(1)}, u32[]{:S(2)}) copy-start(bf16[128,1280]{0,1:T(8,128)(2,1)S(1)} %copy.386) | copy-start | bytes 983044
  193.9 91.5 %all-to-all-start.4 = ((bf16[4,320,896]{2,1,0:T(8,128)(2,1)}), bf16[4,320,896]{2,1,0:T(8,128)(2,1)}, u32[]{:S(2)}, u32[]{:S(2)}) async-start(bf16[4,320,896]{2,1,0:T(8,128)(2,1)} %get-tuple-element.179), calls=%async_computation.4 | async-start | bytes 4587520 | tf_op jit(solution)/shard_map/all_to_all | solution.py:127
  210.3 72.8 %copy-start.52 = (f32[128]{0:T(128)}, f32[128]{0:T(128)S(1)}, u32[]{:S(2)}) copy-start(f32[128]{0:T(128)S(1)} %add_rsqrt_fusion) | copy-start | bytes 1540
  210.4 71.3 %copy-start.26 = (bf16[128,1280]{1,0:T(8,128)(2,1)}, bf16[128,1280]{1,0:T(8,128)(2,1)S(1)}, u32[]{:S(2)}) copy-start(bf16[128,1280]{1,0:T(8,128)(2,1)S(1)} %multiply_convert_fusion.4) | copy-start | bytes 983044
  210.4 66.0 %collective-permute-start.5 = (bf16[128,1280]{1,0:T(8,128)(2,1)S(1)}, bf16[128,1280]{1,0:T(8,128)(2,1)S(1)}, u32[]{:S(2)}, u32[]{:S(2)}) collective-permute-start(bf16[128,1280]{1,0:T(8,128)(2,1)S(1)} %multiply_convert_fusion.4), channel_id=1, source_target_pairs={{0,24},{8,16},{16,8},{24,0},{1,25},{9,17},{17,9},{25,1},{2,26},{10... | collective-permute-start | bytes 983048 | tf_op jit(solution)/shard_map/ppermute | solution.py:104
  211.1 70.7 %collective-permute-start.4 = (bf16[128,1280]{1,0:T(8,128)(2,1)S(1)}, bf16[128,1280]{1,0:T(8,128)(2,1)S(1)}, u32[]{:S(2)}, u32[]{:S(2)}) collective-permute-start(bf16[128,1280]{1,0:T(8,128)(2,1)S(1)} %multiply_convert_fusion.4), channel_id=1, source_target_pairs={{0,16},{8,24},{16,0},{24,8},{1,17},{9,25},{17,1},{25,9},{2,18},{10... | collective-permute-start | bytes 983048 | tf_op jit(solution)/shard_map/ppermute | solution.py:104
  214.3 67.4 %collective-permute-start.3 = (bf16[128,1280]{1,0:T(8,128)(2,1)S(1)}, bf16[128,1280]{1,0:T(8,128)(2,1)S(1)}, u32[]{:S(2)}, u32[]{:S(2)}) collective-permute-start(bf16[128,1280]{1,0:T(8,128)(2,1)S(1)} %multiply_convert_fusion.4), channel_id=1, source_target_pairs={{0,8},{8,0},{16,24},{24,16},{1,9},{9,1},{17,25},{25,17},{2,10},{10... | collective-permute-start | bytes 983048 | tf_op jit(solution)/shard_map/ppermute | solution.py:104
  285.4 51.0 %all-to-all-start.1 = ((bf16[8,4,48,1280]{3,2,1,0:T(8,128)(2,1)}), bf16[8,4,48,1280]{3,2,1,0:T(8,128)(2,1)}, u32[]{:S(2)}, u32[]{:S(2)}) async-start(bf16[8,4,48,1280]{3,2,1,0:T(8,128)(2,1)} %copy.394), calls=%async_computation.1 | async-start | bytes 7864320 | tf_op jit(solution)/shard_map/all_to_all | solution.py:191
  290.1 24.6 %collective-permute-start.11 = (bf16[128,1280]{1,0:T(8,128)(2,1)S(1)}, bf16[128,1280]{1,0:T(8,128)(2,1)S(1)}, u32[]{:S(2)}, u32[]{:S(2)}) collective-permute-start(bf16[128,1280]{1,0:T(8,128)(2,1)S(1)} %copy-done.22), channel_id=1, source_target_pairs={{0,24},{8,16},{16,8},{24,0},{1,25},{9,17},{17,9},{25,1},{2,26},{10... | collective-permute-start | bytes 983048 | tf_op jit(solution)/shard_map/ppermute | solution.py:104
  290.7 28.5 %collective-permute-start.10 = (bf16[128,1280]{1,0:T(8,128)(2,1)S(1)}, bf16[128,1280]{1,0:T(8,128)(2,1)S(1)}, u32[]{:S(2)}, u32[]{:S(2)}) collective-permute-start(bf16[128,1280]{1,0:T(8,128)(2,1)S(1)} %copy-done.22), channel_id=1, source_target_pairs={{0,16},{8,24},{16,0},{24,8},{1,17},{9,25},{17,1},{25,9},{2,18},{10... | collective-permute-start | bytes 983048 | tf_op jit(solution)/shard_map/ppermute | solution.py:104
  295.0 24.2 %collective-permute-start.9 = (bf16[128,1280]{1,0:T(8,128)(2,1)S(1)}, bf16[128,1280]{1,0:T(8,128)(2,1)S(1)}, u32[]{:S(2)}, u32[]{:S(2)}) collective-permute-start(bf16[128,1280]{1,0:T(8,128)(2,1)S(1)} %copy-done.22), channel_id=1, source_target_pairs={{0,8},{8,0},{16,24},{24,16},{1,9},{9,1},{17,25},{25,17},{2,10},{10... | collective-permute-start | bytes 983048 | tf_op jit(solution)/shard_map/ppermute | solution.py:104
  314.7 5.7 copy-start.36
  322.7 18.4 %copy-start.19 = (f32[3,40,896]{2,1,0:T(8,128)S(1)}, f32[3,40,896]{2,1,0:T(8,128)}, u32[]{:S(2)}) copy-start(f32[3,40,896]{2,1,0:T(8,128)} %param.27) | copy-start | bytes 1290244
  336.4 50.9 %all-to-all-start.7 = ((bf16[8,4,48,1280]{3,2,1,0:T(8,128)(2,1)}), bf16[8,4,48,1280]{3,2,1,0:T(8,128)(2,1)}, u32[]{:S(2)}, u32[]{:S(2)}) async-start(bf16[8,4,48,1280]{3,2,1,0:T(8,128)(2,1)} %copy.402), calls=%async_computation.7 | async-start | bytes 7864320 | tf_op jit(solution)/shard_map/all_to_all | solution.py:191
  387.3 29.1 %copy-start.55 = (s32[8]{0:T(128)S(1)}, s32[8]{0:T(128)}, u32[]{:S(2)}) copy-start(s32[8]{0:T(128)} %copy-done.54) | copy-start | bytes 100
  387.3 30.6 %copy-start.44 = (pred[8,4,128]{2,0,1:T(8,128)(4,1)S(1)}, pred[8,4,128]{2,0,1:T(8,128)(4,1)}, u32[]{:S(2)}) copy-start(pred[8,4,128]{2,0,1:T(8,128)(4,1)} %copy-done.43) | copy-start | bytes 12292
  401.6 8.0 all-to-all-start.9
  405.0 34.6 %copy-start.33 = (f32[4,128,32]{1,2,0:T(8,128)}, f32[4,128,32]{1,2,0:T(8,128)S(1)}, u32[]{:S(2)}) copy-start(f32[4,128,32]{1,2,0:T(8,128)S(1)} %broadcast_divide_fusion.1) | copy-start | bytes 196612
  409.6 12.5 %all-to-all-start.6 = ((bf16[4,3,40,224]{3,2,1,0:T(8,128)(2,1)}), bf16[4,3,40,224]{3,2,1,0:T(8,128)(2,1)S(1)}, u32[]{:S(2)}, u32[]{:S(2)}) async-start(bf16[4,3,40,224]{3,2,1,0:T(8,128)(2,1)} %copy.396), calls=%async_computation.6 | async-start | bytes 491520 | tf_op jit(solution)/shard_map/all_to_all | solution.py:132
  422.1 8.0 all-to-all-start
  425.4 38.7 %all-gather.6.cloned.1.call-start = ((), (), s32[]{:S(2)}) async-start(), calls=%async_computation.16 | async-start | bytes 2211840 | tf_op jit(solution)/shard_map/all_gather | solution.py:133
  439.6 7.7 copy-start.12
  439.6 7.7 copy-start.13
  454.8 5.1 copy-start.62
  454.9 51.4 %all-to-all-start.8 = ((bf16[8,4,48,1280]{3,2,1,0:T(8,128)(2,1)}), bf16[8,4,48,1280]{3,2,1,0:T(8,128)(2,1)}, u32[]{:S(2)}, u32[]{:S(2)}) async-start(bf16[8,4,48,1280]{3,2,1,0:T(8,128)(2,1)} %bitcast.302), calls=%async_computation.8 | async-start | bytes 7864320 | tf_op jit(solution)/shard_map/all_to_all | solution.py:196
  506.3 58.8 %all-to-all-start.5 = ((bf16[8,4,48,1280]{3,2,1,0:T(8,128)(2,1)}), bf16[8,4,48,1280]{3,2,1,0:T(8,128)(2,1)}, u32[]{:S(2)}, u32[]{:S(2)}) async-start(bf16[8,4,48,1280]{3,2,1,0:T(8,128)(2,1)} %bitcast.301), calls=%async_computation.5 | async-start | bytes 7864320 | tf_op jit(solution)/shard_map/all_to_all | solution.py:196
  510.8 131.8 %all-reduce.5.cloned.1.call-start = ((), (), s32[]{:S(2)}) async-start(), calls=%async_computation.17 | async-start | bytes 3932160
  521.1 7.0 collective-permute-start.17
  523.0 5.0 collective-permute-start.16
  525.9 3.7 collective-permute-start.15
  527.8 408.2 %reduce-scatter.6.cloned.1.call-start = ((), (), s32[]{:S(2)}) async-start(), calls=%async_computation.18 | async-start | bytes 13854720
  534.9 38.7 %collective-permute-start.14 = (bf16[128,1280]{1,0:T(8,128)(2,1)}, bf16[128,1280]{1,0:T(8,128)(2,1)}, u32[]{:S(2)}, u32[]{:S(2)}) collective-permute-start(bf16[128,1280]{1,0:T(8,128)(2,1)} %get-tuple-element.188), channel_id=1, source_target_pairs={{0,24},{8,16},{16,8},{24,0},{1,25},{9,17},{17,9},{25,1},{2,26},{10... | collective-permute-start | bytes 983048 | tf_op jit(solution)/shard_map/ppermute | solution.py:104
  536.4 37.4 %collective-permute-start.13 = (bf16[128,1280]{1,0:T(8,128)(2,1)}, bf16[128,1280]{1,0:T(8,128)(2,1)}, u32[]{:S(2)}, u32[]{:S(2)}) collective-permute-start(bf16[128,1280]{1,0:T(8,128)(2,1)} %get-tuple-element.189), channel_id=1, source_target_pairs={{0,16},{8,24},{16,0},{24,8},{1,17},{9,25},{17,1},{25,9},{2,18},{10... | collective-permute-start | bytes 983048 | tf_op jit(solution)/shard_map/ppermute | solution.py:104
  538.2 29.8 %copy-start.16 = (bf16[1,4,8,40,224]{4,3,2,1,0:T(8,128)(2,1)S(1)}, bf16[1,4,8,40,224]{4,3,2,1,0:T(8,128)(2,1)}, u32[]{:S(2)}) copy-start(bf16[1,4,8,40,224]{4,3,2,1,0:T(8,128)(2,1)} %copy.399) | copy-start | bytes 1720324
  538.2 35.6 %collective-permute-start.12 = (bf16[128,1280]{1,0:T(8,128)(2,1)}, bf16[128,1280]{1,0:T(8,128)(2,1)}, u32[]{:S(2)}, u32[]{:S(2)}) collective-permute-start(bf16[128,1280]{1,0:T(8,128)(2,1)} %get-tuple-element.187), channel_id=1, source_target_pairs={{0,8},{8,0},{16,24},{24,16},{1,9},{9,1},{17,25},{25,17},{2,10},{10... | collective-permute-start | bytes 983048 | tf_op jit(solution)/shard_map/ppermute | solution.py:104
  568.1 5.8 copy-start.53
  568.6 27.1 %copy-start.18 = (f32[128,1280]{1,0:T(8,128)S(1)}, f32[128,1280]{1,0:T(8,128)}, u32[]{:S(2)}) copy-start(f32[128,1280]{1,0:T(8,128)} %get-tuple-element.222) | copy-start | bytes 1966084
  568.6 27.1 %copy-start.23 = (bf16[128,1280]{1,0:T(8,128)(2,1)S(1)}, bf16[128,1280]{1,0:T(8,128)(2,1)}, u32[]{:S(2)}) copy-start(bf16[128,1280]{1,0:T(8,128)(2,1)} %param.21) | copy-start | bytes 983044
  568.7 27.1 %copy-start.60 = (f32[128]{0:T(128)S(1)}, f32[128]{0:T(128)}, u32[]{:S(2)}) copy-start(f32[128]{0:T(128)} %get-tuple-element.155) | copy-start | bytes 1540
  568.7 23.5 %collective-permute-start.8 = (bf16[128,1280]{1,0:T(8,128)(2,1)S(1)}, bf16[128,1280]{1,0:T(8,128)(2,1)S(1)}, u32[]{:S(2)}, u32[]{:S(2)}) collective-permute-start(bf16[128,1280]{1,0:T(8,128)(2,1)S(1)} %get-tuple-element.191), channel_id=1, source_target_pairs={{0,24},{8,16},{16,8},{24,0},{1,25},{9,17},{17,9},{25,1},{2,26},{10... | collective-permute-start | bytes 983048 | tf_op jit(solution)/shard_map/ppermute | solution.py:104
  570.7 25.0 %collective-permute-start.7 = (bf16[128,1280]{1,0:T(8,128)(2,1)S(1)}, bf16[128,1280]{1,0:T(8,128)(2,1)S(1)}, u32[]{:S(2)}, u32[]{:S(2)}) collective-permute-start(bf16[128,1280]{1,0:T(8,128)(2,1)S(1)} %get-tuple-element.192), channel_id=1, source_target_pairs={{0,16},{8,24},{16,0},{24,8},{1,17},{9,25},{17,1},{25,9},{2,18},{10... | collective-permute-start | bytes 983048 | tf_op jit(solution)/shard_map/ppermute | solution.py:104
  573.7 22.0 %collective-permute-start.6 = (bf16[128,1280]{1,0:T(8,128)(2,1)S(1)}, bf16[128,1280]{1,0:T(8,128)(2,1)S(1)}, u32[]{:S(2)}, u32[]{:S(2)}) collective-permute-start(bf16[128,1280]{1,0:T(8,128)(2,1)S(1)} %get-tuple-element.190), channel_id=1, source_target_pairs={{0,8},{8,0},{16,24},{24,16},{1,9},{9,1},{17,25},{25,17},{2,10},{10... | collective-permute-start | bytes 983048 | tf_op jit(solution)/shard_map/ppermute | solution.py:104
  605.4 8.5 copy-start.25
  644.9 15.6 %all-to-all-start.10 = ((bf16[4,3,40,224]{3,2,1,0:T(8,128)(2,1)}), bf16[4,3,40,224]{3,2,1,0:T(8,128)(2,1)S(1)}, u32[]{:S(2)}, u32[]{:S(2)}) async-start(bf16[4,3,40,224]{3,2,1,0:T(8,128)(2,1)} %copy.419), calls=%async_computation.10 | async-start | bytes 491520 | tf_op jit(solution)/shard_map/all_to_all | solution.py:322
  660.5 61.0 %all-to-all-start.13 = ((bf16[4,320,896]{2,1,0:T(8,128)(2,1)}), bf16[4,320,896]{2,1,0:T(8,128)(2,1)}, u32[]{:S(2)}, u32[]{:S(2)}) async-start(bf16[4,320,896]{2,1,0:T(8,128)(2,1)} %bitcast.306), calls=%async_computation.13 | async-start | bytes 4587520 | tf_op jit(solution)/shard_map/all_to_all | solution.py:307
  721.5 76.7 %all-to-all-start.12 = ((bf16[4,320,896]{2,1,0:T(8,128)(2,1)}), bf16[4,320,896]{2,1,0:T(8,128)(2,1)}, u32[]{:S(2)}, u32[]{:S(2)}) async-start(bf16[4,320,896]{2,1,0:T(8,128)(2,1)} %bitcast.307), calls=%async_computation.12 | async-start | bytes 4587520 | tf_op jit(solution)/shard_map/all_to_all | solution.py:307
  798.2 21.4 %copy-start.20 = (f32[3,40,896]{2,1,0:T(8,128)S(1)}, f32[3,40,896]{2,1,0:T(8,128)}, u32[]{:S(2)}) copy-start(f32[3,40,896]{2,1,0:T(8,128)} %param.27) | copy-start | bytes 1290244
  798.2 21.4 %copy-start.35 = (f32[3,40,896]{2,1,0:T(8,128)S(1)}, f32[3,40,896]{2,1,0:T(8,128)}, u32[]{:S(2)}) copy-start(f32[3,40,896]{2,1,0:T(8,128)} %param.29) | copy-start | bytes 1290244
  798.2 74.3 %all-to-all-start.11 = ((bf16[4,320,896]{2,1,0:T(8,128)(2,1)}), bf16[4,320,896]{2,1,0:T(8,128)(2,1)}, u32[]{:S(2)}, u32[]{:S(2)}) async-start(bf16[4,320,896]{2,1,0:T(8,128)(2,1)} %bitcast.305), calls=%async_computation.11 | async-start | bytes 4587520 | tf_op jit(solution)/shard_map/all_to_all | solution.py:307
  872.5 32.5 %copy-start.32 = (f32[128,1280]{1,0:T(8,128)S(1)}, f32[128,1280]{1,0:T(8,128)}, u32[]{:S(2)}) copy-start(f32[128,1280]{1,0:T(8,128)} %get-tuple-element.231) | copy-start | bytes 1966084
  941.3 4.9 copy-start.7
  941.3 4.9 copy-start.31
  (40 other events, 101.7 us)
Sparse Core Ops, SparseCore 0:
  12.3 170.9 all-gather.3
  641.5 294.5 reduce-scatter.5
Sparse Core Ops, SparseCore 1:
  428.4 29.1 all-gather.5
  527.9 78.0 all-reduce.4

commit v2 on v1

v2 whole, which is shorter than its diff:
```python
import functools
import math

import jax
import jax.numpy as jnp
from jax import lax
from jax.experimental import pallas as pl
from jax.experimental.pallas import tpu as pltpu
from jax.sharding import PartitionSpec as P

HEADS = 10
HD = 128
TOPK = 7
STEP = 3
BF = jnp.bfloat16
F32 = jnp.float32

epsilon = 1e-06
momentum_decay = 0.9
masked_score = -1e30
rate_attn = 5e-05
rate_output = 0.0002
rate_shared = 0.0001
rate_router = 3e-05
rate_gain = 0.002
rate_expert = 0.0015
ALL = ("dp", "expert")


def rope_tables(length, size):
    half = size // 2
    freq = jnp.exp(jnp.arange(half, dtype=F32) * (-2.0 * math.log(10000.0) / size))
    angle = jnp.arange(length, dtype=F32)[:, None] * freq[None, :]
    cosine = jnp.concatenate([jnp.cos(angle), jnp.cos(angle)], -1)
    sine = jnp.concatenate([jnp.sin(angle), jnp.sin(angle)], -1)
    return (cosine, sine)


def update(weight, moment, average, grad, rate):
    moment_new = momentum_decay * moment + grad
    weight_new = weight - rate * (grad + momentum_decay * moment_new)
    average_new = average + (weight_new - average) / (STEP + 1.0)
    return (weight_new, moment_new, average_new)


def mm(a, b):
    return jnp.dot(a, b, preferred_element_type=F32)


def mm_nt(a, b):
    return lax.dot_general(a, b, (((1,), (1,)), ((), ())), preferred_element_type=F32)


def mm_tn(a, b):
    return lax.dot_general(a, b, (((0,), (0,)), ((), ())), preferred_element_type=F32)


def attend_probs(heads_ref, doc_row_ref, doc_col_ref, block):
    share = heads_ref.shape[2] // HD

    def head(b):
        return heads_ref[b // share, :, (b % share) * HD : (b % share + 1) * HD]

    length = heads_ref.shape[1]
    row = lax.broadcasted_iota(jnp.int32, (length, length), 0)
    col = lax.broadcasted_iota(jnp.int32, (length, length), 1)
    allowed = (col <= row) & (doc_row_ref[...] == doc_col_ref[...])
    query, key = head(block), head(HEADS + block)
    scores = jnp.where(allowed, mm_nt(query, key) * HD ** (-0.5), masked_score)
    exponent = jnp.exp(scores - jnp.max(scores, -1, keepdims=True))
    probs = exponent / jnp.sum(exponent, -1, keepdims=True)
    return query, key, head(2 * HEADS + block), probs


def attend_kernel(heads_ref, doc_row_ref, doc_col_ref, out_ref):
    for h in range(HEADS):
        _, _, value, probs = attend_probs(heads_ref, doc_row_ref, doc_col_ref, h)
        out_ref[:, h * HD : (h + 1) * HD] = mm(probs.astype(BF), value).astype(BF)


def attend(heads, doc_row, doc_col):
    return pl.pallas_call(
        attend_kernel,
        out_shape=jax.ShapeDtypeStruct((heads.shape[1], HEADS * HD), BF),
        compiler_params=pltpu.CompilerParams(vmem_limit_bytes=24 << 20),
        name="attend",
    )(heads, doc_row, doc_col)


def out_kernel(heads_ref, tokens_ref, w_ref, gain_ref, middle_ref, inner_ref, square_ref):
    attn_out = mm(heads_ref[...], w_ref[...])
    middle = tokens_ref[...].astype(F32) + attn_out
    scale = lax.rsqrt(jnp.mean(middle * middle, -1, keepdims=True) + epsilon)
    middle_ref[...] = middle
    inner_ref[...] = (middle * scale * gain_ref[...]).astype(BF)
    square = jnp.sum(attn_out * attn_out, -1, keepdims=True)
    square_ref[...] = jnp.broadcast_to(square, square_ref.shape)


def project_out(heads_out, tokens, packed, gain):
    length, width = tokens.shape
    return pl.pallas_call(
        out_kernel,
        grid=(1,),
        in_specs=[
            pl.BlockSpec((length, width), lambda i: (0, 0)),
            pl.BlockSpec((length, width), lambda i: (0, 0)),
            pl.BlockSpec((width, width), lambda i: (0, 0)),
            pl.BlockSpec((1, width), lambda i: (0, 0)),
        ],
        out_specs=[
            pl.BlockSpec((length, width), lambda i: (0, 0)),
            pl.BlockSpec((length, width), lambda i: (0, 0)),
            pl.BlockSpec((length, 128), lambda i: (0, 0)),
        ],
        out_shape=[
            jax.ShapeDtypeStruct((length, width), F32),
            jax.ShapeDtypeStruct((length, width), BF),
            jax.ShapeDtypeStruct((length, 128), F32),
        ],
        compiler_params=pltpu.CompilerParams(vmem_limit_bytes=24 << 20),
        name="project_out",
    )(heads_out, tokens, packed, gain)


def attend_back_kernel(
    ig_ref, g_ref, middle_ref, w_ref, gain_ref, heads_ref, doc_row_ref, doc_col_ref,
    cos_ref, sin_ref, mg_ref, ag_ref, gain_out, out_ref, hg_ref
):
    grad = ig_ref[...]
    middle = middle_ref[...]
    scale = lax.rsqrt(jnp.mean(middle * middle, -1, keepdims=True) + epsilon)
    unit = middle * scale
    scaled = grad * gain_ref[...]
    gain_out[...] = jnp.sum(grad * unit, 0, keepdims=True)
    middle_grad = g_ref[...].astype(F32) + scale * (
        scaled - unit * jnp.mean(scaled * unit, -1, keepdims=True)
    )
    mg_ref[...] = middle_grad
    attn_grad = middle_grad.astype(BF)
    ag_ref[...] = attn_grad
    hg_ref[...] = mm_nt(attn_grad, w_ref[...]).astype(BF)
    share = heads_ref.shape[2] // HD

    def put(b, value):
        out_ref[b // share, :, (b % share) * HD : (b % share + 1) * HD] = value

    lane = lax.broadcasted_iota(jnp.int32, cos_ref.shape, 1)
    sign_sin = jnp.where(lane < HD // 2, -sin_ref[...], sin_ref[...])

    def rotate_back(z):
        return (z * cos_ref[...] + pltpu.roll(z * sign_sin, HD // 2, 1)).astype(BF)

    for h in range(HEADS):
        query, key, value, probs = attend_probs(heads_ref, doc_row_ref, doc_col_ref, h)
        out_grad = hg_ref[:, h * HD : (h + 1) * HD]
        prob_grad = mm_nt(out_grad, value)
        score_grad = (
            probs * (prob_grad - jnp.sum(probs * prob_grad, -1, keepdims=True))
        ).astype(BF)
        put(h, rotate_back(mm(score_grad, key) * HD ** (-0.5)))
        put(HEADS + h, rotate_back(mm_tn(score_grad, query) * HD ** (-0.5)))
        put(2 * HEADS + h, mm_tn(probs.astype(BF), out_grad).astype(BF))
    for b in range(3 * HEADS, heads_ref.shape[0] * share):
        put(b, jnp.zeros((heads_ref.shape[1], HD), BF))


def attend_back(grad, cotangent, middle, packed, gain, heads, doc_row, doc_col, cosine, sine):
    length, width = middle.shape
    whole = pl.BlockSpec((length, width), lambda i: (0, 0))
    table = pl.BlockSpec((length, HD), lambda i: (0, 0))
    row = pl.BlockSpec((1, width), lambda i: (0, 0))
    blocks = pl.BlockSpec(heads.shape, lambda i: (0, 0, 0))
    return pl.pallas_call(
        attend_back_kernel,
        grid=(1,),
        in_specs=[
            whole,
            whole,
            whole,
            pl.BlockSpec((width, width), lambda i: (0, 0)),
            row,
            blocks,
            pl.BlockSpec((1, length), lambda i: (0, 0)),
            pl.BlockSpec((length, 1), lambda i: (0, 0)),
            table,
            table,
        ],
        out_specs=[whole, whole, row, blocks],
        out_shape=[
            jax.ShapeDtypeStruct((length, width), F32),
            jax.ShapeDtypeStruct((length, width), BF),
            jax.ShapeDtypeStruct((1, width), F32),
            jax.ShapeDtypeStruct(heads.shape, BF),
        ],
        scratch_shapes=[pltpu.VMEM((length, width), BF)],
        compiler_params=pltpu.CompilerParams(vmem_limit_bytes=32 << 20),
        name="attend_back",
    )(grad, cotangent, middle, packed, gain, heads, doc_row, doc_col, cosine, sine)


def load_pieces(zi, pieces, dest, sem):
    depth = pieces[0].shape[1]
    copies = [
        pltpu.make_async_copy(
            piece,
            dest.at[:, pl.ds(pl.multiple_of((zi ^ k) * depth, 16), depth)],
            sem.at[k],
        )
        for k, piece in enumerate(pieces)
    ]
    for copy in copies:
        copy.start()
    for copy in copies:
        copy.wait()


def front_kernel(count, place_ref, x_ref, hot_ref, router_ref, *rest):
    pieces = rest[:count]
    eg_ref, eu_ref, gated_ref, gate_ref, w_ref, sem = rest[count:]

    @pl.when(pl.program_id(0) == 0)
    def _():
        half = count // 2
        load_pieces(place_ref[0], pieces[:half], w_ref.at[pl.ds(0, 1)], sem)
        load_pieces(place_ref[0], pieces[half:], w_ref.at[pl.ds(1, 1)], sem)

    x = x_ref[...]
    hot = hot_ref[...].astype(F32) > 0.5
    chosen = jnp.where(hot, mm(x, router_ref[...]), masked_score)
    top = jnp.max(chosen, -1, keepdims=True)
    exponent = jnp.where(hot, jnp.exp(chosen - top), 0.0)
    lane = lax.broadcasted_iota(jnp.int32, exponent.shape, 1)
    own = jnp.sum(jnp.where(lane == place_ref[1], exponent, 0.0), -1, keepdims=True)
    gate = own / jnp.maximum(jnp.sum(exponent, -1, keepdims=True), 0.5)
    eg = mm(x, w_ref[0])
    eu = mm(x, w_ref[1])
    eg_ref[...] = eg
    eu_ref[...] = eu
    gated_ref[...] = (gate * (eg * jax.nn.sigmoid(eg) * eu)).astype(BF)
    gate_ref[...] = jnp.broadcast_to(gate, gate_ref.shape)


def tile_of(count):
    return next(t for t in (256, 192, 128, 64, 48, 16, 8) if count % t == 0)


def expert_front(place, rows, grads_hot, router, pieces):
    count, width = rows.shape
    hidden = pieces[0].shape[2]
    tile = tile_of(count)
    extra = grads_hot.shape[1] - width
    flops = 4 * count * width * hidden
    return pl.pallas_call(
        functools.partial(front_kernel, len(pieces)),
        grid_spec=pltpu.PrefetchScalarGridSpec(
            num_scalar_prefetch=1,
            grid=(count // tile,),
            in_specs=[
                pl.BlockSpec((tile, width), lambda i, p: (i, 0)),
                pl.BlockSpec((tile, extra), lambda i, p: (i, width // extra)),
                pl.BlockSpec((width, extra), lambda i, p: (0, 0)),
            ]
            + [pl.BlockSpec(memory_space=pl.ANY)] * len(pieces),
            out_specs=[pl.BlockSpec((tile, hidden), lambda i, p: (i, 0))] * 3
            + [pl.BlockSpec((tile, 128), lambda i, p: (i, 0))],
            scratch_shapes=[
                pltpu.VMEM((2, width, hidden), BF),
                pltpu.SemaphoreType.DMA((len(pieces),)),
            ],
        ),
        out_shape=[
            jax.ShapeDtypeStruct((count, hidden), F32),
            jax.ShapeDtypeStruct((count, hidden), F32),
            jax.ShapeDtypeStruct((count, hidden), BF),
            jax.ShapeDtypeStruct((count, 128), F32),
        ],
        cost_estimate=pl.CostEstimate(
            flops=flops, bytes_accessed=12 * count * hidden, transcendentals=0
        ),
        compiler_params=pltpu.CompilerParams(vmem_limit_bytes=40 << 20),
        name="expert_front",
    )(place, rows, grads_hot, router, *pieces)


def back_kernel(count, place_ref, g_ref, eg_ref, eu_ref, gated_ref, gate_ref, *rest):
    gate_w, up_w, down = rest[:count], rest[count : 2 * count], rest[2 * count : 3 * count]
    rows_ref, routed_ref, egg_ref, eug_ref, gg_ref, w_ref, wd_ref, sem = rest[3 * count :]

    @pl.when(pl.program_id(0) == 0)
    def _():
        load_pieces(place_ref[0], down, wd_ref, sem)
        load_pieces(place_ref[0], gate_w, w_ref.at[pl.ds(0, 1)], sem)
        load_pieces(place_ref[0], up_w, w_ref.at[pl.ds(1, 1)], sem)

    eg = eg_ref[...]
    eu = eu_ref[...]
    sig = jax.nn.sigmoid(eg)
    silu = eg * sig
    plain = mm(g_ref[...], wd_ref[0])
    gate_grad = jnp.sum(silu * eu * plain, -1, keepdims=True)
    gg_ref[0] = jnp.broadcast_to(gate_grad, (gate_grad.shape[0], 128)).T[:8]
    grad = gate_ref[:, :1] * plain
    eg_grad = (grad * eu * sig * (1.0 + eg * (1.0 - sig))).astype(BF)
    eu_grad = (grad * silu).astype(BF)
    egg_ref[...] = eg_grad
    eug_ref[...] = eu_grad
    rows_ref[...] = (mm_nt(eg_grad, w_ref[0]) + mm_nt(eu_grad, w_ref[1])).astype(BF)
    routed_ref[...] = mm_nt(gated_ref[...], wd_ref[0]).astype(BF)


def expert_back(place, grads_hot, eg, eu, gated, gate, front, down, tile):
    count, hidden = eg.shape
    deep = front[0].shape[1]
    width = deep * len(down)
    wide = pl.BlockSpec((tile, width), lambda i, p: (i, 0))
    thin = pl.BlockSpec((tile, hidden), lambda i, p: (i, 0))
    lanes = pl.BlockSpec((tile, 128), lambda i, p: (i, 0))
    return pl.pallas_call(
        functools.partial(back_kernel, len(down)),
        grid_spec=pltpu.PrefetchScalarGridSpec(
            num_scalar_prefetch=1,
            grid=(count // tile,),
            in_specs=[wide, thin, thin, thin, lanes]
            + [pl.BlockSpec(memory_space=pl.ANY)] * (3 * len(down)),
            out_specs=[wide, wide, thin, thin, pl.BlockSpec((1, 8, tile), lambda i, p: (i, 0, 0))],
            scratch_shapes=[
                pltpu.VMEM((2, width, hidden), BF),
                pltpu.VMEM((1, width, hidden), BF),
                pltpu.SemaphoreType.DMA((len(down),)),
            ],
        ),
        out_shape=[
            jax.ShapeDtypeStruct((count, width), BF),
            jax.ShapeDtypeStruct((count, width), BF),
            jax.ShapeDtypeStruct((count, hidden), BF),
            jax.ShapeDtypeStruct((count, hidden), BF),
            jax.ShapeDtypeStruct((count // tile, 8, tile), F32),
        ],
        cost_estimate=pl.CostEstimate(
            flops=8 * count * width * hidden,
            bytes_accessed=16 * count * hidden,
            transcendentals=0,
        ),
        compiler_params=pltpu.CompilerParams(vmem_limit_bytes=48 << 20),
        name="expert_back",
    )(place, grads_hot, eg, eu, gated, gate, *front, *down)


def weight_grads(x, ys, width):
    count = x.shape[0]
    hidden = ys[0].shape[1]
    tile = 256
    return pl.pallas_call(
        grads_body(len(ys)),
        grid=(width // tile,),
        in_specs=[pl.BlockSpec((count, tile), lambda i: (0, i))]
        + [pl.BlockSpec((count, hidden), lambda i: (0, 0))] * len(ys),
        out_specs=pl.BlockSpec((len(ys), tile, hidden), lambda i: (0, i, 0)),
        out_shape=jax.ShapeDtypeStruct((len(ys), width, hidden), BF),
        cost_estimate=pl.CostEstimate(
            flops=2 * len(ys) * count * width * hidden,
            bytes_accessed=2 * count * (width + hidden),
            transcendentals=0,
        ),
        compiler_params=pltpu.CompilerParams(vmem_limit_bytes=40 << 20),
        name="weight_grads",
    )(x, *ys)


def grads_body(many):
    def kernel(x_ref, *rest):
        x = x_ref[...]
        for i in range(many):
            rest[many][i] = mm_tn(x, rest[i][...]).astype(BF)

    return kernel


def update_kernel(place_ref, w_ref, m_ref, a_ref, g_ref, *rest):
    w_out, m_out, a_out = rest[-3:]
    new = update(w_ref[0, 0], m_ref[0, 0], a_ref[0, 0], g_ref[0].astype(F32), rate_expert)
    w_out[0, 0], m_out[0, 0], a_out[0, 0] = new


def update_part(owned, so_far, grad, low, place):
    count, deep, width = grad.shape
    tile = deep // 2
    state = pl.BlockSpec((1, 1, tile, width), lambda m, t, p: (p[0], low + m, t, 0))
    moved = 6 * 4 * grad.size + 2 * grad.size
    return pl.pallas_call(
        update_kernel,
        grid_spec=pltpu.PrefetchScalarGridSpec(
            num_scalar_prefetch=1,
            grid=(count, deep // tile),
            in_specs=[state] * 3
            + [pl.BlockSpec((1, tile, width), lambda m, t, p: (m, t, 0))]
            + [pl.BlockSpec(memory_space=pl.ANY)] * len(so_far),
            out_specs=[state] * 3,
        ),
        out_shape=[jax.ShapeDtypeStruct(x.shape, x.dtype) for x in owned],
        input_output_aliases={5 + i: i for i in range(len(so_far))},
        cost_estimate=pl.CostEstimate(
            flops=8 * grad.size, bytes_accessed=moved, transcendentals=0
        ),
        compiler_params=pltpu.CompilerParams(vmem_limit_bytes=60 << 20),
        name="update_part",
    )(jnp.reshape(place, (1,)).astype(jnp.int32), *owned, grad, *so_far)


def body(
    tokens,
    cotangent,
    routes,
    doc_ids,
    attn_weight,
    attn_momentum,
    attn_average,
    shared_weight,
    shared_momentum,
    shared_average,
    router_weight,
    router_momentum,
    router_average,
    gain_weight,
    gain_momentum,
    gain_average,
    expert_weight,
    expert_momentum,
    expert_average,
):
    Z = lax.axis_size("dp")
    E = lax.axis_size("expert")
    L, D = tokens.shape
    rows_own = attn_weight.shape[1]
    local, _, deep, FF = expert_weight.shape
    experts = router_weight.shape[1]
    parts = Z // local
    FP = FF // parts
    FS = shared_weight.shape[2] // Z
    cap = min(L, (L * TOPK * 3 // (2 * experts) + 7) // 8 * 8)
    zi = lax.axis_index("dp")

    def swap_z(pieces):
        out = [pieces[0]]
        for k in range(1, Z):
            out.append(lax.ppermute(pieces[k], "dp", [(i, i ^ k) for i in range(Z)]))
        return out

    strides = [1 << b for b in range(Z.bit_length() - 1)][::-1]
    offs = [0]
    for stride in strides:
        offs = offs + [o ^ stride for o in offs]

    def gather_z(x, then=()):
        held = x[None]
        for step, stride in enumerate(strides):
            if step > 0 and then:
                held = after(held, *then)
            got = lax.ppermute(held, "dp", [(i, i ^ stride) for i in range(Z)])
            held = jnp.concatenate([held, got], 0)
        return held

    def reduce_z(x):
        for stride in strides[::-1]:
            keep, send = jnp.split(x, 2, 0)
            got = lax.ppermute(send, "dp", [(i, i ^ stride) for i in range(Z)])
            total = keep.astype(F32) + got.astype(F32)
            x = total.astype(BF)
        return total[0]

    R = rows_own
    ei = lax.axis_index("expert")

    def after(x, *needed):
        return lax.optimization_barrier((x,) + needed)[0]

    blocks = 3 * D // HD
    share = -(-blocks // E)
    wide = share * HD
    gain_low = gain_weight.astype(BF).astype(F32)
    folded = (attn_weight[:3].astype(BF).astype(F32) * gain_low[0][None, :, None]).astype(BF)
    folded = jnp.swapaxes(folded, 0, 1).reshape(R, 3 * D)
    folded = jnp.pad(folded, ((0, 0), (0, E * wide - 3 * D)))
    folded = jnp.swapaxes(folded.reshape(R, E, wide), 0, 1)
    folded = jnp.broadcast_to(folded[None], (Z, E, R, wide)).reshape(Z * E, R, wide)
    w_proj = lax.all_to_all(folded, ALL, split_axis=0, concat_axis=0, tiled=True)
    w_proj = w_proj.reshape(D, wide)

    inputs = tokens.astype(F32)
    inv_first = lax.rsqrt(jnp.mean(inputs * inputs, -1, keepdims=True) + epsilon)
    unit_first = inputs * inv_first
    unit_all = lax.all_gather(unit_first.astype(BF), "expert", axis=0, tiled=True)

    extra = jnp.concatenate([router_weight, gain_weight[1:].T], 1).astype(BF)
    extra = jnp.pad(extra, ((0, 0), (0, 128 - extra.shape[1])))
    packed = jnp.concatenate([attn_weight[3].astype(BF), extra], 1)
    packed = lax.all_gather(gather_z(packed), "expert", axis=0, tiled=False)
    full = jnp.zeros((Z, E, R, D + 128), BF)
    for k, o in enumerate(offs):
        full = lax.dynamic_update_slice(full, packed[:, k][None], (zi ^ o, 0, 0, 0))
    packed = full.reshape(D, D + 128)
    w_o = packed[:, :D]
    router_w = packed[:, D : D + experts]
    gain_second = packed[:, D + experts].astype(F32)

    def piece_of(k, low, high):
        there = zi ^ k
        w = lax.dynamic_slice(
            expert_weight,
            (there // parts, low, 0, (there % parts) * FP),
            (1, high - low, deep, FP),
        )
        return w[0].astype(BF)

    def fetch(k, low, high, *needed):
        return lax.ppermute(
            after(piece_of(k, low, high), *needed), "dp", [(i, i ^ k) for i in range(Z)]
        )

    gate_far = fetch(2, 0, 1, w_proj)
    up_far = fetch(2, 1, 2, gate_far)

    cosine, sine = rope_tables(L, HD)
    score_scale = HD ** (-0.5)
    documents = doc_ids[0]
    position = jnp.arange(L)
    allowed = (
        (position[None, :] <= position[:, None]) & (documents[None, :] == documents[:, None])
    )[None]
    turned = (lax.axis_index("expert") * share + jnp.arange(share)) < 2 * D // HD
    turned = turned[None, None, :, None].astype(F32)
    cos_mine = cosine[None, :, None, :] * turned + (1.0 - turned)
    sin_mine = sine[None, :, None, :] * turned
    projected = mm(unit_all, w_proj).reshape(E, L, share, HD)
    half = HD // 2
    crossed = jnp.concatenate([-projected[..., half:], projected[..., :half]], -1)
    heads_in = (projected * cos_mine + crossed * sin_mine).astype(BF).reshape(E, L, wide)
    hot_own = jnp.sum(
        (routes[:, :, None] == jnp.arange(experts, dtype=jnp.int32)).astype(F32), 1
    )
    hot_wide = jnp.pad(hot_own, ((0, 0), (0, 128 - experts))).astype(BF)
    grad_hot = jnp.concatenate([cotangent, hot_wide], 1)
    heads_in = lax.all_to_all(heads_in, "expert", split_axis=0, concat_axis=0, tiled=True)
    grad_hot = gather_z(after(grad_hot, w_proj), (heads_in,))
    grad_in = grad_hot[:, :, :D]
    hot = grad_hot[:, :, D : D + experts].astype(F32)

    doc_row = doc_ids.astype(jnp.int32)
    doc_col = doc_row.reshape(L, 1)
    heads_out = attend(after(heads_in, gate_far), doc_row, doc_col)
    gain_row = gain_second[None, :]
    middle, inner, attn_square = project_out(
        heads_out, tokens, packed, gain_row
    )

    sw = after(shared_weight, inner).astype(BF)
    sw = [lax.dynamic_slice(sw, (0, 0, (zi ^ k) * FS), (3, R, FS)) for k in range(Z)]
    sw = jnp.stack(swap_z(sw), 1)
    sw = lax.all_gather(sw, "expert", axis=2, tiled=False)
    full = jnp.zeros((3, Z, E, R, FS), BF)
    for k in range(Z):
        full = lax.dynamic_update_slice(full, sw[:, k][:, None], (0, zi ^ k, 0, 0, 0))
    shared_w = full.reshape(3, D, FS)

    before = (position[None, :] < position[:, None]).astype(BF)
    rank = jnp.einsum("tu,sux->stx", before, hot.astype(BF), preferred_element_type=F32)
    first = zi // parts
    mine = jnp.arange(E) * local + first
    pick = (jnp.arange(experts)[:, None] == mine[None, :]).astype(F32)
    hot_mine = jnp.einsum("stx,xe->est", hot, pick)
    rank_mine = jnp.einsum("stx,xe->est", rank, pick, precision=lax.Precision.HIGHEST)
    place = (
        (rank_mine[:, :, None, :] == jnp.arange(cap, dtype=F32)[None, None, :, None])
        & (hot_mine[:, :, None, :] > 0.5)
    ).astype(BF)

    def dispatch(x):
        rows = jnp.einsum("esct,std->escd", place, x, preferred_element_type=F32).astype(BF)
        return lax.all_to_all(rows, "expert", split_axis=0, concat_axis=0, tiled=True).reshape(
            E * Z * cap, x.shape[-1]
        )

    def gates_of(logits, hot_in):
        chosen = jnp.where(hot_in > 0.5, logits, masked_score)
        top = jnp.max(chosen, -1, keepdims=True)
        parts_in = jnp.where(hot_in > 0.5, jnp.exp(chosen - top), 0.0)
        return parts_in / jnp.maximum(jnp.sum(parts_in, -1, keepdims=True), 0.5)

    grad_rows_hot = dispatch(grad_hot)

    inner_z = gather_z(after(inner, grad_hot, up_far))
    near = fetch(1, 0, 2, inner_z)
    front = [[piece_of(0, 0, 1), near[:1], gate_far], [piece_of(0, 1, 2), near[1:], up_far]]
    last = up_far
    for k in range(3, Z):
        for m in range(2):
            last = fetch(k, m, m + 1, last)
            front[m].append(last)
    rows = dispatch(after(inner_z, grad_rows_hot, *[f[3] for f in front[:1] if Z > 3]))
    down = [piece_of(0, 2, 3)] + [fetch(k, 2, 3, last) for k in range(1, Z)]

    place_of = jnp.stack([zi, ei * local + first]).astype(jnp.int32)
    router_wide = packed[:, D:]
    eg, eu, gated, gate_col = expert_front(place_of, rows, grad_rows_hot, router_wide, front[0] + front[1])
    down_grad = weight_grads(grad_rows_hot, [gated], D)

    def send_grads(g, last):
        got = [None] * Z
        for k in [0] + list(range(2, Z)) + [1]:
            piece = lax.dynamic_slice(g, (0, (zi ^ k) * deep, 0), (g.shape[0], deep, FP))
            if k > 0:
                piece = after(piece, last) if last is not None else piece
                piece = lax.ppermute(piece, "dp", [(i, i ^ k) for i in range(Z)])
                last = piece if k != 1 else last
            got[k] = piece
        return got, last

    down_got, last_down = send_grads(down_grad, None)
    rows_grad, routed_rows, eg_grad, eu_grad, gate_grad = expert_back(
        place_of, grad_rows_hot, eg, eu, after(gated, down_grad), gate_col, front[0] + front[1], down,
        Z * cap,
    )

    gate_grad_back = lax.all_to_all(
        gate_grad, "expert", split_axis=0, concat_axis=0, tiled=True
    )[:, 0].reshape(E, Z, cap)
    front_grad = weight_grads(
        after(rows, gate_grad_back, down_got[2]), [eg_grad, eu_grad], D
    )
    front_got, _ = send_grads(front_grad, last_down)

    flat_inner = after(inner_z, front_grad).reshape(Z * L, D)
    flat_grad = grad_in.reshape(Z * L, D)
    sg = mm(flat_inner, shared_w[0])
    su = mm(flat_inner, shared_w[1])
    ssig = jax.nn.sigmoid(sg)
    ssilu = sg * ssig
    shared_hidden = (ssilu * su).astype(BF)
    shared_out = mm_nt(shared_hidden, shared_w[2])
    shared_hidden_grad = mm(flat_grad, shared_w[2])
    sg_grad = (shared_hidden_grad * su * ssig * (1.0 + sg * (1.0 - ssig))).astype(BF)
    su_grad = (shared_hidden_grad * ssilu).astype(BF)
    shared_back = mm_nt(sg_grad, shared_w[0]) + mm_nt(su_grad, shared_w[1])
    shared_grads = jnp.stack(
        [mm_tn(flat_inner, sg_grad), mm_tn(flat_inner, su_grad), mm_tn(flat_grad, shared_hidden)]
    ).astype(BF)

    def collect(rows_in, add):
        back = lax.all_to_all(
            rows_in.reshape(E, Z, cap, D), "expert", split_axis=0, concat_axis=0, tiled=True
        )
        total = jnp.einsum("esct,escd->std", place, back, preferred_element_type=F32) + add
        return back, total.astype(BF)

    gate_grad_mine = jnp.sum(place.astype(F32) * gate_grad_back[:, :, :, None], 2)
    gate_grad_z = jnp.einsum(
        "est,xe->stx", gate_grad_mine, pick, precision=lax.Precision.HIGHEST
    ).reshape(Z * L, experts)
    gates_z = gates_of(mm(flat_inner, router_w), hot.reshape(Z * L, experts))
    logit_grad = gates_z * (gate_grad_z - jnp.sum(gates_z * gate_grad_z, -1, keepdims=True))
    router_grad = mm_tn(flat_inner.astype(F32), logit_grad)
    router_back = mm_nt(logit_grad, router_w.astype(F32))

    rows_back, inner_grad = collect(rows_grad, (shared_back + router_back).reshape(Z, L, D))
    inner_grad = reduce_z(after(inner_grad, *down_got[2:]))
    routed_back, branch = collect(after(routed_rows, rows_back), shared_out.reshape(Z, L, D))

    def reduce_rows(x):
        x = jnp.swapaxes(x.reshape(Z, E, R, x.shape[1]), 0, 1).reshape(D, x.shape[1])
        x = lax.psum_scatter(x, "expert", scatter_dimension=0, tiled=True)
        x = x.reshape(Z, R, x.shape[1])
        return jnp.concatenate([lax.dynamic_slice_in_dim(x, zi ^ o, 1, 0) for o in offs], 0)

    middle_grad, attn_grad, second_gain_grad, proj_grad = attend_back(
        after(inner_grad, front_got[2]), cotangent, middle, packed, gain_row, heads_in, doc_row, doc_col, cosine, sine
    )
    output_grad = mm_tn(heads_out, attn_grad)
    pad = jnp.zeros((D, 128 - experts - 1), F32)
    small_all = jnp.concatenate(
        [output_grad, router_grad, second_gain_grad.T, pad], 1
    ).astype(BF)
    small_own = reduce_rows(small_all)

    proj_grad = lax.all_to_all(after(proj_grad, routed_back), "expert", split_axis=0, concat_axis=0, tiled=True)
    proj_grad = proj_grad.reshape(E * L, wide)
    proj_w_grad = mm_tn(unit_all, proj_grad).astype(BF).reshape(Z * E, R, wide)
    proj_w_local = proj_w_grad
    small_own = reduce_z(after(small_own, proj_w_local))
    proj_w_grad = lax.all_to_all(proj_w_grad, ALL, split_axis=0, concat_axis=0, tiled=True)
    proj_sum = jnp.sum(proj_w_grad.reshape(Z, E, R, wide).astype(F32), 0)
    proj_sum = jnp.swapaxes(proj_sum, 0, 1).reshape(R, E * wide)[:, : 3 * D]
    proj_sum = jnp.swapaxes(proj_sum.reshape(R, 3, D), 0, 1)

    back = mm_nt(proj_grad, w_proj).astype(BF)
    back_local = back
    scaled_first = lax.psum_scatter(back, "expert", scatter_dimension=0, tiled=True).astype(F32)
    input_grad = middle_grad + inv_first * (
        scaled_first - unit_first * jnp.mean(scaled_first * unit_first, -1, keepdims=True)
    )

    branch = reduce_z(after(branch, back_local))
    layer_out = (middle + branch).astype(BF)
    first_mask = jnp.concatenate([jnp.ones((1,), bool), documents[1:] != documents[:-1]])
    kept_mask = 1.0 - first_mask.astype(F32)
    kept_total = jnp.sum(kept_mask) * D
    attn_rms = jnp.sqrt(jnp.sum(kept_mask * attn_square[:, 0]) / kept_total)
    branch_rms = jnp.sqrt(jnp.sum(kept_mask[:, None] * branch * branch) / kept_total)
    sublayer_rms = jnp.stack([attn_rms, branch_rms])[None, :]

    first_gain_grad = jnp.sum(proj_sum * attn_weight[:3].astype(BF).astype(F32), (0, 2))
    attn_sum = jnp.concatenate(
        [proj_sum * gain_low[0][None, :, None], small_own[None, :, :D]], 0
    )
    router_sum = small_own[:, D : D + experts]
    gain_sum = jnp.stack([first_gain_grad, small_own[:, D + experts]])

    owned = (expert_weight, expert_momentum, expert_average)
    expert_new = ()
    expert_sum = jnp.zeros((local, 3, deep, FF), BF)
    for m, gots in ((2, down_got), (0, front_got)):
        for k in [0] + list(range(2, Z)) + [1]:
            there = zi ^ k
            got = gots[k]
            if parts == 1:
                if k > 0:
                    got = after(got, proj_w_local, branch)
                expert_new = update_part(owned, expert_new, got, m, there)
            else:
                expert_sum = lax.dynamic_update_slice(
                    expert_sum, got[None], (there // parts, m, 0, (there % parts) * FP)
                )
    if parts > 1:
        expert_new = update(*owned, expert_sum.astype(F32), rate_expert)

    sgr = shared_grads.reshape(3, Z, E, R, FS).transpose(2, 1, 0, 3, 4).reshape(E * Z * 3 * R, FS)
    sgr = lax.psum_scatter(sgr, "expert", scatter_dimension=0, tiled=True)
    sgr = after(sgr.reshape(Z, 3, R, FS), inner_grad)
    got = swap_z(
        [lax.dynamic_index_in_dim(sgr, zi ^ k, 0, keepdims=False) for k in range(Z)]
    )
    shared_sum = jnp.zeros((3, R, Z * FS), BF)
    for k in range(Z):
        shared_sum = lax.dynamic_update_slice(shared_sum, got[k], (0, 0, (zi ^ k) * FS))
    shared_sum = shared_sum.astype(F32)

    attn_rates = jnp.array([rate_attn, rate_attn, rate_attn, rate_output], F32).reshape(4, 1, 1)
    return (
        layer_out,
        input_grad,
        *update(attn_weight, attn_momentum, attn_average, attn_sum, attn_rates),
        *update(shared_weight, shared_momentum, shared_average, shared_sum, rate_shared),
        *update(router_weight, router_momentum, router_average, router_sum, rate_router),
        *update(gain_weight, gain_momentum, gain_average, gain_sum, rate_gain),
        *expert_new,
        sublayer_rms,
    )


def solution(mesh):
    rows = P(ALL, None)
    middle = P(None, ALL, None)
    gains = P(None, ALL)
    routed = P("expert", None, "dp", None)
    weights = (middle,) * 6 + (rows,) * 3 + (gains,) * 3 + (routed,) * 3
    return jax.shard_map(
        body,
        mesh=mesh,
        in_specs=(rows,) * 4 + weights,
        out_specs=(rows,) * 2 + weights + (rows,),
        check_vma=False,
    )
```

time: 967 us -> 687 us (0.71)
  waiting for transfers between devices: 532 us -> 255 us
  Pallas kernels: 0 us -> 114 us
  matrix products: 138 us -> 40.5 us
  other arithmetic: 75.5 us -> 31.6 us
  local copies, waits for them, and re-layouts: 56.1 us -> 91.7 us
  starting transfers between devices: 136 us -> 124 us
    all_to_all x12 -> x7, waiting for transfers between devices: 276 us -> 50.9 us  [the longest x1 27.2 us: body(): lax.all_to_all(folded, ALL, split_axis=0, concat_axis=0, tiled=True)]
    ppermute x0 -> x26, waiting for transfers between devices: none -> 177 us  [the longest x6 73.9 us: reduce_z(): got = lax.ppermute(send, 'dp', [(i, i ^ stride) for i in range(Z)])]
    pallas_call x0 -> x15, Pallas kernels: none -> 114 us  [the longest x8 38.9 us: update_part(): pl.pallas_call(update_kernel, grid_spec=pltpu.PrefetchScalarGridSpec(num_...]
    ppermute x18 -> x6, waiting for transfers between devices: 113 us -> 27.5 us  [swap_z(): out.append(lax.ppermute(pieces[k], 'dp', [(i, i ^ k) for i in range(Z)]))]
    ppermute x0 -> x26, starting transfers between devices: none -> 73 us  [the longest x8 35 us: fetch(): lax.ppermute(after(piece_of(k, low, high), *needed), 'dp', [(i, i ^ k) fo...]
    all_gather x2 -> x3, waiting for transfers between devices: 72.9 us -> 0.02 us  [the longest x1 0.02 us: body(): packed = lax.all_gather(gather_z(packed), 'expert', axis=0, tiled=False)]
    all_to_all x12 -> x7, starting transfers between devices: 99.8 us -> 33 us  [the longest x2 9.49 us: collect(): lax.all_to_all(rows_in.reshape(E, Z, cap, D), 'expert', split_axis=0, con...]
    all_to_all x2, waiting for transfers between devices: 39.2 us -> 0.01 us  [dispatch(): lax.all_to_all(rows, 'expert', split_axis=0, concat_axis=0, tiled=True)]
  transfers between devices with their start and end apart: 36 -> 47, of which waited for: 20 -> 17; matrix products, arithmetic and copies ran while one was open for 25% -> 20% of each run, Pallas kernels for 0% -> 17%
where the time goes in v2:
time: 687 us; the launch traced here: 675 us
  waiting for transfers between devices  255 us (37%)
  starting transfers between devices  124 us (18%)
  Pallas kernels  114 us (17%)
  local copies, waits for them, and re-layouts  91.7 us (13%)
  matrix products  40.5 us (6%)
  other arithmetic  31.6 us (5%)
  between operations  17.9 us (3%)
    ppermute x6, waiting for transfers between devices, reduce_z(): got = lax.ppermute(send, 'dp', [(i, i ^ stride) for i in range(Z)])  73.9 us
    ppermute x6, waiting for transfers between devices, gather_z(): got = lax.ppermute(held, 'dp', [(i, i ^ stride) for i in range(Z)])  46.4 us
    pallas_call x8, Pallas kernels, update_part(): pl.pallas_call(update_kernel, grid_spec=pltpu.PrefetchScalarGridSpec(num_...  38.9 us
    ppermute x8, starting transfers between devices, fetch(): lax.ppermute(after(piece_of(k, low, high), *needed), 'dp', [(i, i ^ k) fo...  35 us
    ppermute x8, waiting for transfers between devices, fetch(): lax.ppermute(after(piece_of(k, low, high), *needed), 'dp', [(i, i ^ k) fo...  32 us
    pallas_call x1, Pallas kernels, expert_back(): pl.pallas_call(functools.partial(back_kernel, len(down)), grid_spec=pltpu...  30.5 us
    ppermute x6, waiting for transfers between devices, swap_z(): out.append(lax.ppermute(pieces[k], 'dp', [(i, i ^ k) for i in range(Z)]))  27.5 us
    all_to_all x1, waiting for transfers between devices, body(): lax.all_to_all(folded, ALL, split_axis=0, concat_axis=0, tiled=True)  27.2 us
  transfers between devices with their start and end apart: 47, of which 17 were waited for; matrix products, arithmetic and copies ran while one was open for 20% of the time, Pallas kernels for 17%

profile of v2, /device:TPU:16, one launch (start us, length us, event | category | flops | bytes accessed | tf_op | source)
XLA Modules:
  0.0 674.9 jit_solution(5199196837355332224)
XLA Ops:
  13.1 5.8 collective-permute-done.1
  18.9 3.8 collective-permute-start.2
  24.4 4.9 all-to-all-start
  31.8 27.2 %all-to-all-done = bf16[32,40,512]{2,1,0:T(8,128)(2,1)S(1)} async-done(((bf16[32,40,512]{2,1,0:T(8,128)(2,1)}), bf16[32,40,512]{2,1,0:T(8,128)(2,1)S(1)}, u32[]{:S(2)}, u32[]{:S(2)}) %all-to-all-start) | async-done | bytes 1310752 | tf_op jit(solution)/shard_map/all_to_all | solution.py:487
  60.5 3.7 fusion.112
  66.3 3.6 all-to-all-start.1
  69.9 2.9 collective-permute-start.3
  72.9 15.5 %collective-permute-done.3 = bf16[1,128,1408]{1,2,0:T(8,128)(2,1)S(1)} collective-permute-done((bf16[1,128,1408]{1,2,0:T(8,128)(2,1)S(1)}, bf16[1,128,1408]{1,2,0:T(8,128)(2,1)S(1)}, u32[]{:S(2)}, u32[]{:S(2)}) %collective-permute-start.3) | collective-permute-done | bytes 360480 | tf_op jit(solution)/shard_map/ppermute | solution.py:460
  88.5 2.9 all-to-all-done.1.heads_ref
  93.5 6.7 fusion.57
  100.3 2.9 collective-permute-start
  103.2 12.0 %collective-permute-done.4 = bf16[2,128,1408]{1,2,0:T(8,128)(2,1)} collective-permute-done((bf16[2,128,1408]{1,2,0:T(8,128)(2,1)S(1)}, bf16[2,128,1408]{1,2,0:T(8,128)(2,1)}, u32[]{:S(2)}, u32[]{:S(2)}) %collective-permute-start.4) | collective-permute-done | bytes 720928 | tf_op jit(solution)/shard_map/ppermute | solution.py:460
  121.3 4.7 all-to-all-start.2
  126.4 2.7 collective-permute-start.5
  129.1 3.3 attend.1.heads_ref
  136.7 17.4 %collective-permute-done.5.rest_6_ = bf16[1,320,896]{2,1,0:T(8,128)(2,1)} collective-permute-done((bf16[1,320,896]{2,1,0:T(8,128)(2,1)}, bf16[1,320,896]{2,1,0:T(8,128)(2,1)}, u32[]{:S(2)}, u32[]{:S(2)}) %collective-permute-start.5) | collective-permute-done | bytes 573472 | tf_op jit(solution)/shard_map/ppermute | solution.py:517
  154.1 3.4 collective-permute-start.6
  157.5 13.1 %collective-permute-done.6 = bf16[1,128,1280]{2,1,0:T(8,128)(2,1)S(1)} collective-permute-done((bf16[1,128,1280]{2,1,0:T(8,128)(2,1)S(1)}, bf16[1,128,1280]{2,1,0:T(8,128)(2,1)S(1)}, u32[]{:S(2)}, u32[]{:S(2)}) %collective-permute-start.6) | collective-permute-done | bytes 327712 | tf_op jit(solution)/shard_map/ppermute | solution.py:460
  172.2 3.3 collective-permute-start.7
  179.9 27.5 %collective-permute-done.17 = bf16[3,40,224]{2,1,0:T(8,128)(2,1)S(1)} collective-permute-done((bf16[3,40,224]{2,1,0:T(8,128)(2,1)S(1)}, bf16[3,40,224]{2,1,0:T(8,128)(2,1)S(1)}, u32[]{:S(2)}, u32[]{:S(2)}) %collective-permute-start.17) | collective-permute-done | bytes 53792 | tf_op jit(solution)/shard_map/ppermute | solution.py:447
  210.5 2.5 fusion.5
  215.3 4.8 all-to-all-start.3
  220.1 2.8 fusion.26
  225.7 14.6 %collective-permute-done.10.rest_7_ = bf16[1,320,896]{2,1,0:T(8,128)(2,1)S(1)} collective-permute-done((bf16[1,320,896]{2,1,0:T(8,128)(2,1)}, bf16[1,320,896]{2,1,0:T(8,128)(2,1)S(1)}, u32[]{:S(2)}, u32[]{:S(2)}) %collective-permute-start.10) | collective-permute-done | bytes 573472 | tf_op jit(solution)/shard_map/ppermute | solution.py:517
  240.3 24.7 %collective-permute-start.11 = (bf16[1,320,896]{2,1,0:T(8,128)(2,1)}, bf16[1,320,896]{2,1,0:T(8,128)(2,1)}, u32[]{:S(2)}, u32[]{:S(2)}) collective-permute-start(bf16[1,320,896]{2,1,0:T(8,128)(2,1)} %get-tuple-element.110), channel_id=1, source_target_pairs={{0,8},{8,0},{16,24},{24,16},{1,9},{9,1},{17,25},{25,17},{2,10},{10... | collective-permute-start | bytes 1720328 | tf_op jit(solution)/shard_map/ppermute | solution.py:517
  271.3 2.5 copy.349
  288.8 15.8 %expert_front.1 = (f32[1536,896]{1,0:T(8,128)}, f32[1536,896]{1,0:T(8,128)}, bf16[1536,896]{1,0:T(8,128)(2,1)S(1)}, f32[1536,128]{1,0:T(8,128)S(1)}) custom-call(s32[2]{0:T(128)S(1)} %pad_add_fusion.place_ref, bf16[1536,1280]{1,0:T(8,128)(2,1)} %bitcast.38.x_ref, bf16[1536,1408]{1,0:T(8,128)(2,1)} %bitcast.31.hot_ref.x_ref.g_ref, ...), custom_call_target="tpu_custom_call" | custom-call | flops 7046430720 | bytes 16515072 | tf_op jit(solution)/shard_map/expert_front/pallas_call | solution.py:254
  305.5 7.1 %weight_grads.2 = bf16[1,1280,896]{2,1,0:T(8,128)(2,1)S(1)} custom-call(bf16[1536,1408]{1,0:T(8,128)(2,1)} %bitcast.31.hot_ref.x_ref.g_ref, bf16[1536,896]{1,0:T(8,128)(2,1)S(1)} %get-tuple-element.108.rest_0_.gated_ref), custom_call_target="tpu_custom_call" | custom-call | flops 3523215360 | bytes 6684672 | tf_op jit(solution)/shard_map/weight_grads/pallas_call | solution.py:354
  314.2 3.7 collective-permute-start.14
  318.0 30.5 %expert_back.1 = (bf16[1536,1280]{1,0:T(8,128)(2,1)}, bf16[1536,1280]{1,0:T(8,128)(2,1)}, bf16[1536,896]{1,0:T(8,128)(2,1)}, bf16[1536,896]{1,0:T(8,128)(2,1)}, f32[8,8,192]{2,1,0:T(8,128)}) custom-call(s32[2]{0:T(128)S(1)} %pad_add_fusion.place_ref, bf16[1536,1408]{1,0:T(8,128)(2,1)} %bitcast.31.hot_ref.x_ref.g_ref, f32[1536,896]{1,0:T(8,128)} %get-tuple-element.105.eg_ref, ...), custom_call_target="tpu_custom_call" | custom-call | flops 14092861440 | bytes 22020096 | tf_op jit(solution)/shard_map/expert_back/pallas_call | solution.py:319
  348.5 3.9 all-to-all-start.6
  352.4 2.7 fusion.109
  357.4 4.5 all-to-all-start.4
  367.0 10.7 %weight_grads.3 = bf16[2,1280,896]{2,1,0:T(8,128)(2,1)S(1)} custom-call(bf16[1536,1280]{1,0:T(8,128)(2,1)} %bitcast.38.x_ref, bf16[1536,896]{1,0:T(8,128)(2,1)S(1)} %copy-done.24, bf16[1536,896]{1,0:T(8,128)(2,1)S(1)} %copy-done.25), custom_call_target="tpu_custom_call" | custom-call | flops 7046430720 | bytes 6684672 | tf_op jit(solution)/shard_map/weight_grads/pallas_call | solution.py:354
  380.5 2.5 copy.345
  395.9 3.0 convolution_add_fusion
  398.9 9.3 %all-to-all-done.4 = bf16[8,4,48,1280]{3,2,1,0:T(8,128)(2,1)} async-done(((bf16[8,4,48,1280]{3,2,1,0:T(8,128)(2,1)}), bf16[8,4,48,1280]{3,2,1,0:T(8,128)(2,1)}, u32[]{:S(2)}, u32[]{:S(2)}) %all-to-all-start.4) | async-done | bytes 3932192 | tf_op jit(solution)/shard_map/all_to_all | solution.py:650
  408.2 4.0 fusion.15
  416.7 17.7 %collective-permute-done.19 = bf16[2,128,1280]{2,1,0:T(8,128)(2,1)S(1)} collective-permute-done((bf16[2,128,1280]{2,1,0:T(8,128)(2,1)S(1)}, bf16[2,128,1280]{2,1,0:T(8,128)(2,1)S(1)}, u32[]{:S(2)}, u32[]{:S(2)}) %collective-permute-start.19) | collective-permute-done | bytes 655392 | tf_op jit(solution)/shard_map/ppermute | solution.py:467
  435.3 3.8 collective-permute-start.20
  439.1 5.0 all-to-all-start.5
  447.6 29.4 %collective-permute-done.20 = bf16[1,128,1280]{2,1,0:T(8,128)(2,1)} collective-permute-done((bf16[1,128,1280]{2,1,0:T(8,128)(2,1)}, bf16[1,128,1280]{2,1,0:T(8,128)(2,1)}, u32[]{:S(2)}, u32[]{:S(2)}) %collective-permute-start.20) | collective-permute-done | bytes 327712 | tf_op jit(solution)/shard_map/ppermute | solution.py:467
  480.1 6.9 %attend_back.1 = (f32[128,1280]{1,0:T(8,128)S(1)}, bf16[128,1280]{1,0:T(8,128)(2,1)S(1)}, f32[1,1280]{1,0:T(1,128)S(1)}, bf16[8,128,512]{2,1,0:T(8,128)(2,1)}) custom-call(f32[128,1280]{1,0:T(8,128)S(1)} %add_bitcast_fusion.1.ig_ref, bf16[128,1280]{1,0:T(8,128)(2,1)S(1)} %copy-done.5, f32[128,1280]{1,0:T(8,128)S(1)} %get-tuple-element.95.middle_ref, ...), custom_call_target="tpu_custom_call" | custom-call | tf_op jit(solution)/shard_map/attend_back/pallas_call | solution.py:174
  490.6 6.5 concatenate.77
  499.8 5.2 all-to-all-start.7
  506.5 3.1 fusion.6
  511.3 9.2 %all-to-all-done.7 = bf16[8,128,512]{2,1,0:T(8,128)(2,1)} async-done(((bf16[8,128,512]{2,1,0:T(8,128)(2,1)}), bf16[8,128,512]{2,1,0:T(8,128)(2,1)}, u32[]{:S(2)}, u32[]{:S(2)}) %all-to-all-start.7) | async-done | bytes 1048608 | tf_op jit(solution)/shard_map/all_to_all | solution.py:685
  520.5 4.3 convolution_convert_fusion.3
  526.8 3.3 collective-permute-start.22
  536.8 3.4 update_part.8
  540.2 20.6 %collective-permute-done.29.g_ref = bf16[2,320,896]{2,1,0:T(8,128)(2,1)} collective-permute-done((bf16[2,320,896]{2,1,0:T(8,128)(2,1)}, bf16[2,320,896]{2,1,0:T(8,128)(2,1)}, u32[]{:S(2)}, u32[]{:S(2)}) %collective-permute-start.29) | collective-permute-done | bytes 1146912 | tf_op jit(solution)/shard_map/ppermute | solution.py:614
  565.9 2.6 multiply_add_fusion.2
  572.0 3.9 convolution_convert_fusion.4
  575.9 6.0 all-to-all-start.8
  582.5 26.8 %collective-permute-done.23 = bf16[1,128,1280]{2,1,0:T(8,128)(2,1)S(1)} collective-permute-done((bf16[1,128,1280]{2,1,0:T(8,128)(2,1)S(1)}, bf16[1,128,1280]{2,1,0:T(8,128)(2,1)S(1)}, u32[]{:S(2)}, u32[]{:S(2)}) %collective-permute-start.23) | collective-permute-done | bytes 327712 | tf_op jit(solution)/shard_map/ppermute | solution.py:467
  612.8 3.7 collective-permute-done.30.g_ref
  616.5 3.4 update_part.9
  619.9 3.4 update_part.10
  623.3 3.4 update_part.11
  626.7 6.5 update_part.12
  633.2 6.3 update_part.13
  639.4 6.3 update_part.14
  646.7 3.6 collective-permute-start.25
  650.3 6.3 update_part.15
  (369 shorter events, 139.9 us)
Async XLA Ops:
  7.2 53.3 %all-gather.6.cloned.1.call-start = ((), (), s32[]{:S(2)}) async-start(), calls=%async_computation.12 | async-start | bytes 2949120 | tf_op jit(solution)/shard_map/all_gather | solution.py:493
  11.6 11.3 %copy-start.71 = (f32[40]{0:T(128)}, f32[40]{0:T(128)S(1)}, u32[]{:S(2)}) copy-start(f32[40]{0:T(128)S(1)} %get-tuple-element.336) | copy-start | bytes 484
  12.9 11.4 %copy-start.39 = (bf16[4,40,1280]{2,1,0:T(8,128)(2,1)}, bf16[4,40,1280]{2,1,0:T(8,128)(2,1)S(1)}, u32[]{:S(2)}) copy-start(bf16[4,40,1280]{2,1,0:T(8,128)(2,1)S(1)} %convert.43) | copy-start | bytes 1228804
  13.0 5.9 collective-permute-start.1
  18.9 10.4 %collective-permute-start.2 = (bf16[2,40,1408]{2,1,0:T(8,128)(2,1)S(1)}, bf16[2,40,1408]{2,1,0:T(8,128)(2,1)S(1)}, u32[]{:S(2)}, u32[]{:S(2)}) collective-permute-start(bf16[2,40,1408]{2,1,0:T(8,128)(2,1)S(1)} %pad_maximum_fusion.7), channel_id=1, source_target_pairs={{0,8},{8,0},{16,24},{24,16},{1,9},{9,1},{17,25},{25,17},{2,10},{10... | collective-permute-start | bytes 675848 | tf_op jit(solution)/shard_map/ppermute | solution.py:460
  24.4 34.7 %all-to-all-start = ((bf16[32,40,512]{2,1,0:T(8,128)(2,1)}), bf16[32,40,512]{2,1,0:T(8,128)(2,1)S(1)}, u32[]{:S(2)}, u32[]{:S(2)}) async-start(bf16[32,40,512]{2,1,0:T(8,128)(2,1)} %bitcast.331), calls=%async_computation | async-start | bytes 2621440 | tf_op jit(solution)/shard_map/all_to_all | solution.py:487
  29.3 103.1 %all-gather.8.cloned.1.call-start = ((), (), s32[]{:S(2)}) async-start(), calls=%async_computation.16 | async-start | bytes 4055040 | tf_op jit(solution)/shard_map/all_gather | solution.py:498
  66.3 25.0 %all-to-all-start.1 = ((bf16[8,128,512]{2,1,0:T(8,128)(2,1)}), bf16[8,128,512]{2,1,0:T(8,128)(2,1)S(1)}, u32[]{:S(2)}, u32[]{:S(2)}) async-start(bf16[8,128,512]{2,1,0:T(8,128)(2,1)} %copy.368), calls=%async_computation.1 | async-start | bytes 2097152 | tf_op jit(solution)/shard_map/all_to_all | solution.py:544
  69.9 18.4 %collective-permute-start.3 = (bf16[1,128,1408]{1,2,0:T(8,128)(2,1)S(1)}, bf16[1,128,1408]{1,2,0:T(8,128)(2,1)S(1)}, u32[]{:S(2)}, u32[]{:S(2)}) collective-permute-start(bf16[1,128,1408]{1,2,0:T(8,128)(2,1)S(1)} %bitcast.348), channel_id=1, source_target_pairs={{0,16},{8,24},{16,0},{24,8},{1,17},{9,25},{17,1},{25,9},{2,18},{10... | collective-permute-start | bytes 1081352 | tf_op jit(solution)/shard_map/ppermute | solution.py:460
  91.3 23.9 %collective-permute-start.4 = (bf16[2,128,1408]{1,2,0:T(8,128)(2,1)S(1)}, bf16[2,128,1408]{1,2,0:T(8,128)(2,1)}, u32[]{:S(2)}, u32[]{:S(2)}) collective-permute-start(bf16[2,128,1408]{1,2,0:T(8,128)(2,1)S(1)} %pad_maximum_fusion.2), channel_id=1, source_target_pairs={{0,8},{8,0},{16,24},{24,16},{1,9},{9,1},{17,25},{25,17},{2,10},{10... | collective-permute-start | bytes 2162696 | tf_op jit(solution)/shard_map/ppermute | solution.py:460
  93.5 23.3 %copy-start.78 = (s32[8]{0:T(128)}, s32[8]{0:T(128)S(1)}, u32[]{:S(2)}) copy-start(s32[8]{0:T(128)S(1)} %multiply_add_fusion.8) | copy-start | bytes 100
  100.3 26.1 %collective-permute-start = (bf16[1,320,896]{2,1,0:T(8,128)(2,1)S(1)}, bf16[1,320,896]{2,1,0:T(8,128)(2,1)S(1)}, u32[]{:S(2)}, u32[]{:S(2)}) collective-permute-start(bf16[1,320,896]{2,1,0:T(8,128)(2,1)S(1)} %get-tuple-element.93), channel_id=1, source_target_pairs={{0,16},{8,24},{16,0},{24,8},{1,17},{9,25},{17,1},{25,9},{2,18},{10... | collective-permute-start | bytes 1720328 | tf_op jit(solution)/shard_map/ppermute | solution.py:517
  116.8 291.4 %copy-start.56 = (f32[8,4,128]{2,0,1:T(8,128)}, f32[8,4,128]{2,0,1:T(8,128)S(1)}, u32[]{:S(2)}) copy-start(f32[8,4,128]{2,0,1:T(8,128)S(1)} %fusion.99) | copy-start | bytes 49156
  121.3 89.2 %all-to-all-start.2 = ((bf16[8,4,48,1408]{3,2,1,0:T(8,128)(2,1)}), bf16[8,4,48,1408]{3,2,1,0:T(8,128)(2,1)}, u32[]{:S(2)}, u32[]{:S(2)}) async-start(bf16[8,4,48,1408]{3,2,1,0:T(8,128)(2,1)} %copy.329), calls=%async_computation.2 | async-start | bytes 8650752 | tf_op jit(solution)/shard_map/all_to_all | solution.py:580
  126.0 151.9 %all-gather.10.cloned.1.call-start = ((), (), s32[]{:S(2)}) async-start(), calls=%async_computation.17 | async-start | bytes 2211840 | tf_op jit(solution)/shard_map/all_gather | solution.py:560
  126.4 27.7 %collective-permute-start.5 = (bf16[1,320,896]{2,1,0:T(8,128)(2,1)}, bf16[1,320,896]{2,1,0:T(8,128)(2,1)}, u32[]{:S(2)}, u32[]{:S(2)}) collective-permute-start(bf16[1,320,896]{2,1,0:T(8,128)(2,1)} %get-tuple-element.99), channel_id=1, source_target_pairs={{0,16},{8,24},{16,0},{24,8},{1,17},{9,25},{17,1},{25,9},{2,18},{10... | collective-permute-start | bytes 1720328 | tf_op jit(solution)/shard_map/ppermute | solution.py:517
  135.7 40.5 %copy-start.46 = (f32[3,40,896]{2,1,0:T(8,128)S(1)}, f32[3,40,896]{2,1,0:T(8,128)}, u32[]{:S(2)}) copy-start(f32[3,40,896]{2,1,0:T(8,128)} %param.27) | copy-start | bytes 1290244
  136.7 73.8 %copy-start.14 = (f32[128,128]{1,0:T(8,128)}, f32[128,128]{1,0:T(8,128)S(1)}, u32[]{:S(2)}) copy-start(f32[128,128]{1,0:T(8,128)S(1)} %get-tuple-element.167) | copy-start | bytes 196612
  154.1 16.5 %collective-permute-start.6 = (bf16[1,128,1280]{2,1,0:T(8,128)(2,1)S(1)}, bf16[1,128,1280]{2,1,0:T(8,128)(2,1)S(1)}, u32[]{:S(2)}, u32[]{:S(2)}) collective-permute-start(bf16[1,128,1280]{2,1,0:T(8,128)(2,1)S(1)} %bitcast.307), channel_id=1, source_target_pairs={{0,16},{8,24},{16,0},{24,8},{1,17},{9,25},{17,1},{25,9},{2,18},{10... | collective-permute-start | bytes 983048 | tf_op jit(solution)/shard_map/ppermute | solution.py:460
  172.2 36.0 %collective-permute-start.7 = (bf16[2,128,1280]{2,1,0:T(8,128)(2,1)}, bf16[2,128,1280]{2,1,0:T(8,128)(2,1)}, u32[]{:S(2)}, u32[]{:S(2)}) collective-permute-start(bf16[2,128,1280]{2,1,0:T(8,128)(2,1)} %pad_maximum_fusion.3), channel_id=1, source_target_pairs={{0,8},{8,0},{16,24},{24,16},{1,9},{9,1},{17,25},{25,17},{2,10},{10... | collective-permute-start | bytes 1966088 | tf_op jit(solution)/shard_map/ppermute | solution.py:460
  175.5 35.0 %collective-permute-start.8 = (bf16[1,320,896]{2,1,0:T(8,128)(2,1)}, bf16[1,320,896]{2,1,0:T(8,128)(2,1)}, u32[]{:S(2)}, u32[]{:S(2)}) collective-permute-start(bf16[1,320,896]{2,1,0:T(8,128)(2,1)} %get-tuple-element.101), channel_id=1, source_target_pairs={{0,24},{8,16},{16,8},{24,0},{1,25},{9,17},{17,9},{25,1},{2,26},{10... | collective-permute-start | bytes 1720328 | tf_op jit(solution)/shard_map/ppermute | solution.py:517
  176.3 31.0 %collective-permute-start.17 = (bf16[3,40,224]{2,1,0:T(8,128)(2,1)S(1)}, bf16[3,40,224]{2,1,0:T(8,128)(2,1)S(1)}, u32[]{:S(2)}, u32[]{:S(2)}) collective-permute-start(bf16[3,40,224]{2,1,0:T(8,128)(2,1)S(1)} %get-tuple-element.332), channel_id=1, source_target_pairs={{0,24},{8,16},{16,8},{24,0},{1,25},{9,17},{17,9},{25,1},{2,26},{10... | collective-permute-start | bytes 161288 | tf_op jit(solution)/shard_map/ppermute | solution.py:447
  177.8 29.5 %collective-permute-start.16 = (bf16[3,40,224]{2,1,0:T(8,128)(2,1)S(1)}, bf16[3,40,224]{2,1,0:T(8,128)(2,1)S(1)}, u32[]{:S(2)}, u32[]{:S(2)}) collective-permute-start(bf16[3,40,224]{2,1,0:T(8,128)(2,1)S(1)} %get-tuple-element.333), channel_id=1, source_target_pairs={{0,16},{8,24},{16,0},{24,8},{1,17},{9,25},{17,1},{25,9},{2,18},{10... | collective-permute-start | bytes 161288 | tf_op jit(solution)/shard_map/ppermute | solution.py:447
  179.7 27.7 %collective-permute-start.15 = (bf16[3,40,224]{2,1,0:T(8,128)(2,1)S(1)}, bf16[3,40,224]{2,1,0:T(8,128)(2,1)S(1)}, u32[]{:S(2)}, u32[]{:S(2)}) collective-permute-start(bf16[3,40,224]{2,1,0:T(8,128)(2,1)S(1)} %get-tuple-element.334), channel_id=1, source_target_pairs={{0,8},{8,0},{16,24},{24,16},{1,9},{9,1},{17,25},{25,17},{2,10},{10... | collective-permute-start | bytes 161288 | tf_op jit(solution)/shard_map/ppermute | solution.py:447
  215.3 68.2 %all-to-all-start.3 = ((bf16[8,4,48,1280]{3,2,1,0:T(8,128)(2,1)}), bf16[8,4,48,1280]{3,2,1,0:T(8,128)(2,1)}, u32[]{:S(2)}, u32[]{:S(2)}) async-start(bf16[8,4,48,1280]{3,2,1,0:T(8,128)(2,1)} %copy.330), calls=%async_computation.3 | async-start | bytes 7864320 | tf_op jit(solution)/shard_map/all_to_all | solution.py:580
  222.9 52.7 %collective-permute-start.9 = (bf16[2,320,896]{2,1,0:T(8,128)(2,1)}, bf16[2,320,896]{2,1,0:T(8,128)(2,1)}, u32[]{:S(2)}, u32[]{:S(2)}) collective-permute-start(bf16[2,320,896]{2,1,0:T(8,128)(2,1)} %fusion.26), channel_id=1, source_target_pairs={{0,8},{8,0},{16,24},{24,16},{1,9},{9,1},{17,25},{25,17},{2,10},{10... | collective-permute-start | bytes 3440648 | tf_op jit(solution)/shard_map/ppermute | solution.py:517
  225.0 15.3 %collective-permute-start.10 = (bf16[1,320,896]{2,1,0:T(8,128)(2,1)}, bf16[1,320,896]{2,1,0:T(8,128)(2,1)S(1)}, u32[]{:S(2)}, u32[]{:S(2)}) collective-permute-start(bf16[1,320,896]{2,1,0:T(8,128)(2,1)} %get-tuple-element.104), channel_id=1, source_target_pairs={{0,24},{8,16},{16,8},{24,0},{1,25},{9,17},{17,9},{25,1},{2,26},{10... | collective-permute-start | bytes 1720328 | tf_op jit(solution)/shard_map/ppermute | solution.py:517
  240.3 31.0 %copy-start.20 = (bf16[1,320,896]{2,1,0:T(8,128)(2,1)}, bf16[1,320,896]{2,1,0:T(8,128)(2,1)S(1)}, u32[]{:S(2)}) copy-start(bf16[1,320,896]{2,1,0:T(8,128)(2,1)S(1)} %collective-permute-done.10.rest_7_) | copy-start | bytes 1720324
  240.3 77.6 %collective-permute-start.11 = (bf16[1,320,896]{2,1,0:T(8,128)(2,1)}, bf16[1,320,896]{2,1,0:T(8,128)(2,1)}, u32[]{:S(2)}, u32[]{:S(2)}) collective-permute-start(bf16[1,320,896]{2,1,0:T(8,128)(2,1)} %get-tuple-element.110), channel_id=1, source_target_pairs={{0,8},{8,0},{16,24},{24,16},{1,9},{9,1},{17,25},{25,17},{2,10},{10... | collective-permute-start | bytes 1720328 | tf_op jit(solution)/shard_map/ppermute | solution.py:517
  265.0 52.9 %collective-permute-start.12 = (bf16[1,320,896]{2,1,0:T(8,128)(2,1)}, bf16[1,320,896]{2,1,0:T(8,128)(2,1)}, u32[]{:S(2)}, u32[]{:S(2)}) collective-permute-start(bf16[1,320,896]{2,1,0:T(8,128)(2,1)} %get-tuple-element.111), channel_id=1, source_target_pairs={{0,16},{8,24},{16,0},{24,8},{1,17},{9,25},{17,1},{25,9},{2,18},{10... | collective-permute-start | bytes 1720328 | tf_op jit(solution)/shard_map/ppermute | solution.py:517
  265.8 52.1 %collective-permute-start.13 = (bf16[1,320,896]{2,1,0:T(8,128)(2,1)}, bf16[1,320,896]{2,1,0:T(8,128)(2,1)}, u32[]{:S(2)}, u32[]{:S(2)}) collective-permute-start(bf16[1,320,896]{2,1,0:T(8,128)(2,1)} %get-tuple-element.112), channel_id=1, source_target_pairs={{0,24},{8,16},{16,8},{24,0},{1,25},{9,17},{17,9},{25,1},{2,26},{10... | collective-permute-start | bytes 1720328 | tf_op jit(solution)/shard_map/ppermute | solution.py:517
  274.6 121.3 %copy-start.58 = (pred[4,4,8,128]{3,2,1,0:T(8,128)(4,1)}, pred[4,4,8,128]{3,2,1,0:T(8,128)(4,1)S(1)}, u32[]{:S(2)}) copy-start(pred[4,4,8,128]{3,2,1,0:T(8,128)(4,1)S(1)} %fusion.90) | copy-start | bytes 49156
  305.5 7.1 %copy-start.23 = (bf16[1536,896]{1,0:T(8,128)(2,1)}, bf16[1536,896]{1,0:T(8,128)(2,1)S(1)}, u32[]{:S(2)}) copy-start(bf16[1536,896]{1,0:T(8,128)(2,1)S(1)} %get-tuple-element.108.rest_0_.gated_ref) | copy-start | bytes 8257540
  314.2 49.3 %collective-permute-start.14 = (bf16[1,320,896]{2,1,0:T(8,128)(2,1)}, bf16[1,320,896]{2,1,0:T(8,128)(2,1)}, u32[]{:S(2)}, u32[]{:S(2)}) collective-permute-start(bf16[1,320,896]{2,1,0:T(8,128)(2,1)} %get-tuple-element.308), channel_id=1, source_target_pairs={{0,16},{8,24},{16,0},{24,8},{1,17},{9,25},{17,1},{25,9},{2,18},{10... | collective-permute-start | bytes 1720328 | tf_op jit(solution)/shard_map/ppermute | solution.py:614
  348.5 8.9 %all-to-all-start.6 = ((f32[8,8,192]{2,1,0:T(8,128)}), f32[8,8,192]{2,1,0:T(8,128)S(1)}, u32[]{:S(2)}, u32[]{:S(2)}) async-start(f32[8,8,192]{2,1,0:T(8,128)} %get-tuple-element.121), calls=%async_computation.6 | async-start | bytes 131072 | tf_op jit(solution)/shard_map/all_to_all | solution.py:625
  357.4 50.8 %all-to-all-start.4 = ((bf16[8,4,48,1280]{3,2,1,0:T(8,128)(2,1)}), bf16[8,4,48,1280]{3,2,1,0:T(8,128)(2,1)}, u32[]{:S(2)}, u32[]{:S(2)}) async-start(bf16[8,4,48,1280]{3,2,1,0:T(8,128)(2,1)} %bitcast.334), calls=%async_computation.4 | async-start | bytes 7864320 | tf_op jit(solution)/shard_map/all_to_all | solution.py:650
  361.9 168.3 %reduce-scatter.8.cloned.1.call-start = ((), (), s32[]{:S(2)}) async-start(), calls=%async_computation.15 | async-start | bytes 2211840 | tf_op jit(solution)/shard_map/reduce_scatter | solution.py:737
  379.9 32.3 %collective-permute-start.18 = (bf16[1,320,896]{2,1,0:T(8,128)(2,1)}, bf16[1,320,896]{2,1,0:T(8,128)(2,1)}, u32[]{:S(2)}, u32[]{:S(2)}) collective-permute-start(bf16[1,320,896]{2,1,0:T(8,128)(2,1)} %get-tuple-element.122), channel_id=1, source_target_pairs={{0,24},{8,16},{16,8},{24,0},{1,25},{9,17},{17,9},{25,1},{2,26},{10... | collective-permute-start | bytes 1720328 | tf_op jit(solution)/shard_map/ppermute | solution.py:614
  412.3 22.1 %collective-permute-start.19 = (bf16[2,128,1280]{2,1,0:T(8,128)(2,1)S(1)}, bf16[2,128,1280]{2,1,0:T(8,128)(2,1)S(1)}, u32[]{:S(2)}, u32[]{:S(2)}) collective-permute-start(bf16[2,128,1280]{2,1,0:T(8,128)(2,1)S(1)} %split.37), channel_id=1, source_target_pairs={{0,8},{8,0},{16,24},{24,16},{1,9},{9,1},{17,25},{25,17},{2,10},{10... | collective-permute-start | bytes 1966088 | tf_op jit(solution)/shard_map/ppermute | solution.py:467
  414.9 63.2 %collective-permute-start.21 = (bf16[2,320,896]{2,1,0:T(8,128)(2,1)}, bf16[2,320,896]{2,1,0:T(8,128)(2,1)}, u32[]{:S(2)}, u32[]{:S(2)}) collective-permute-start(bf16[2,320,896]{2,1,0:T(8,128)(2,1)} %get-tuple-element.124), channel_id=1, source_target_pairs={{0,16},{8,24},{16,0},{24,8},{1,17},{9,25},{17,1},{25,9},{2,18},{10... | collective-permute-start | bytes 3440648 | tf_op jit(solution)/shard_map/ppermute | solution.py:614
  435.3 41.7 %collective-permute-start.20 = (bf16[1,128,1280]{2,1,0:T(8,128)(2,1)}, bf16[1,128,1280]{2,1,0:T(8,128)(2,1)}, u32[]{:S(2)}, u32[]{:S(2)}) collective-permute-start(bf16[1,128,1280]{2,1,0:T(8,128)(2,1)} %split.49), channel_id=1, source_target_pairs={{0,16},{8,24},{16,0},{24,8},{1,17},{9,25},{17,1},{25,9},{2,18},{10... | collective-permute-start | bytes 983048 | tf_op jit(solution)/shard_map/ppermute | solution.py:467
  439.1 60.7 %all-to-all-start.5 = ((bf16[8,4,48,1280]{3,2,1,0:T(8,128)(2,1)}), bf16[8,4,48,1280]{3,2,1,0:T(8,128)(2,1)}, u32[]{:S(2)}, u32[]{:S(2)}) async-start(bf16[8,4,48,1280]{3,2,1,0:T(8,128)(2,1)} %bitcast.333), calls=%async_computation.5 | async-start | bytes 7864320 | tf_op jit(solution)/shard_map/all_to_all | solution.py:650
  444.1 165.2 %reduce-scatter.6.cloned.1.call-start = ((), (), s32[]{:S(2)}) async-start(), calls=%async_computation.14 | async-start | bytes 4055040 | tf_op jit(solution)/shard_map/reduce_scatter | solution.py:671
  497.1 9.4 %copy-start.57 = (f32[8,4,128]{2,0,1:T(8,128)S(1)}, f32[8,4,128]{2,0,1:T(8,128)}, u32[]{:S(2)}) copy-start(f32[8,4,128]{2,0,1:T(8,128)} %copy-done.56) | copy-start | bytes 49156
  499.8 20.7 %all-to-all-start.7 = ((bf16[8,128,512]{2,1,0:T(8,128)(2,1)}), bf16[8,128,512]{2,1,0:T(8,128)(2,1)}, u32[]{:S(2)}, u32[]{:S(2)}) async-start(bf16[8,128,512]{2,1,0:T(8,128)(2,1)} %get-tuple-element.127), calls=%async_computation.7 | async-start | bytes 2097152 | tf_op jit(solution)/shard_map/all_to_all | solution.py:685
  505.1 55.6 %collective-permute-start.29 = (bf16[2,320,896]{2,1,0:T(8,128)(2,1)}, bf16[2,320,896]{2,1,0:T(8,128)(2,1)}, u32[]{:S(2)}, u32[]{:S(2)}) collective-permute-start(bf16[2,320,896]{2,1,0:T(8,128)(2,1)} %get-tuple-element.134), channel_id=1, source_target_pairs={{0,24},{8,16},{16,8},{24,0},{1,25},{9,17},{17,9},{25,1},{2,26},{10... | collective-permute-start | bytes 3440648 | tf_op jit(solution)/shard_map/ppermute | solution.py:614
  509.7 10.9 %copy-start.33 = (bf16[32,40,512]{2,1,0:T(8,128)(2,1)S(1)}, bf16[32,40,512]{2,1,0:T(8,128)(2,1)}, u32[]{:S(2)}) copy-start(bf16[32,40,512]{2,1,0:T(8,128)(2,1)} %copy-done.32) | copy-start | bytes 3932164
  520.5 9.6 %copy-start.15 = (f32[128,128]{1,0:T(8,128)S(1)}, f32[128,128]{1,0:T(8,128)}, u32[]{:S(2)}) copy-start(f32[128,128]{1,0:T(8,128)} %copy-done.14) | copy-start | bytes 196612
  526.8 41.7 %collective-permute-start.22 = (bf16[2,128,1280]{2,1,0:T(8,128)(2,1)}, bf16[2,128,1280]{2,1,0:T(8,128)(2,1)}, u32[]{:S(2)}, u32[]{:S(2)}) collective-permute-start(bf16[2,128,1280]{2,1,0:T(8,128)(2,1)} %split.41), channel_id=1, source_target_pairs={{0,8},{8,0},{16,24},{24,16},{1,9},{9,1},{17,25},{25,17},{2,10},{10... | collective-permute-start | bytes 1966088 | tf_op jit(solution)/shard_map/ppermute | solution.py:467
  531.2 33.8 %collective-permute-start.28 = (bf16[3,40,224]{2,1,0:T(8,128)(2,1)S(1)}, bf16[3,40,224]{2,1,0:T(8,128)(2,1)S(1)}, u32[]{:S(2)}, u32[]{:S(2)}) collective-permute-start(bf16[3,40,224]{2,1,0:T(8,128)(2,1)S(1)} %get-tuple-element.327), channel_id=1, source_target_pairs={{0,24},{8,16},{16,8},{24,0},{1,25},{9,17},{17,9},{25,1},{2,26},{10... | collective-permute-start | bytes 161288 | tf_op jit(solution)/shard_map/ppermute | solution.py:447
  531.9 32.6 %collective-permute-start.27 = (bf16[3,40,224]{2,1,0:T(8,128)(2,1)S(1)}, bf16[3,40,224]{2,1,0:T(8,128)(2,1)S(1)}, u32[]{:S(2)}, u32[]{:S(2)}) collective-permute-start(bf16[3,40,224]{2,1,0:T(8,128)(2,1)S(1)} %get-tuple-element.328), channel_id=1, source_target_pairs={{0,16},{8,24},{16,0},{24,8},{1,17},{9,25},{17,1},{25,9},{2,18},{10... | collective-permute-start | bytes 161288 | tf_op jit(solution)/shard_map/ppermute | solution.py:447
  533.6 28.1 %collective-permute-start.26 = (bf16[3,40,224]{2,1,0:T(8,128)(2,1)S(1)}, bf16[3,40,224]{2,1,0:T(8,128)(2,1)S(1)}, u32[]{:S(2)}, u32[]{:S(2)}) collective-permute-start(bf16[3,40,224]{2,1,0:T(8,128)(2,1)S(1)} %get-tuple-element.329), channel_id=1, source_target_pairs={{0,8},{8,0},{16,24},{24,16},{1,9},{9,1},{17,25},{25,17},{2,10},{10... | collective-permute-start | bytes 161288 | tf_op jit(solution)/shard_map/ppermute | solution.py:447
  540.2 28.3 %copy-start.36 = (bf16[4,128,1280]{2,1,0:T(8,128)(2,1)S(1)}, bf16[4,128,1280]{2,1,0:T(8,128)(2,1)}, u32[]{:S(2)}) copy-start(bf16[4,128,1280]{2,1,0:T(8,128)(2,1)} %fusion.18) | copy-start | bytes 3932164
  560.7 52.0 %collective-permute-start.31 = (bf16[1,320,896]{2,1,0:T(8,128)(2,1)}, bf16[1,320,896]{2,1,0:T(8,128)(2,1)}, u32[]{:S(2)}, u32[]{:S(2)}) collective-permute-start(bf16[1,320,896]{2,1,0:T(8,128)(2,1)} %get-tuple-element.139), channel_id=1, source_target_pairs={{0,8},{8,0},{16,24},{24,16},{1,9},{9,1},{17,25},{25,17},{2,10},{10... | collective-permute-start | bytes 1720328 | tf_op jit(solution)/shard_map/ppermute | solution.py:614
  561.7 54.8 %collective-permute-start.30 = (bf16[2,320,896]{2,1,0:T(8,128)(2,1)}, bf16[2,320,896]{2,1,0:T(8,128)(2,1)}, u32[]{:S(2)}, u32[]{:S(2)}) collective-permute-start(bf16[2,320,896]{2,1,0:T(8,128)(2,1)} %get-tuple-element.135), channel_id=1, source_target_pairs={{0,8},{8,0},{16,24},{24,16},{1,9},{9,1},{17,25},{25,17},{2,10},{10... | collective-permute-start | bytes 3440648 | tf_op jit(solution)/shard_map/ppermute | solution.py:614
  570.6 38.7 %collective-permute-start.23 = (bf16[1,128,1280]{2,1,0:T(8,128)(2,1)S(1)}, bf16[1,128,1280]{2,1,0:T(8,128)(2,1)S(1)}, u32[]{:S(2)}, u32[]{:S(2)}) collective-permute-start(bf16[1,128,1280]{2,1,0:T(8,128)(2,1)S(1)} %split.51), channel_id=1, source_target_pairs={{0,16},{8,24},{16,0},{24,8},{1,17},{9,25},{17,1},{25,9},{2,18},{10... | collective-permute-start | bytes 983048 | tf_op jit(solution)/shard_map/ppermute | solution.py:467
  575.9 83.5 %all-to-all-start.8 = ((bf16[32,40,512]{2,1,0:T(8,128)(2,1)}), bf16[32,40,512]{2,1,0:T(8,128)(2,1)}, u32[]{:S(2)}, u32[]{:S(2)}) async-start(bf16[32,40,512]{2,1,0:T(8,128)(2,1)} %bitcast.70), calls=%async_computation.9 | async-start | bytes 2621440 | tf_op jit(solution)/shard_map/all_to_all | solution.py:690
  581.9 28.7 %copy-start.44 = (bf16[2,128,1280]{2,1,0:T(8,128)(2,1)S(1)}, bf16[2,128,1280]{2,1,0:T(8,128)(2,1)}, u32[]{:S(2)}) copy-start(bf16[2,128,1280]{2,1,0:T(8,128)(2,1)} %copy-done.43) | copy-start | bytes 1966084
  581.9 82.5 %reduce-scatter.4.cloned.1.call-start = ((), (), s32[]{:S(2)}) async-start(), calls=%async_computation.13 | async-start | bytes 2949120 | tf_op jit(solution)/shard_map/reduce_scatter | solution.py:697
  610.5 35.2 %collective-permute-start.24 = (bf16[2,40,1408]{2,1,0:T(8,128)(2,1)S(1)}, bf16[2,40,1408]{2,1,0:T(8,128)(2,1)}, u32[]{:S(2)}, u32[]{:S(2)}) collective-permute-start(bf16[2,40,1408]{2,1,0:T(8,128)(2,1)S(1)} %split.45), channel_id=1, source_target_pairs={{0,8},{8,0},{16,24},{24,16},{1,9},{9,1},{17,25},{25,17},{2,10},{10... | collective-permute-start | bytes 675848 | tf_op jit(solution)/shard_map/ppermute | solution.py:467
  646.7 10.4 %collective-permute-start.25 = (bf16[1,40,1408]{2,1,0:T(8,128)(2,1)S(1)}, bf16[1,40,1408]{2,1,0:T(8,128)(2,1)S(1)}, u32[]{:S(2)}, u32[]{:S(2)}) collective-permute-start(bf16[1,40,1408]{2,1,0:T(8,128)(2,1)S(1)} %split.53), channel_id=1, source_target_pairs={{0,16},{8,24},{16,0},{24,8},{1,17},{9,25},{17,1},{25,9},{2,18},{10... | collective-permute-start | bytes 337928 | tf_op jit(solution)/shard_map/ppermute | solution.py:467
  650.3 6.9 %copy-start.60 = (f32[40,32]{1,0:T(8,128)S(1)}, f32[40,32]{1,0:T(8,128)}, u32[]{:S(2)}) copy-start(f32[40,32]{1,0:T(8,128)} %copy.352) | copy-start | bytes 15364
  650.3 6.9 %copy-start.61 = (f32[40,32]{1,0:T(8,128)S(1)}, f32[40,32]{1,0:T(8,128)}, u32[]{:S(2)}) copy-start(f32[40,32]{1,0:T(8,128)} %copy.351) | copy-start | bytes 15364
  650.3 6.9 %copy-start.62 = (f32[40,32]{1,0:T(8,128)S(1)}, f32[40,32]{1,0:T(8,128)}, u32[]{:S(2)}) copy-start(f32[40,32]{1,0:T(8,128)} %copy.354) | copy-start | bytes 15364
  (65 other events, 170.8 us)
Sparse Core Ops, SparseCore 0:
  10.5 40.8 all-gather.5
  53.8 41.7 all-gather.7
  208.3 44.8 all-gather.9
  391.0 42.0 reduce-scatter.7
  497.2 52.3 reduce-scatter.5
  586.1 48.2 reduce-scatter.3

commit v3 on v2

--- a/solution.py
+++ b/solution.py
@@ -299,7 +299,10 @@
     silu = eg * sig
     plain = mm(g_ref[...], wd_ref[0])
     gate_grad = jnp.sum(silu * eu * plain, -1, keepdims=True)
-    gg_ref[0] = jnp.broadcast_to(gate_grad, (gate_grad.shape[0], 128)).T[:8]
+    count = gg_ref.shape[2]
+    for i in range(gg_ref.shape[0]):
+        part = gate_grad[i * count : (i + 1) * count]
+        gg_ref[i] = jnp.broadcast_to(part, (count, 128)).T[:8]
     grad = gate_ref[:, :1] * plain
     eg_grad = (grad * eu * sig * (1.0 + eg * (1.0 - sig))).astype(BF)
     eu_grad = (grad * silu).astype(BF)
@@ -309,10 +312,11 @@
     routed_ref[...] = mm_nt(gated_ref[...], wd_ref[0]).astype(BF)
 
 
-def expert_back(place, grads_hot, eg, eu, gated, gate, front, down, tile):
+def expert_back(place, grads_hot, eg, eu, gated, gate, front, down, group):
     count, hidden = eg.shape
     deep = front[0].shape[1]
     width = deep * len(down)
+    tile = 2 * group if count % (2 * group) == 0 else group
     wide = pl.BlockSpec((tile, width), lambda i, p: (i, 0))
     thin = pl.BlockSpec((tile, hidden), lambda i, p: (i, 0))
     lanes = pl.BlockSpec((tile, 128), lambda i, p: (i, 0))
@@ -323,7 +327,7 @@
             grid=(count // tile,),
             in_specs=[wide, thin, thin, thin, lanes]
             + [pl.BlockSpec(memory_space=pl.ANY)] * (3 * len(down)),
-            out_specs=[wide, wide, thin, thin, pl.BlockSpec((1, 8, tile), lambda i, p: (i, 0, 0))],
+            out_specs=[wide, wide, thin, thin, pl.BlockSpec((tile // group, 8, group), lambda i, p: (i, 0, 0))],
             scratch_shapes=[
                 pltpu.VMEM((2, width, hidden), BF),
                 pltpu.VMEM((1, width, hidden), BF),
@@ -335,7 +339,7 @@
             jax.ShapeDtypeStruct((count, width), BF),
             jax.ShapeDtypeStruct((count, hidden), BF),
             jax.ShapeDtypeStruct((count, hidden), BF),
-            jax.ShapeDtypeStruct((count // tile, 8, tile), F32),
+            jax.ShapeDtypeStruct((count // group, 8, group), F32),
         ],
         cost_estimate=pl.CostEstimate(
             flops=8 * count * width * hidden,
@@ -607,14 +611,18 @@
 
     def send_grads(g, last):
         got = [None] * Z
-        for k in [0] + list(range(2, Z)) + [1]:
+        for k in [0] + list(range(2, Z)):
             piece = lax.dynamic_slice(g, (0, (zi ^ k) * deep, 0), (g.shape[0], deep, FP))
             if k > 0:
                 piece = after(piece, last) if last is not None else piece
                 piece = lax.ppermute(piece, "dp", [(i, i ^ k) for i in range(Z)])
-                last = piece if k != 1 else last
+                last = piece
             got[k] = piece
         return got, last
+
+    def send_near(g, *needed):
+        piece = lax.dynamic_slice(g, (0, (zi ^ 1) * deep, 0), (g.shape[0], deep, FP))
+        return lax.ppermute(after(piece, *needed), "dp", [(i, i ^ 1) for i in range(Z)])
 
     down_got, last_down = send_grads(down_grad, None)
     rows_grad, routed_rows, eg_grad, eu_grad, gate_grad = expert_back(
@@ -699,7 +707,7 @@
         scaled_first - unit_first * jnp.mean(scaled_first * unit_first, -1, keepdims=True)
     )
 
-    branch = reduce_z(after(branch, back_local))
+    branch = reduce_z(after(branch, back_local, proj_w_local))
     layer_out = (middle + branch).astype(BF)
     first_mask = jnp.concatenate([jnp.ones((1,), bool), documents[1:] != documents[:-1]])
     kept_mask = 1.0 - first_mask.astype(F32)
@@ -718,13 +726,13 @@
     owned = (expert_weight, expert_momentum, expert_average)
     expert_new = ()
     expert_sum = jnp.zeros((local, 3, deep, FF), BF)
-    for m, gots in ((2, down_got), (0, front_got)):
-        for k in [0] + list(range(2, Z)) + [1]:
+    down_got[1] = send_near(down_grad, proj_w_local)
+    front_got[1] = send_near(front_grad, proj_w_local)
+    for k in [0] + list(range(2, Z)) + [1]:
+        for m, gots in ((2, down_got), (0, front_got)):
             there = zi ^ k
-            got = gots[k]
+            got = after(gots[k], proj_w_local, *((branch,) if m == 0 and k == 1 else ()))
             if parts == 1:
-                if k > 0:
-                    got = after(got, proj_w_local, branch)
                 expert_new = update_part(owned, expert_new, got, m, there)
             else:
                 expert_sum = lax.dynamic_update_slice(
@@ -735,7 +743,7 @@
 
     sgr = shared_grads.reshape(3, Z, E, R, FS).transpose(2, 1, 0, 3, 4).reshape(E * Z * 3 * R, FS)
     sgr = lax.psum_scatter(sgr, "expert", scatter_dimension=0, tiled=True)
-    sgr = after(sgr.reshape(Z, 3, R, FS), inner_grad)
+    sgr = after(sgr.reshape(Z, 3, R, FS), proj_w_local)
     got = swap_z(
         [lax.dynamic_index_in_dim(sgr, zi ^ k, 0, keepdims=False) for k in range(Z)]
     )

time: 687 us -> 674 us (0.981)
  waiting for transfers between devices: 255 us -> 248 us
    ppermute x6 -> x4, waiting for transfers between devices: 24.3 us -> 18.7 us  [send_grads(): piece = lax.ppermute(piece, 'dp', [(i, i ^ k) for i in range(Z)])]
    unnamed x174 -> x190, local copies, waits for them, and re-layouts: 26.7 us -> 26.7 us
where the time goes in v3:
time: 674 us; the launch traced here: 661 us
  waiting for transfers between devices  248 us (37%)
  starting transfers between devices  122 us (18%)
  Pallas kernels  111 us (16%)
  local copies, waits for them, and re-layouts  90.6 us (13%)
  matrix products  40.1 us (6%)
  other arithmetic  31.7 us (5%)
  between operations  17.9 us (3%)
    ppermute x6, waiting for transfers between devices, reduce_z(): got = lax.ppermute(send, 'dp', [(i, i ^ stride) for i in range(Z)])  71.9 us
    ppermute x6, waiting for transfers between devices, gather_z(): got = lax.ppermute(held, 'dp', [(i, i ^ stride) for i in range(Z)])  46.4 us
    pallas_call x8, Pallas kernels, update_part(): pl.pallas_call(update_kernel, grid_spec=pltpu.PrefetchScalarGridSpec(num_...  39.4 us
    ppermute x8, starting transfers between devices, fetch(): lax.ppermute(after(piece_of(k, low, high), *needed), 'dp', [(i, i ^ k) fo...  35 us
    ppermute x8, waiting for transfers between devices, fetch(): lax.ppermute(after(piece_of(k, low, high), *needed), 'dp', [(i, i ^ k) fo...  32 us
    ppermute x6, waiting for transfers between devices, swap_z(): out.append(lax.ppermute(pieces[k], 'dp', [(i, i ^ k) for i in range(Z)]))  27.5 us
    pallas_call x1, Pallas kernels, expert_back(): pl.pallas_call(functools.partial(back_kernel, len(down)), grid_spec=pltpu...  27.4 us
    all_to_all x1, waiting for transfers between devices, body(): lax.all_to_all(folded, ALL, split_axis=0, concat_axis=0, tiled=True)  27.2 us
  transfers between devices with their start and end apart: 47, of which 17 were waited for; matrix products, arithmetic and copies ran while one was open for 20% of the time, Pallas kernels for 17%

profile of v3, /device:TPU:16, one launch (start us, length us, event | category | flops | bytes accessed | tf_op | source)
XLA Modules:
  0.0 661.4 jit_solution(911698724407712149)
XLA Ops:
  13.1 5.8 collective-permute-done.1
  18.9 3.8 collective-permute-start.2
  24.4 4.9 all-to-all-start
  31.8 27.2 %all-to-all-done = bf16[32,40,512]{2,1,0:T(8,128)(2,1)S(1)} async-done(((bf16[32,40,512]{2,1,0:T(8,128)(2,1)}), bf16[32,40,512]{2,1,0:T(8,128)(2,1)S(1)}, u32[]{:S(2)}, u32[]{:S(2)}) %all-to-all-start) | async-done | bytes 1310752 | tf_op jit(solution)/shard_map/all_to_all | solution.py:491
  60.5 3.7 fusion.112
  66.3 3.6 all-to-all-start.1
  70.0 2.9 collective-permute-start.3
  72.9 15.5 %collective-permute-done.3 = bf16[1,128,1408]{1,2,0:T(8,128)(2,1)S(1)} collective-permute-done((bf16[1,128,1408]{1,2,0:T(8,128)(2,1)S(1)}, bf16[1,128,1408]{1,2,0:T(8,128)(2,1)S(1)}, u32[]{:S(2)}, u32[]{:S(2)}) %collective-permute-start.3) | collective-permute-done | bytes 360480 | tf_op jit(solution)/shard_map/ppermute | solution.py:464
  88.5 2.9 all-to-all-done.1.heads_ref
  93.5 6.7 %fusion.57 = (bf16[1,320,896]{2,1,0:T(8,128)(2,1)}, bf16[1,320,896]{2,1,0:T(8,128)(2,1)}, bf16[1,320,896]{2,1,0:T(8,128)(2,1)}, bf16[1,320,896]{2,1,0:T(8,128)(2...) fusion(f32[4,3,320,896]{3,2,1,0:T(8,128)} %w_ref.15, ...), kind=kLoop, calls=%fused_computation.103 | loop fusion | bytes 11468816 | tf_op jit(solution)/shard_map/convert_element_type | solution.py:518
  100.3 2.9 collective-permute-start
  103.2 12.0 %collective-permute-done.4 = bf16[2,128,1408]{1,2,0:T(8,128)(2,1)} collective-permute-done((bf16[2,128,1408]{1,2,0:T(8,128)(2,1)S(1)}, bf16[2,128,1408]{1,2,0:T(8,128)(2,1)}, u32[]{:S(2)}, u32[]{:S(2)}) %collective-permute-start.4) | collective-permute-done | bytes 720928 | tf_op jit(solution)/shard_map/ppermute | solution.py:464
  118.8 2.5 copy.329
  121.3 4.7 all-to-all-start.2
  126.5 2.7 collective-permute-start.5
  129.2 3.3 attend.1.heads_ref
  136.8 17.4 %collective-permute-done.5.rest_6_ = bf16[1,320,896]{2,1,0:T(8,128)(2,1)} collective-permute-done((bf16[1,320,896]{2,1,0:T(8,128)(2,1)}, bf16[1,320,896]{2,1,0:T(8,128)(2,1)}, u32[]{:S(2)}, u32[]{:S(2)}) %collective-permute-start.5) | collective-permute-done | bytes 573472 | tf_op jit(solution)/shard_map/ppermute | solution.py:521
  154.2 3.4 collective-permute-start.6
  157.6 13.1 %collective-permute-done.6 = bf16[1,128,1280]{2,1,0:T(8,128)(2,1)S(1)} collective-permute-done((bf16[1,128,1280]{2,1,0:T(8,128)(2,1)S(1)}, bf16[1,128,1280]{2,1,0:T(8,128)(2,1)S(1)}, u32[]{:S(2)}, u32[]{:S(2)}) %collective-permute-start.6) | collective-permute-done | bytes 327712 | tf_op jit(solution)/shard_map/ppermute | solution.py:464
  172.3 3.3 collective-permute-start.7
  180.0 27.5 %collective-permute-done.17 = bf16[3,40,224]{2,1,0:T(8,128)(2,1)S(1)} collective-permute-done((bf16[3,40,224]{2,1,0:T(8,128)(2,1)S(1)}, bf16[3,40,224]{2,1,0:T(8,128)(2,1)S(1)}, u32[]{:S(2)}, u32[]{:S(2)}) %collective-permute-start.17) | collective-permute-done | bytes 53792 | tf_op jit(solution)/shard_map/ppermute | solution.py:451
  210.6 2.5 fusion.5
  215.4 5.1 all-to-all-start.3
  220.4 2.8 fusion.26
  226.0 14.6 %collective-permute-done.10.rest_7_ = bf16[1,320,896]{2,1,0:T(8,128)(2,1)S(1)} collective-permute-done((bf16[1,320,896]{2,1,0:T(8,128)(2,1)}, bf16[1,320,896]{2,1,0:T(8,128)(2,1)S(1)}, u32[]{:S(2)}, u32[]{:S(2)}) %collective-permute-start.10) | collective-permute-done | bytes 573472 | tf_op jit(solution)/shard_map/ppermute | solution.py:521
  240.6 24.7 %collective-permute-start.11 = (bf16[1,320,896]{2,1,0:T(8,128)(2,1)}, bf16[1,320,896]{2,1,0:T(8,128)(2,1)}, u32[]{:S(2)}, u32[]{:S(2)}) collective-permute-start(bf16[1,320,896]{2,1,0:T(8,128)(2,1)} %get-tuple-element.112), channel_id=1, source_target_pairs={{0,8},{8,0},{16,24},{24,16},{1,9},{9,1},{17,25},{25,17},{2,10},{10... | collective-permute-start | bytes 1720328 | tf_op jit(solution)/shard_map/ppermute | solution.py:521
  266.8 2.5 slice.162
  271.7 2.5 copy.349
  289.2 15.8 %expert_front.1 = (f32[1536,896]{1,0:T(8,128)}, f32[1536,896]{1,0:T(8,128)}, bf16[1536,896]{1,0:T(8,128)(2,1)S(1)}, f32[1536,128]{1,0:T(8,128)S(1)}) custom-call(s32[2]{0:T(128)S(1)} %pad_add_fusion.place_ref, bf16[1536,1280]{1,0:T(8,128)(2,1)} %bitcast.38.x_ref, bf16[1536,1408]{1,0:T(8,128)(2,1)} %bitcast.31.hot_ref.x_ref.g_ref, ...), custom_call_target="tpu_custom_call" | custom-call | flops 7046430720 | bytes 16515072 | tf_op jit(solution)/shard_map/expert_front/pallas_call | solution.py:254
  305.9 7.1 %weight_grads.2 = bf16[1,1280,896]{2,1,0:T(8,128)(2,1)S(1)} custom-call(bf16[1536,1408]{1,0:T(8,128)(2,1)} %bitcast.31.hot_ref.x_ref.g_ref, bf16[1536,896]{1,0:T(8,128)(2,1)S(1)} %get-tuple-element.110.rest_0_.gated_ref), custom_call_target="tpu_custom_call" | custom-call | flops 3523215360 | bytes 6684672 | tf_op jit(solution)/shard_map/weight_grads/pallas_call | solution.py:358
  314.5 3.7 collective-permute-start.14
  318.3 27.4 %expert_back.1 = (bf16[1536,1280]{1,0:T(8,128)(2,1)}, bf16[1536,1280]{1,0:T(8,128)(2,1)}, bf16[1536,896]{1,0:T(8,128)(2,1)}, bf16[1536,896]{1,0:T(8,128)(2,1)}, f32[8,8,192]{2,1,0:T(8,128)}) custom-call(s32[2]{0:T(128)S(1)} %pad_add_fusion.place_ref, bf16[1536,1408]{1,0:T(8,128)(2,1)} %bitcast.31.hot_ref.x_ref.g_ref, f32[1536,896]{1,0:T(8,128)} %get-tuple-element.107.eg_ref, ...), custom_call_target="tpu_custom_call" | custom-call | flops 14092861440 | bytes 22020096 | tf_op jit(solution)/shard_map/expert_back/pallas_call | solution.py:323
  345.7 3.9 all-to-all-start.6
  349.6 2.7 fusion.109
  354.6 4.5 all-to-all-start.4
  364.0 10.7 %weight_grads.3 = bf16[2,1280,896]{2,1,0:T(8,128)(2,1)S(1)} custom-call(bf16[1536,1280]{1,0:T(8,128)(2,1)} %bitcast.38.x_ref, bf16[1536,896]{1,0:T(8,128)(2,1)S(1)} %copy-done.24, bf16[1536,896]{1,0:T(8,128)(2,1)S(1)} %copy-done.25), custom_call_target="tpu_custom_call" | custom-call | flops 7046430720 | bytes 6684672 | tf_op jit(solution)/shard_map/weight_grads/pallas_call | solution.py:358
  377.5 2.5 copy.345
  392.8 3.0 convolution_add_fusion
  395.8 9.6 %all-to-all-done.4 = bf16[8,4,48,1280]{3,2,1,0:T(8,128)(2,1)} async-done(((bf16[8,4,48,1280]{3,2,1,0:T(8,128)(2,1)}), bf16[8,4,48,1280]{3,2,1,0:T(8,128)(2,1)}, u32[]{:S(2)}, u32[]{:S(2)}) %all-to-all-start.4) | async-done | bytes 3932192 | tf_op jit(solution)/shard_map/all_to_all | solution.py:658
  405.4 4.0 fusion.15
  414.0 17.5 %collective-permute-done.19 = bf16[2,128,1280]{2,1,0:T(8,128)(2,1)S(1)} collective-permute-done((bf16[2,128,1280]{2,1,0:T(8,128)(2,1)S(1)}, bf16[2,128,1280]{2,1,0:T(8,128)(2,1)S(1)}, u32[]{:S(2)}, u32[]{:S(2)}) %collective-permute-start.19) | collective-permute-done | bytes 655392 | tf_op jit(solution)/shard_map/ppermute | solution.py:471
  432.5 3.8 collective-permute-start.20
  438.2 5.0 all-to-all-start.5
  443.4 30.9 %collective-permute-done.20 = bf16[1,128,1280]{2,1,0:T(8,128)(2,1)} collective-permute-done((bf16[1,128,1280]{2,1,0:T(8,128)(2,1)}, bf16[1,128,1280]{2,1,0:T(8,128)(2,1)}, u32[]{:S(2)}, u32[]{:S(2)}) %collective-permute-start.20) | collective-permute-done | bytes 327712 | tf_op jit(solution)/shard_map/ppermute | solution.py:471
  477.4 6.9 %attend_back.1 = (f32[128,1280]{1,0:T(8,128)S(1)}, bf16[128,1280]{1,0:T(8,128)(2,1)S(1)}, f32[1,1280]{1,0:T(1,128)S(1)}, bf16[8,128,512]{2,1,0:T(8,128)(2,1)}) custom-call(f32[128,1280]{1,0:T(8,128)S(1)} %add_bitcast_fusion.1.ig_ref, bf16[128,1280]{1,0:T(8,128)(2,1)S(1)} %copy-done.5, f32[128,1280]{1,0:T(8,128)S(1)} %get-tuple-element.97.middle_ref, ...), custom_call_target="tpu_custom_call" | custom-call | tf_op jit(solution)/shard_map/attend_back/pallas_call | solution.py:174
  487.9 6.5 concatenate.77
  497.1 5.0 all-to-all-start.7
  503.5 3.2 fusion.6
  508.5 9.1 %all-to-all-done.7 = bf16[8,128,512]{2,1,0:T(8,128)(2,1)} async-done(((bf16[8,128,512]{2,1,0:T(8,128)(2,1)}), bf16[8,128,512]{2,1,0:T(8,128)(2,1)}, u32[]{:S(2)}, u32[]{:S(2)}) %all-to-all-start.7) | async-done | bytes 1048608 | tf_op jit(solution)/shard_map/all_to_all | solution.py:693
  517.6 4.3 convolution_convert_fusion.3
  521.9 4.8 convolution_convert_fusion.4
  527.5 3.3 collective-permute-start.22
  532.8 3.6 collective-permute-start.27
  536.4 18.7 %collective-permute-done.31.g_ref = bf16[2,320,896]{2,1,0:T(8,128)(2,1)} collective-permute-done((bf16[2,320,896]{2,1,0:T(8,128)(2,1)}, bf16[2,320,896]{2,1,0:T(8,128)(2,1)}, u32[]{:S(2)}, u32[]{:S(2)}) %collective-permute-start.31) | collective-permute-done | bytes 1146912 | tf_op jit(solution)/shard_map/ppermute | solution.py:618
  557.7 7.0 %all-to-all-start.8 = ((bf16[32,40,512]{2,1,0:T(8,128)(2,1)}), bf16[32,40,512]{2,1,0:T(8,128)(2,1)}, u32[]{:S(2)}, u32[]{:S(2)}) async-start(bf16[32,40,512]{2,1,0:T(8,128)(2,1)} %bitcast.69), calls=%async_computation.9 | async-start | bytes 2621440 | tf_op jit(solution)/shard_map/all_to_all | solution.py:698
  566.2 3.4 update_part.8
  569.6 6.3 update_part.9
  575.9 3.7 update_part.10
  579.5 6.5 update_part.11
  586.0 3.4 update_part.12
  589.4 6.4 update_part.13
  602.5 3.5 update_part.14
  609.8 21.5 %collective-permute-done.23 = bf16[1,128,1280]{2,1,0:T(8,128)(2,1)S(1)} collective-permute-done((bf16[1,128,1280]{2,1,0:T(8,128)(2,1)S(1)}, bf16[1,128,1280]{2,1,0:T(8,128)(2,1)S(1)}, u32[]{:S(2)}, u32[]{:S(2)}) %collective-permute-start.23) | collective-permute-done | bytes 327712 | tf_op jit(solution)/shard_map/ppermute | solution.py:471
  637.4 6.3 update_part.15
  (385 shorter events, 133.9 us)
Async XLA Ops:
  7.2 53.3 %all-gather.6.cloned.1.call-start = ((), (), s32[]{:S(2)}) async-start(), calls=%async_computation.12 | async-start | bytes 2949120 | tf_op jit(solution)/shard_map/all_gather | solution.py:497
  11.6 11.3 %copy-start.79 = (f32[40]{0:T(128)}, f32[40]{0:T(128)S(1)}, u32[]{:S(2)}) copy-start(f32[40]{0:T(128)S(1)} %get-tuple-element.340) | copy-start | bytes 484
  12.9 11.4 %copy-start.41 = (bf16[4,40,1280]{2,1,0:T(8,128)(2,1)}, bf16[4,40,1280]{2,1,0:T(8,128)(2,1)S(1)}, u32[]{:S(2)}) copy-start(bf16[4,40,1280]{2,1,0:T(8,128)(2,1)S(1)} %convert.43) | copy-start | bytes 1228804
  13.0 5.9 collective-permute-start.1
  18.9 10.4 %collective-permute-start.2 = (bf16[2,40,1408]{2,1,0:T(8,128)(2,1)S(1)}, bf16[2,40,1408]{2,1,0:T(8,128)(2,1)S(1)}, u32[]{:S(2)}, u32[]{:S(2)}) collective-permute-start(bf16[2,40,1408]{2,1,0:T(8,128)(2,1)S(1)} %pad_maximum_fusion.7), channel_id=1, source_target_pairs={{0,8},{8,0},{16,24},{24,16},{1,9},{9,1},{17,25},{25,17},{2,10},{10... | collective-permute-start | bytes 675848 | tf_op jit(solution)/shard_map/ppermute | solution.py:464
  24.4 34.7 %all-to-all-start = ((bf16[32,40,512]{2,1,0:T(8,128)(2,1)}), bf16[32,40,512]{2,1,0:T(8,128)(2,1)S(1)}, u32[]{:S(2)}, u32[]{:S(2)}) async-start(bf16[32,40,512]{2,1,0:T(8,128)(2,1)} %bitcast.331), calls=%async_computation | async-start | bytes 2621440 | tf_op jit(solution)/shard_map/all_to_all | solution.py:491
  29.3 103.2 %all-gather.8.cloned.1.call-start = ((), (), s32[]{:S(2)}) async-start(), calls=%async_computation.16 | async-start | bytes 4055040 | tf_op jit(solution)/shard_map/all_gather | solution.py:502
  66.3 25.0 %all-to-all-start.1 = ((bf16[8,128,512]{2,1,0:T(8,128)(2,1)}), bf16[8,128,512]{2,1,0:T(8,128)(2,1)S(1)}, u32[]{:S(2)}, u32[]{:S(2)}) async-start(bf16[8,128,512]{2,1,0:T(8,128)(2,1)} %copy.368), calls=%async_computation.1 | async-start | bytes 2097152 | tf_op jit(solution)/shard_map/all_to_all | solution.py:548
  70.0 18.4 %collective-permute-start.3 = (bf16[1,128,1408]{1,2,0:T(8,128)(2,1)S(1)}, bf16[1,128,1408]{1,2,0:T(8,128)(2,1)S(1)}, u32[]{:S(2)}, u32[]{:S(2)}) collective-permute-start(bf16[1,128,1408]{1,2,0:T(8,128)(2,1)S(1)} %bitcast.348), channel_id=1, source_target_pairs={{0,16},{8,24},{16,0},{24,8},{1,17},{9,25},{17,1},{25,9},{2,18},{10... | collective-permute-start | bytes 1081352 | tf_op jit(solution)/shard_map/ppermute | solution.py:464
  91.3 23.9 %collective-permute-start.4 = (bf16[2,128,1408]{1,2,0:T(8,128)(2,1)S(1)}, bf16[2,128,1408]{1,2,0:T(8,128)(2,1)}, u32[]{:S(2)}, u32[]{:S(2)}) collective-permute-start(bf16[2,128,1408]{1,2,0:T(8,128)(2,1)S(1)} %pad_maximum_fusion.2), channel_id=1, source_target_pairs={{0,8},{8,0},{16,24},{24,16},{1,9},{9,1},{17,25},{25,17},{2,10},{10... | collective-permute-start | bytes 2162696 | tf_op jit(solution)/shard_map/ppermute | solution.py:464
  93.5 23.2 %copy-start.87 = (s32[8]{0:T(128)}, s32[8]{0:T(128)S(1)}, u32[]{:S(2)}) copy-start(s32[8]{0:T(128)S(1)} %multiply_add_fusion.8) | copy-start | bytes 100
  100.3 26.2 %collective-permute-start = (bf16[1,320,896]{2,1,0:T(8,128)(2,1)S(1)}, bf16[1,320,896]{2,1,0:T(8,128)(2,1)S(1)}, u32[]{:S(2)}, u32[]{:S(2)}) collective-permute-start(bf16[1,320,896]{2,1,0:T(8,128)(2,1)S(1)} %get-tuple-element.95), channel_id=1, source_target_pairs={{0,16},{8,24},{16,0},{24,8},{1,17},{9,25},{17,1},{25,9},{2,18},{10... | collective-permute-start | bytes 1720328 | tf_op jit(solution)/shard_map/ppermute | solution.py:521
  116.8 288.6 %copy-start.57 = (f32[8,4,128]{2,0,1:T(8,128)}, f32[8,4,128]{2,0,1:T(8,128)S(1)}, u32[]{:S(2)}) copy-start(f32[8,4,128]{2,0,1:T(8,128)S(1)} %fusion.99) | copy-start | bytes 49156
  121.3 89.3 %all-to-all-start.2 = ((bf16[8,4,48,1408]{3,2,1,0:T(8,128)(2,1)}), bf16[8,4,48,1408]{3,2,1,0:T(8,128)(2,1)}, u32[]{:S(2)}, u32[]{:S(2)}) async-start(bf16[8,4,48,1408]{3,2,1,0:T(8,128)(2,1)} %copy.329), calls=%async_computation.2 | async-start | bytes 8650752 | tf_op jit(solution)/shard_map/all_to_all | solution.py:584
  126.0 152.3 %all-gather.10.cloned.1.call-start = ((), (), s32[]{:S(2)}) async-start(), calls=%async_computation.17 | async-start | bytes 2211840 | tf_op jit(solution)/shard_map/all_gather | solution.py:564
  126.5 27.7 %collective-permute-start.5 = (bf16[1,320,896]{2,1,0:T(8,128)(2,1)}, bf16[1,320,896]{2,1,0:T(8,128)(2,1)}, u32[]{:S(2)}, u32[]{:S(2)}) collective-permute-start(bf16[1,320,896]{2,1,0:T(8,128)(2,1)} %get-tuple-element.101), channel_id=1, source_target_pairs={{0,16},{8,24},{16,0},{24,8},{1,17},{9,25},{17,1},{25,9},{2,18},{10... | collective-permute-start | bytes 1720328 | tf_op jit(solution)/shard_map/ppermute | solution.py:521
  135.8 40.4 %copy-start.46 = (f32[3,40,896]{2,1,0:T(8,128)S(1)}, f32[3,40,896]{2,1,0:T(8,128)}, u32[]{:S(2)}) copy-start(f32[3,40,896]{2,1,0:T(8,128)} %param.27) | copy-start | bytes 1290244
  136.8 73.8 %copy-start.14 = (f32[128,128]{1,0:T(8,128)}, f32[128,128]{1,0:T(8,128)S(1)}, u32[]{:S(2)}) copy-start(f32[128,128]{1,0:T(8,128)S(1)} %get-tuple-element.171) | copy-start | bytes 196612
  154.2 16.5 %collective-permute-start.6 = (bf16[1,128,1280]{2,1,0:T(8,128)(2,1)S(1)}, bf16[1,128,1280]{2,1,0:T(8,128)(2,1)S(1)}, u32[]{:S(2)}, u32[]{:S(2)}) collective-permute-start(bf16[1,128,1280]{2,1,0:T(8,128)(2,1)S(1)} %bitcast.307), channel_id=1, source_target_pairs={{0,16},{8,24},{16,0},{24,8},{1,17},{9,25},{17,1},{25,9},{2,18},{10... | collective-permute-start | bytes 983048 | tf_op jit(solution)/shard_map/ppermute | solution.py:464
  172.3 36.0 %collective-permute-start.7 = (bf16[2,128,1280]{2,1,0:T(8,128)(2,1)}, bf16[2,128,1280]{2,1,0:T(8,128)(2,1)}, u32[]{:S(2)}, u32[]{:S(2)}) collective-permute-start(bf16[2,128,1280]{2,1,0:T(8,128)(2,1)} %pad_maximum_fusion.3), channel_id=1, source_target_pairs={{0,8},{8,0},{16,24},{24,16},{1,9},{9,1},{17,25},{25,17},{2,10},{10... | collective-permute-start | bytes 1966088 | tf_op jit(solution)/shard_map/ppermute | solution.py:464
  175.6 35.0 %collective-permute-start.8 = (bf16[1,320,896]{2,1,0:T(8,128)(2,1)}, bf16[1,320,896]{2,1,0:T(8,128)(2,1)}, u32[]{:S(2)}, u32[]{:S(2)}) collective-permute-start(bf16[1,320,896]{2,1,0:T(8,128)(2,1)} %get-tuple-element.103), channel_id=1, source_target_pairs={{0,24},{8,16},{16,8},{24,0},{1,25},{9,17},{17,9},{25,1},{2,26},{10... | collective-permute-start | bytes 1720328 | tf_op jit(solution)/shard_map/ppermute | solution.py:521
  176.4 31.0 %collective-permute-start.17 = (bf16[3,40,224]{2,1,0:T(8,128)(2,1)S(1)}, bf16[3,40,224]{2,1,0:T(8,128)(2,1)S(1)}, u32[]{:S(2)}, u32[]{:S(2)}) collective-permute-start(bf16[3,40,224]{2,1,0:T(8,128)(2,1)S(1)} %get-tuple-element.336), channel_id=1, source_target_pairs={{0,24},{8,16},{16,8},{24,0},{1,25},{9,17},{17,9},{25,1},{2,26},{10... | collective-permute-start | bytes 161288 | tf_op jit(solution)/shard_map/ppermute | solution.py:451
  177.9 29.5 %collective-permute-start.16 = (bf16[3,40,224]{2,1,0:T(8,128)(2,1)S(1)}, bf16[3,40,224]{2,1,0:T(8,128)(2,1)S(1)}, u32[]{:S(2)}, u32[]{:S(2)}) collective-permute-start(bf16[3,40,224]{2,1,0:T(8,128)(2,1)S(1)} %get-tuple-element.337), channel_id=1, source_target_pairs={{0,16},{8,24},{16,0},{24,8},{1,17},{9,25},{17,1},{25,9},{2,18},{10... | collective-permute-start | bytes 161288 | tf_op jit(solution)/shard_map/ppermute | solution.py:451
  179.8 27.7 %collective-permute-start.15 = (bf16[3,40,224]{2,1,0:T(8,128)(2,1)S(1)}, bf16[3,40,224]{2,1,0:T(8,128)(2,1)S(1)}, u32[]{:S(2)}, u32[]{:S(2)}) collective-permute-start(bf16[3,40,224]{2,1,0:T(8,128)(2,1)S(1)} %get-tuple-element.338), channel_id=1, source_target_pairs={{0,8},{8,0},{16,24},{24,16},{1,9},{9,1},{17,25},{25,17},{2,10},{10... | collective-permute-start | bytes 161288 | tf_op jit(solution)/shard_map/ppermute | solution.py:451
  215.4 68.5 %all-to-all-start.3 = ((bf16[8,4,48,1280]{3,2,1,0:T(8,128)(2,1)}), bf16[8,4,48,1280]{3,2,1,0:T(8,128)(2,1)}, u32[]{:S(2)}, u32[]{:S(2)}) async-start(bf16[8,4,48,1280]{3,2,1,0:T(8,128)(2,1)} %copy.330), calls=%async_computation.3 | async-start | bytes 7864320 | tf_op jit(solution)/shard_map/all_to_all | solution.py:584
  223.2 52.7 %collective-permute-start.9 = (bf16[2,320,896]{2,1,0:T(8,128)(2,1)}, bf16[2,320,896]{2,1,0:T(8,128)(2,1)}, u32[]{:S(2)}, u32[]{:S(2)}) collective-permute-start(bf16[2,320,896]{2,1,0:T(8,128)(2,1)} %fusion.26), channel_id=1, source_target_pairs={{0,8},{8,0},{16,24},{24,16},{1,9},{9,1},{17,25},{25,17},{2,10},{10... | collective-permute-start | bytes 3440648 | tf_op jit(solution)/shard_map/ppermute | solution.py:521
  225.4 15.3 %collective-permute-start.10 = (bf16[1,320,896]{2,1,0:T(8,128)(2,1)}, bf16[1,320,896]{2,1,0:T(8,128)(2,1)S(1)}, u32[]{:S(2)}, u32[]{:S(2)}) collective-permute-start(bf16[1,320,896]{2,1,0:T(8,128)(2,1)} %get-tuple-element.106), channel_id=1, source_target_pairs={{0,24},{8,16},{16,8},{24,0},{1,25},{9,17},{17,9},{25,1},{2,26},{10... | collective-permute-start | bytes 1720328 | tf_op jit(solution)/shard_map/ppermute | solution.py:521
  240.6 31.0 %copy-start.20 = (bf16[1,320,896]{2,1,0:T(8,128)(2,1)}, bf16[1,320,896]{2,1,0:T(8,128)(2,1)S(1)}, u32[]{:S(2)}) copy-start(bf16[1,320,896]{2,1,0:T(8,128)(2,1)S(1)} %collective-permute-done.10.rest_7_) | copy-start | bytes 1720324
  240.6 77.6 %collective-permute-start.11 = (bf16[1,320,896]{2,1,0:T(8,128)(2,1)}, bf16[1,320,896]{2,1,0:T(8,128)(2,1)}, u32[]{:S(2)}, u32[]{:S(2)}) collective-permute-start(bf16[1,320,896]{2,1,0:T(8,128)(2,1)} %get-tuple-element.112), channel_id=1, source_target_pairs={{0,8},{8,0},{16,24},{24,16},{1,9},{9,1},{17,25},{25,17},{2,10},{10... | collective-permute-start | bytes 1720328 | tf_op jit(solution)/shard_map/ppermute | solution.py:521
  265.3 52.9 %collective-permute-start.12 = (bf16[1,320,896]{2,1,0:T(8,128)(2,1)}, bf16[1,320,896]{2,1,0:T(8,128)(2,1)}, u32[]{:S(2)}, u32[]{:S(2)}) collective-permute-start(bf16[1,320,896]{2,1,0:T(8,128)(2,1)} %get-tuple-element.113), channel_id=1, source_target_pairs={{0,16},{8,24},{16,0},{24,8},{1,17},{9,25},{17,1},{25,9},{2,18},{10... | collective-permute-start | bytes 1720328 | tf_op jit(solution)/shard_map/ppermute | solution.py:521
  266.1 52.1 %collective-permute-start.13 = (bf16[1,320,896]{2,1,0:T(8,128)(2,1)}, bf16[1,320,896]{2,1,0:T(8,128)(2,1)}, u32[]{:S(2)}, u32[]{:S(2)}) collective-permute-start(bf16[1,320,896]{2,1,0:T(8,128)(2,1)} %get-tuple-element.114), channel_id=1, source_target_pairs={{0,24},{8,16},{16,8},{24,0},{1,25},{9,17},{17,9},{25,1},{2,26},{10... | collective-permute-start | bytes 1720328 | tf_op jit(solution)/shard_map/ppermute | solution.py:521
  274.9 117.8 %copy-start.61 = (pred[4,4,8,128]{3,2,1,0:T(8,128)(4,1)}, pred[4,4,8,128]{3,2,1,0:T(8,128)(4,1)S(1)}, u32[]{:S(2)}) copy-start(pred[4,4,8,128]{3,2,1,0:T(8,128)(4,1)S(1)} %fusion.90) | copy-start | bytes 49156
  314.5 45.9 %collective-permute-start.14 = (bf16[1,320,896]{2,1,0:T(8,128)(2,1)}, bf16[1,320,896]{2,1,0:T(8,128)(2,1)}, u32[]{:S(2)}, u32[]{:S(2)}) collective-permute-start(bf16[1,320,896]{2,1,0:T(8,128)(2,1)} %get-tuple-element.312), channel_id=1, source_target_pairs={{0,16},{8,24},{16,0},{24,8},{1,17},{9,25},{17,1},{25,9},{2,18},{10... | collective-permute-start | bytes 1720328 | tf_op jit(solution)/shard_map/ppermute | solution.py:618
  345.7 8.9 %all-to-all-start.6 = ((f32[8,8,192]{2,1,0:T(8,128)}), f32[8,8,192]{2,1,0:T(8,128)S(1)}, u32[]{:S(2)}, u32[]{:S(2)}) async-start(f32[8,8,192]{2,1,0:T(8,128)} %get-tuple-element.123), calls=%async_computation.6 | async-start | bytes 131072 | tf_op jit(solution)/shard_map/all_to_all | solution.py:633
  354.6 50.8 %all-to-all-start.4 = ((bf16[8,4,48,1280]{3,2,1,0:T(8,128)(2,1)}), bf16[8,4,48,1280]{3,2,1,0:T(8,128)(2,1)}, u32[]{:S(2)}, u32[]{:S(2)}) async-start(bf16[8,4,48,1280]{3,2,1,0:T(8,128)(2,1)} %bitcast.334), calls=%async_computation.4 | async-start | bytes 7864320 | tf_op jit(solution)/shard_map/all_to_all | solution.py:658
  359.1 171.8 %reduce-scatter.8.cloned.1.call-start = ((), (), s32[]{:S(2)}) async-start(), calls=%async_computation.15 | async-start | bytes 2211840 | tf_op jit(solution)/shard_map/reduce_scatter | solution.py:745
  376.8 32.6 %collective-permute-start.18 = (bf16[1,320,896]{2,1,0:T(8,128)(2,1)}, bf16[1,320,896]{2,1,0:T(8,128)(2,1)}, u32[]{:S(2)}, u32[]{:S(2)}) collective-permute-start(bf16[1,320,896]{2,1,0:T(8,128)(2,1)} %get-tuple-element.124), channel_id=1, source_target_pairs={{0,24},{8,16},{16,8},{24,0},{1,25},{9,17},{17,9},{25,1},{2,26},{10... | collective-permute-start | bytes 1720328 | tf_op jit(solution)/shard_map/ppermute | solution.py:618
  409.5 22.1 %collective-permute-start.19 = (bf16[2,128,1280]{2,1,0:T(8,128)(2,1)S(1)}, bf16[2,128,1280]{2,1,0:T(8,128)(2,1)S(1)}, u32[]{:S(2)}, u32[]{:S(2)}) collective-permute-start(bf16[2,128,1280]{2,1,0:T(8,128)(2,1)S(1)} %split.37), channel_id=1, source_target_pairs={{0,8},{8,0},{16,24},{24,16},{1,9},{9,1},{17,25},{25,17},{2,10},{10... | collective-permute-start | bytes 1966088 | tf_op jit(solution)/shard_map/ppermute | solution.py:471
  412.1 24.1 %copy-start.29 = (bf16[1280,512]{1,0:T(8,128)(2,1)S(1)}, bf16[1280,512]{1,0:T(8,128)(2,1)}, u32[]{:S(2)}) copy-start(bf16[1280,512]{1,0:T(8,128)(2,1)} %copy.345) | copy-start | bytes 3932164
  412.1 24.1 %copy-start.62 = (pred[4,4,8,128]{3,2,1,0:T(8,128)(4,1)S(1)}, pred[4,4,8,128]{3,2,1,0:T(8,128)(4,1)}, u32[]{:S(2)}) copy-start(pred[4,4,8,128]{3,2,1,0:T(8,128)(4,1)} %copy-done.61) | copy-start | bytes 49156
  412.2 24.1 %copy-start.64 = (f32[512,32]{0,1:T(8,128)S(1)}, f32[512,32]{0,1:T(8,128)}, u32[]{:S(2)}) copy-start(f32[512,32]{0,1:T(8,128)} %copy-done.63) | copy-start | bytes 196612
  412.2 24.1 %copy-start.70 = (f32[512]{0:T(512)S(1)}, f32[512]{0:T(512)}, u32[]{:S(2)}) copy-start(f32[512]{0:T(512)} %copy-done.69) | copy-start | bytes 6148
  412.2 24.1 %copy-start.72 = (f32[512]{0:T(512)S(1)}, f32[512]{0:T(512)}, u32[]{:S(2)}) copy-start(f32[512]{0:T(512)} %copy-done.71) | copy-start | bytes 6148
  412.2 24.1 %copy-start.76 = (f32[512]{0:T(512)S(1)}, f32[512]{0:T(512)}, u32[]{:S(2)}) copy-start(f32[512]{0:T(512)} %copy-done.75) | copy-start | bytes 6148
  412.2 63.2 %collective-permute-start.21 = (bf16[2,320,896]{2,1,0:T(8,128)(2,1)}, bf16[2,320,896]{2,1,0:T(8,128)(2,1)}, u32[]{:S(2)}, u32[]{:S(2)}) collective-permute-start(bf16[2,320,896]{2,1,0:T(8,128)(2,1)} %get-tuple-element.126), channel_id=1, source_target_pairs={{0,16},{8,24},{16,0},{24,8},{1,17},{9,25},{17,1},{25,9},{2,18},{10... | collective-permute-start | bytes 3440648 | tf_op jit(solution)/shard_map/ppermute | solution.py:618
  432.5 41.9 %collective-permute-start.20 = (bf16[1,128,1280]{2,1,0:T(8,128)(2,1)}, bf16[1,128,1280]{2,1,0:T(8,128)(2,1)}, u32[]{:S(2)}, u32[]{:S(2)}) collective-permute-start(bf16[1,128,1280]{2,1,0:T(8,128)(2,1)} %split.49), channel_id=1, source_target_pairs={{0,16},{8,24},{16,0},{24,8},{1,17},{9,25},{17,1},{25,9},{2,18},{10... | collective-permute-start | bytes 983048 | tf_op jit(solution)/shard_map/ppermute | solution.py:471
  438.2 58.9 %all-to-all-start.5 = ((bf16[8,4,48,1280]{3,2,1,0:T(8,128)(2,1)}), bf16[8,4,48,1280]{3,2,1,0:T(8,128)(2,1)}, u32[]{:S(2)}, u32[]{:S(2)}) async-start(bf16[8,4,48,1280]{3,2,1,0:T(8,128)(2,1)} %bitcast.333), calls=%async_computation.5 | async-start | bytes 7864320 | tf_op jit(solution)/shard_map/all_to_all | solution.py:658
  443.2 165.3 %reduce-scatter.6.cloned.1.call-start = ((), (), s32[]{:S(2)}) async-start(), calls=%async_computation.14 | async-start | bytes 4055040 | tf_op jit(solution)/shard_map/reduce_scatter | solution.py:679
  497.1 20.5 %all-to-all-start.7 = ((bf16[8,128,512]{2,1,0:T(8,128)(2,1)}), bf16[8,128,512]{2,1,0:T(8,128)(2,1)}, u32[]{:S(2)}, u32[]{:S(2)}) async-start(bf16[8,128,512]{2,1,0:T(8,128)(2,1)} %get-tuple-element.129), calls=%async_computation.7 | async-start | bytes 2097152 | tf_op jit(solution)/shard_map/all_to_all | solution.py:693
  502.2 53.0 %collective-permute-start.31 = (bf16[2,320,896]{2,1,0:T(8,128)(2,1)}, bf16[2,320,896]{2,1,0:T(8,128)(2,1)}, u32[]{:S(2)}, u32[]{:S(2)}) collective-permute-start(bf16[2,320,896]{2,1,0:T(8,128)(2,1)} %get-tuple-element.140), channel_id=1, source_target_pairs={{0,24},{8,16},{16,8},{24,0},{1,25},{9,17},{17,9},{25,1},{2,26},{10... | collective-permute-start | bytes 3440648 | tf_op jit(solution)/shard_map/ppermute | solution.py:618
  506.8 10.8 %copy-start.34 = (bf16[32,40,512]{2,1,0:T(8,128)(2,1)S(1)}, bf16[32,40,512]{2,1,0:T(8,128)(2,1)}, u32[]{:S(2)}) copy-start(bf16[32,40,512]{2,1,0:T(8,128)(2,1)} %copy-done.33) | copy-start | bytes 3932164
  527.5 78.4 %collective-permute-start.22 = (bf16[2,128,1280]{2,1,0:T(8,128)(2,1)}, bf16[2,128,1280]{2,1,0:T(8,128)(2,1)}, u32[]{:S(2)}, u32[]{:S(2)}) collective-permute-start(bf16[2,128,1280]{2,1,0:T(8,128)(2,1)} %split.41), channel_id=1, source_target_pairs={{0,8},{8,0},{16,24},{24,16},{1,9},{9,1},{17,25},{25,17},{2,10},{10... | collective-permute-start | bytes 1966088 | tf_op jit(solution)/shard_map/ppermute | solution.py:471
  530.9 70.7 %collective-permute-start.30 = (bf16[1,320,896]{2,1,0:T(8,128)(2,1)}, bf16[1,320,896]{2,1,0:T(8,128)(2,1)S(1)}, u32[]{:S(2)}, u32[]{:S(2)}) collective-permute-start(bf16[1,320,896]{2,1,0:T(8,128)(2,1)} %get-tuple-element.138), channel_id=1, source_target_pairs={{0,8},{8,0},{16,24},{24,16},{1,9},{9,1},{17,25},{25,17},{2,10},{10... | collective-permute-start | bytes 1720328 | tf_op jit(solution)/shard_map/ppermute | solution.py:625
  532.0 66.6 %collective-permute-start.28 = (bf16[3,40,224]{2,1,0:T(8,128)(2,1)S(1)}, bf16[3,40,224]{2,1,0:T(8,128)(2,1)S(1)}, u32[]{:S(2)}, u32[]{:S(2)}) collective-permute-start(bf16[3,40,224]{2,1,0:T(8,128)(2,1)S(1)} %get-tuple-element.331), channel_id=1, source_target_pairs={{0,24},{8,16},{16,8},{24,0},{1,25},{9,17},{17,9},{25,1},{2,26},{10... | collective-permute-start | bytes 161288 | tf_op jit(solution)/shard_map/ppermute | solution.py:451
  532.8 65.3 %collective-permute-start.27 = (bf16[3,40,224]{2,1,0:T(8,128)(2,1)S(1)}, bf16[3,40,224]{2,1,0:T(8,128)(2,1)S(1)}, u32[]{:S(2)}, u32[]{:S(2)}) collective-permute-start(bf16[3,40,224]{2,1,0:T(8,128)(2,1)S(1)} %get-tuple-element.332), channel_id=1, source_target_pairs={{0,16},{8,24},{16,0},{24,8},{1,17},{9,25},{17,1},{25,9},{2,18},{10... | collective-permute-start | bytes 161288 | tf_op jit(solution)/shard_map/ppermute | solution.py:451
  555.1 40.7 %collective-permute-start.26 = (bf16[3,40,224]{2,1,0:T(8,128)(2,1)S(1)}, bf16[3,40,224]{2,1,0:T(8,128)(2,1)S(1)}, u32[]{:S(2)}, u32[]{:S(2)}) collective-permute-start(bf16[3,40,224]{2,1,0:T(8,128)(2,1)S(1)} %get-tuple-element.333), channel_id=1, source_target_pairs={{0,8},{8,0},{16,24},{24,16},{1,9},{9,1},{17,25},{25,17},{2,10},{10... | collective-permute-start | bytes 161288 | tf_op jit(solution)/shard_map/ppermute | solution.py:451
  557.7 88.3 %all-to-all-start.8 = ((bf16[32,40,512]{2,1,0:T(8,128)(2,1)}), bf16[32,40,512]{2,1,0:T(8,128)(2,1)}, u32[]{:S(2)}, u32[]{:S(2)}) async-start(bf16[32,40,512]{2,1,0:T(8,128)(2,1)} %bitcast.69), calls=%async_computation.9 | async-start | bytes 2621440 | tf_op jit(solution)/shard_map/all_to_all | solution.py:698
  564.7 86.3 %reduce-scatter.4.cloned.1.call-start = ((), (), s32[]{:S(2)}) async-start(), calls=%async_computation.13 | async-start | bytes 2949120 | tf_op jit(solution)/shard_map/reduce_scatter | solution.py:705
  589.4 10.1 %copy-start.60 = (f32[3,40,896]{2,1,0:T(8,128)S(1)}, f32[3,40,896]{2,1,0:T(8,128)}, u32[]{:S(2)}) copy-start(f32[3,40,896]{2,1,0:T(8,128)} %param.29) | copy-start | bytes 1290244
  595.9 41.4 %collective-permute-start.29 = (bf16[2,320,896]{2,1,0:T(8,128)(2,1)}, bf16[2,320,896]{2,1,0:T(8,128)(2,1)}, u32[]{:S(2)}, u32[]{:S(2)}) collective-permute-start(bf16[2,320,896]{2,1,0:T(8,128)(2,1)} %get-tuple-element.136), channel_id=1, source_target_pairs={{0,8},{8,0},{16,24},{24,16},{1,9},{9,1},{17,25},{25,17},{2,10},{10... | collective-permute-start | bytes 3440648 | tf_op jit(solution)/shard_map/ppermute | solution.py:625
  606.0 25.3 %copy-start.82 = (f32[128]{0:T(128)S(1)}, f32[128]{0:T(128)}, u32[]{:S(2)}) copy-start(f32[128]{0:T(128)} %get-tuple-element.282) | copy-start | bytes 1540
  607.3 24.0 %collective-permute-start.23 = (bf16[1,128,1280]{2,1,0:T(8,128)(2,1)S(1)}, bf16[1,128,1280]{2,1,0:T(8,128)(2,1)S(1)}, u32[]{:S(2)}, u32[]{:S(2)}) collective-permute-start(bf16[1,128,1280]{2,1,0:T(8,128)(2,1)S(1)} %split.51), channel_id=1, source_target_pairs={{0,16},{8,24},{16,0},{24,8},{1,17},{9,25},{17,1},{25,9},{2,18},{10... | collective-permute-start | bytes 983048 | tf_op jit(solution)/shard_map/ppermute | solution.py:471
  609.7 25.7 %collective-permute-start.24 = (bf16[2,40,1408]{2,1,0:T(8,128)(2,1)S(1)}, bf16[2,40,1408]{2,1,0:T(8,128)(2,1)}, u32[]{:S(2)}, u32[]{:S(2)}) collective-permute-start(bf16[2,40,1408]{2,1,0:T(8,128)(2,1)S(1)} %split.45), channel_id=1, source_target_pairs={{0,8},{8,0},{16,24},{24,16},{1,9},{9,1},{17,25},{25,17},{2,10},{10... | collective-permute-start | bytes 675848 | tf_op jit(solution)/shard_map/ppermute | solution.py:471
  636.4 7.2 %collective-permute-start.25 = (bf16[1,40,1408]{2,1,0:T(8,128)(2,1)S(1)}, bf16[1,40,1408]{2,1,0:T(8,128)(2,1)S(1)}, u32[]{:S(2)}, u32[]{:S(2)}) collective-permute-start(bf16[1,40,1408]{2,1,0:T(8,128)(2,1)S(1)} %split.53), channel_id=1, source_target_pairs={{0,16},{8,24},{16,0},{24,8},{1,17},{9,25},{17,1},{25,9},{2,18},{10... | collective-permute-start | bytes 337928 | tf_op jit(solution)/shard_map/ppermute | solution.py:471
  (73 other events, 227.3 us)
Sparse Core Ops, SparseCore 0:
  10.5 40.8 all-gather.5
  53.8 41.7 all-gather.7
  208.3 44.9 all-gather.9
  387.9 42.0 reduce-scatter.7
  494.5 52.4 reduce-scatter.5
  568.9 45.4 reduce-scatter.3

commit v4 on v3

--- a/solution.py
+++ b/solution.py
@@ -681,7 +681,7 @@
         return jnp.concatenate([lax.dynamic_slice_in_dim(x, zi ^ o, 1, 0) for o in offs], 0)
 
     middle_grad, attn_grad, second_gain_grad, proj_grad = attend_back(
-        after(inner_grad, front_got[2]), cotangent, middle, packed, gain_row, heads_in, doc_row, doc_col, cosine, sine
+        after(inner_grad, routed_back, front_got[2]), cotangent, middle, packed, gain_row, heads_in, doc_row, doc_col, cosine, sine
     )
     output_grad = mm_tn(heads_out, attn_grad)
     pad = jnp.zeros((D, 128 - experts - 1), F32)
@@ -690,7 +690,7 @@
     ).astype(BF)
     small_own = reduce_rows(small_all)
 
-    proj_grad = lax.all_to_all(after(proj_grad, routed_back), "expert", split_axis=0, concat_axis=0, tiled=True)
+    proj_grad = lax.all_to_all(after(proj_grad, small_all), "expert", split_axis=0, concat_axis=0, tiled=True)
     proj_grad = proj_grad.reshape(E * L, wide)
     proj_w_grad = mm_tn(unit_all, proj_grad).astype(BF).reshape(Z * E, R, wide)
     proj_w_local = proj_w_grad
@@ -726,7 +726,7 @@
     owned = (expert_weight, expert_momentum, expert_average)
     expert_new = ()
     expert_sum = jnp.zeros((local, 3, deep, FF), BF)
-    down_got[1] = send_near(down_grad, proj_w_local)
+    down_got[1] = send_near(down_grad, proj_w_local, proj_w_grad)
     front_got[1] = send_near(front_grad, proj_w_local)
     for k in [0] + list(range(2, Z)) + [1]:
         for m, gots in ((2, down_got), (0, front_got)):

time: 674 us -> 738 us (1.095)
  waiting for transfers between devices: 248 us -> 288 us
  blocking collectives: 0 us -> 19 us
  local copies, waits for them, and re-layouts: 90.6 us -> 101 us
    ppermute x4, waiting for transfers between devices: 18.7 us -> 56.1 us  [send_grads(): piece = lax.ppermute(piece, 'dp', [(i, i ^ k) for i in range(Z)])]
    all_to_all x0 -> x1, blocking collectives: none -> 19 us  [body(): lax.all_to_all(after(proj_grad, small_all), 'expert', split_axis=0, conca...]
    ppermute x6, waiting for transfers between devices: 71.9 us -> 86 us  [reduce_z(): got = lax.ppermute(send, 'dp', [(i, i ^ stride) for i in range(Z)])]
    all_to_all x2, waiting for transfers between devices: 9.59 us -> 0.01 us  [collect(): lax.all_to_all(rows_in.reshape(E, Z, cap, D), 'expert', split_axis=0, con...]
    all_to_all x1 -> x0, waiting for transfers between devices: 9.12 us -> none  [body(): lax.all_to_all(after(proj_grad, routed_back), 'expert', split_axis=0, con...]
    unnamed x190 -> x174, local copies, waits for them, and re-layouts: 26.7 us -> 34.5 us
    ppermute x2, waiting for transfers between devices: 0.01 us -> 7.43 us  [send_near(): lax.ppermute(after(piece, *needed), 'dp', [(i, i ^ 1) for i in range(Z)])]
  transfers between devices with their start and end apart: 47 -> 46, of which waited for: 17 -> 18; matrix products, arithmetic and copies ran while one was open for 20% -> 19% of each run, Pallas kernels for 17% -> 11%
where the time goes in v4:
time: 738 us; the launch traced here: 725 us
  waiting for transfers between devices  288 us (39%)
  starting transfers between devices  116 us (16%)
  Pallas kernels  110 us (15%)
  local copies, waits for them, and re-layouts  101 us (14%)
  matrix products  39.5 us (5%)
  other arithmetic  33.6 us (5%)
  blocking collectives  19 us (3%)
  between operations  17.8 us (2%)
    ppermute x6, waiting for transfers between devices, reduce_z(): got = lax.ppermute(send, 'dp', [(i, i ^ stride) for i in range(Z)])  86 us
    ppermute x4, waiting for transfers between devices, send_grads(): piece = lax.ppermute(piece, 'dp', [(i, i ^ k) for i in range(Z)])  56.1 us
    ppermute x6, waiting for transfers between devices, gather_z(): got = lax.ppermute(held, 'dp', [(i, i ^ stride) for i in range(Z)])  46.4 us
    pallas_call x8, Pallas kernels, update_part(): pl.pallas_call(update_kernel, grid_spec=pltpu.PrefetchScalarGridSpec(num_...  38.7 us
    ppermute x8, starting transfers between devices, fetch(): lax.ppermute(after(piece_of(k, low, high), *needed), 'dp', [(i, i ^ k) fo...  35 us
    unnamed x174, local copies, waits for them, and re-layouts  34.5 us
    ppermute x8, waiting for transfers between devices, fetch(): lax.ppermute(after(piece_of(k, low, high), *needed), 'dp', [(i, i ^ k) fo...  34.2 us
    ppermute x6, waiting for transfers between devices, swap_z(): out.append(lax.ppermute(pieces[k], 'dp', [(i, i ^ k) for i in range(Z)]))  27.5 us
  transfers between devices with their start and end apart: 46, of which 18 were waited for; matrix products, arithmetic and copies ran while one was open for 19% of the time, Pallas kernels for 11%

profile of v4, /device:TPU:16, one launch (start us, length us, event | category | flops | bytes accessed | tf_op | source)
XLA Modules:
  0.0 724.6 jit_solution(31947484144923405)
XLA Ops:
  13.1 5.8 collective-permute-done.1
  18.9 3.8 collective-permute-start.2
  24.4 4.9 all-to-all-start
  31.8 27.2 %all-to-all-done = bf16[32,40,512]{2,1,0:T(8,128)(2,1)S(1)} async-done(((bf16[32,40,512]{2,1,0:T(8,128)(2,1)}), bf16[32,40,512]{2,1,0:T(8,128)(2,1)S(1)}, u32[]{:S(2)}, u32[]{:S(2)}) %all-to-all-start) | async-done | bytes 1310752 | tf_op jit(solution)/shard_map/all_to_all | solution.py:491
  60.5 3.7 fusion.112
  66.3 3.6 all-to-all-start.1
  70.0 2.9 collective-permute-start.3
  72.9 15.5 %collective-permute-done.3 = bf16[1,128,1408]{1,2,0:T(8,128)(2,1)S(1)} collective-permute-done((bf16[1,128,1408]{1,2,0:T(8,128)(2,1)S(1)}, bf16[1,128,1408]{1,2,0:T(8,128)(2,1)S(1)}, u32[]{:S(2)}, u32[]{:S(2)}) %collective-permute-start.3) | collective-permute-done | bytes 360480 | tf_op jit(solution)/shard_map/ppermute | solution.py:464
  88.5 2.9 all-to-all-done.1.heads_ref
  93.6 6.7 fusion.57
  100.3 2.9 collective-permute-start
  103.2 12.0 %collective-permute-done.4 = bf16[2,128,1408]{1,2,0:T(8,128)(2,1)} collective-permute-done((bf16[2,128,1408]{1,2,0:T(8,128)(2,1)S(1)}, bf16[2,128,1408]{1,2,0:T(8,128)(2,1)}, u32[]{:S(2)}, u32[]{:S(2)}) %collective-permute-start.4) | collective-permute-done | bytes 720928 | tf_op jit(solution)/shard_map/ppermute | solution.py:464
  118.9 2.5 copy.329
  121.3 4.7 all-to-all-start.2
  126.5 2.7 collective-permute-start.5
  129.2 3.3 attend.1.heads_ref
  137.5 16.7 %collective-permute-done.5.rest_6_ = bf16[1,320,896]{2,1,0:T(8,128)(2,1)} collective-permute-done((bf16[1,320,896]{2,1,0:T(8,128)(2,1)}, bf16[1,320,896]{2,1,0:T(8,128)(2,1)}, u32[]{:S(2)}, u32[]{:S(2)}) %collective-permute-start.5) | collective-permute-done | bytes 573472 | tf_op jit(solution)/shard_map/ppermute | solution.py:521
  154.2 3.4 collective-permute-start.6
  157.6 13.1 %collective-permute-done.6 = bf16[1,128,1280]{2,1,0:T(8,128)(2,1)S(1)} collective-permute-done((bf16[1,128,1280]{2,1,0:T(8,128)(2,1)S(1)}, bf16[1,128,1280]{2,1,0:T(8,128)(2,1)S(1)}, u32[]{:S(2)}, u32[]{:S(2)}) %collective-permute-start.6) | collective-permute-done | bytes 327712 | tf_op jit(solution)/shard_map/ppermute | solution.py:464
  172.3 3.3 collective-permute-start.7
  180.0 27.5 %collective-permute-done.17 = bf16[3,40,224]{2,1,0:T(8,128)(2,1)S(1)} collective-permute-done((bf16[3,40,224]{2,1,0:T(8,128)(2,1)S(1)}, bf16[3,40,224]{2,1,0:T(8,128)(2,1)S(1)}, u32[]{:S(2)}, u32[]{:S(2)}) %collective-permute-start.17) | collective-permute-done | bytes 53792 | tf_op jit(solution)/shard_map/ppermute | solution.py:451
  210.6 2.5 fusion.5
  215.4 5.1 all-to-all-start.3
  220.5 2.8 fusion.26
  226.0 14.6 %collective-permute-done.10.rest_7_ = bf16[1,320,896]{2,1,0:T(8,128)(2,1)S(1)} collective-permute-done((bf16[1,320,896]{2,1,0:T(8,128)(2,1)}, bf16[1,320,896]{2,1,0:T(8,128)(2,1)S(1)}, u32[]{:S(2)}, u32[]{:S(2)}) %collective-permute-start.10) | collective-permute-done | bytes 573472 | tf_op jit(solution)/shard_map/ppermute | solution.py:521
  240.6 24.7 %collective-permute-start.11 = (bf16[1,320,896]{2,1,0:T(8,128)(2,1)}, bf16[1,320,896]{2,1,0:T(8,128)(2,1)}, u32[]{:S(2)}, u32[]{:S(2)}) collective-permute-start(bf16[1,320,896]{2,1,0:T(8,128)(2,1)} %get-tuple-element.111), channel_id=1, source_target_pairs={{0,8},{8,0},{16,24},{24,16},{1,9},{9,1},{17,25},{25,17},{2,10},{10... | collective-permute-start | bytes 1720328 | tf_op jit(solution)/shard_map/ppermute | solution.py:521
  266.8 2.5 slice.162
  288.2 15.9 %expert_front.1 = (f32[1536,896]{1,0:T(8,128)}, f32[1536,896]{1,0:T(8,128)}, bf16[1536,896]{1,0:T(8,128)(2,1)S(1)}, f32[1536,128]{1,0:T(8,128)S(1)}) custom-call(s32[2]{0:T(128)S(1)} %pad_add_fusion.place_ref, bf16[1536,1280]{1,0:T(8,128)(2,1)} %bitcast.38.x_ref, bf16[1536,1408]{1,0:T(8,128)(2,1)} %bitcast.31.hot_ref.x_ref.g_ref, ...), custom_call_target="tpu_custom_call" | custom-call | flops 7046430720 | bytes 16515072 | tf_op jit(solution)/shard_map/expert_front/pallas_call | solution.py:254
  305.0 7.4 %weight_grads.2 = bf16[1,1280,896]{2,1,0:T(8,128)(2,1)S(1)} custom-call(bf16[1536,1408]{1,0:T(8,128)(2,1)} %bitcast.31.hot_ref.x_ref.g_ref, bf16[1536,896]{1,0:T(8,128)(2,1)S(1)} %get-tuple-element.109.rest_0_.gated_ref), custom_call_target="tpu_custom_call" | custom-call | flops 3523215360 | bytes 6684672 | tf_op jit(solution)/shard_map/weight_grads/pallas_call | solution.py:358
  313.8 2.9 collective-permute-done.13.rest_11_
  316.7 27.3 %expert_back.1 = (bf16[1536,1280]{1,0:T(8,128)(2,1)}, bf16[1536,1280]{1,0:T(8,128)(2,1)}, bf16[1536,896]{1,0:T(8,128)(2,1)}, bf16[1536,896]{1,0:T(8,128)(2,1)}, f32[8,8,192]{2,1,0:T(8,128)}) custom-call(s32[2]{0:T(128)S(1)} %pad_add_fusion.place_ref, bf16[1536,1408]{1,0:T(8,128)(2,1)} %bitcast.31.hot_ref.x_ref.g_ref, f32[1536,896]{1,0:T(8,128)} %get-tuple-element.106.eg_ref, ...), custom_call_target="tpu_custom_call" | custom-call | flops 14092861440 | bytes 22020096 | tf_op jit(solution)/shard_map/expert_back/pallas_call | solution.py:323
  344.0 3.7 all-to-all-start.6
  347.7 3.0 constant_dynamic-slice_fusion
  353.7 4.7 all-to-all-start.4
  358.3 2.7 fusion.109
  362.1 15.2 %collective-permute-done.14.g_ref = bf16[1,320,896]{2,1,0:T(8,128)(2,1)} collective-permute-done((bf16[1,320,896]{2,1,0:T(8,128)(2,1)}, bf16[1,320,896]{2,1,0:T(8,128)(2,1)}, u32[]{:S(2)}, u32[]{:S(2)}) %collective-permute-start.14) | collective-permute-done | bytes 573472 | tf_op jit(solution)/shard_map/ppermute | solution.py:618
  380.9 10.8 %weight_grads.3 = bf16[2,1280,896]{2,1,0:T(8,128)(2,1)S(1)} custom-call(bf16[1536,1280]{1,0:T(8,128)(2,1)} %bitcast.38.x_ref, bf16[1536,896]{1,0:T(8,128)(2,1)S(1)} %copy-done.29, bf16[1536,896]{1,0:T(8,128)(2,1)S(1)} %copy-done.30), custom_call_target="tpu_custom_call" | custom-call | flops 7046430720 | bytes 6684672 | tf_op jit(solution)/shard_map/weight_grads/pallas_call | solution.py:358
  409.4 4.5 all-to-all-start.5
  422.6 3.2 fusion.15
  425.9 4.3 collective-permute-start.19
  432.8 22.4 %collective-permute-done.19 = bf16[2,128,1280]{2,1,0:T(8,128)(2,1)S(1)} collective-permute-done((bf16[2,128,1280]{2,1,0:T(8,128)(2,1)S(1)}, bf16[2,128,1280]{2,1,0:T(8,128)(2,1)S(1)}, u32[]{:S(2)}, u32[]{:S(2)}) %collective-permute-start.19) | collective-permute-done | bytes 655392 | tf_op jit(solution)/shard_map/ppermute | solution.py:471
  456.2 3.2 collective-permute-start.20
  461.3 35.4 %collective-permute-done.20 = bf16[1,128,1280]{2,1,0:T(8,128)(2,1)} collective-permute-done((bf16[1,128,1280]{2,1,0:T(8,128)(2,1)S(1)}, bf16[1,128,1280]{2,1,0:T(8,128)(2,1)}, u32[]{:S(2)}, u32[]{:S(2)}) %collective-permute-start.20) | collective-permute-done | bytes 327712 | tf_op jit(solution)/shard_map/ppermute | solution.py:471
  499.9 5.9 attend_back.1
  511.2 6.5 concatenate.77
  518.9 19.0 %all_to_all.45 = bf16[8,128,512]{2,1,0:T(8,128)(2,1)S(1)} all-to-all(bf16[8,128,512]{2,1,0:T(8,128)(2,1)S(1)} %copy-done.8), channel_id=1, replica_groups=mesh['dp'=4,'expert'=8] {'expert'}, dimensions={0} | all-to-all | bytes 2097152 | tf_op jit(solution)/shard_map/all_to_all | solution.py:693
  538.9 3.0 convolution_convert_fusion.3
  543.3 4.4 convolution_convert_fusion.4
  547.7 6.2 all-to-all-start.8
  554.0 3.1 fusion.6
  568.6 23.5 %collective-permute-done.22 = bf16[2,128,1280]{2,1,0:T(8,128)(2,1)} collective-permute-done((bf16[2,128,1280]{2,1,0:T(8,128)(2,1)S(1)}, bf16[2,128,1280]{2,1,0:T(8,128)(2,1)}, u32[]{:S(2)}, u32[]{:S(2)}) %collective-permute-start.22) | collective-permute-done | bytes 655392 | tf_op jit(solution)/shard_map/ppermute | solution.py:471
  594.6 40.8 %collective-permute-done.31.g_ref = bf16[2,320,896]{2,1,0:T(8,128)(2,1)} collective-permute-done((bf16[2,320,896]{2,1,0:T(8,128)(2,1)}, bf16[2,320,896]{2,1,0:T(8,128)(2,1)}, u32[]{:S(2)}, u32[]{:S(2)}) %collective-permute-start.31) | collective-permute-done | bytes 1146912 | tf_op jit(solution)/shard_map/ppermute | solution.py:618
  638.5 3.4 update_part.8
  641.9 6.3 update_part.9
  648.1 3.4 update_part.10
  651.5 6.3 update_part.11
  657.8 3.4 update_part.12
  661.2 6.3 update_part.13
  672.8 3.4 collective-permute-start.30
  681.1 7.4 %collective-permute-done.30.g_ref = bf16[1,320,896]{2,1,0:T(8,128)(2,1)} collective-permute-done((bf16[1,320,896]{2,1,0:T(8,128)(2,1)}, bf16[1,320,896]{2,1,0:T(8,128)(2,1)}, u32[]{:S(2)}, u32[]{:S(2)}) %collective-permute-start.30) | collective-permute-done | bytes 573472 | tf_op jit(solution)/shard_map/ppermute | solution.py:625
  688.5 3.4 update_part.14
  691.9 6.3 update_part.15
  702.6 2.9 collective-permute-done.24
  714.4 3.1 multiply_add_fusion
  (368 shorter events, 151.0 us)
Async XLA Ops:
  7.2 53.3 %all-gather.6.cloned.1.call-start = ((), (), s32[]{:S(2)}) async-start(), calls=%async_computation.12 | async-start | bytes 2949120 | tf_op jit(solution)/shard_map/all_gather | solution.py:497
  12.9 11.4 %copy-start.44 = (bf16[4,40,1280]{2,1,0:T(8,128)(2,1)}, bf16[4,40,1280]{2,1,0:T(8,128)(2,1)S(1)}, u32[]{:S(2)}) copy-start(bf16[4,40,1280]{2,1,0:T(8,128)(2,1)S(1)} %convert.43) | copy-start | bytes 1228804
  13.0 5.9 collective-permute-start.1
  18.9 10.4 %collective-permute-start.2 = (bf16[2,40,1408]{2,1,0:T(8,128)(2,1)S(1)}, bf16[2,40,1408]{2,1,0:T(8,128)(2,1)S(1)}, u32[]{:S(2)}, u32[]{:S(2)}) collective-permute-start(bf16[2,40,1408]{2,1,0:T(8,128)(2,1)S(1)} %pad_maximum_fusion.7), channel_id=1, source_target_pairs={{0,8},{8,0},{16,24},{24,16},{1,9},{9,1},{17,25},{25,17},{2,10},{10... | collective-permute-start | bytes 675848 | tf_op jit(solution)/shard_map/ppermute | solution.py:464
  24.4 34.7 %all-to-all-start = ((bf16[32,40,512]{2,1,0:T(8,128)(2,1)}), bf16[32,40,512]{2,1,0:T(8,128)(2,1)S(1)}, u32[]{:S(2)}, u32[]{:S(2)}) async-start(bf16[32,40,512]{2,1,0:T(8,128)(2,1)} %bitcast.332), calls=%async_computation | async-start | bytes 2621440 | tf_op jit(solution)/shard_map/all_to_all | solution.py:491
  29.3 103.3 %all-gather.8.cloned.1.call-start = ((), (), s32[]{:S(2)}) async-start(), calls=%async_computation.16 | async-start | bytes 4055040 | tf_op jit(solution)/shard_map/all_gather | solution.py:502
  66.3 25.0 %all-to-all-start.1 = ((bf16[8,128,512]{2,1,0:T(8,128)(2,1)}), bf16[8,128,512]{2,1,0:T(8,128)(2,1)S(1)}, u32[]{:S(2)}, u32[]{:S(2)}) async-start(bf16[8,128,512]{2,1,0:T(8,128)(2,1)} %copy.368), calls=%async_computation.1 | async-start | bytes 2097152 | tf_op jit(solution)/shard_map/all_to_all | solution.py:548
  70.0 18.4 %collective-permute-start.3 = (bf16[1,128,1408]{1,2,0:T(8,128)(2,1)S(1)}, bf16[1,128,1408]{1,2,0:T(8,128)(2,1)S(1)}, u32[]{:S(2)}, u32[]{:S(2)}) collective-permute-start(bf16[1,128,1408]{1,2,0:T(8,128)(2,1)S(1)} %bitcast.349), channel_id=1, source_target_pairs={{0,16},{8,24},{16,0},{24,8},{1,17},{9,25},{17,1},{25,9},{2,18},{10... | collective-permute-start | bytes 1081352 | tf_op jit(solution)/shard_map/ppermute | solution.py:464
  91.4 23.9 %collective-permute-start.4 = (bf16[2,128,1408]{1,2,0:T(8,128)(2,1)S(1)}, bf16[2,128,1408]{1,2,0:T(8,128)(2,1)}, u32[]{:S(2)}, u32[]{:S(2)}) collective-permute-start(bf16[2,128,1408]{1,2,0:T(8,128)(2,1)S(1)} %pad_maximum_fusion.2), channel_id=1, source_target_pairs={{0,8},{8,0},{16,24},{24,16},{1,9},{9,1},{17,25},{25,17},{2,10},{10... | collective-permute-start | bytes 2162696 | tf_op jit(solution)/shard_map/ppermute | solution.py:464
  93.6 23.2 %copy-start.79 = (s32[8]{0:T(128)}, s32[8]{0:T(128)S(1)}, u32[]{:S(2)}) copy-start(s32[8]{0:T(128)S(1)} %multiply_add_fusion.8) | copy-start | bytes 100
  100.3 26.2 %collective-permute-start = (bf16[1,320,896]{2,1,0:T(8,128)(2,1)S(1)}, bf16[1,320,896]{2,1,0:T(8,128)(2,1)S(1)}, u32[]{:S(2)}, u32[]{:S(2)}) collective-permute-start(bf16[1,320,896]{2,1,0:T(8,128)(2,1)S(1)} %get-tuple-element.94), channel_id=1, source_target_pairs={{0,16},{8,24},{16,0},{24,8},{1,17},{9,25},{17,1},{25,9},{2,18},{10... | collective-permute-start | bytes 1720328 | tf_op jit(solution)/shard_map/ppermute | solution.py:521
  116.8 305.8 %copy-start.59 = (f32[8,4,128]{2,0,1:T(8,128)}, f32[8,4,128]{2,0,1:T(8,128)S(1)}, u32[]{:S(2)}) copy-start(f32[8,4,128]{2,0,1:T(8,128)S(1)} %fusion.99) | copy-start | bytes 49156
  121.3 89.3 %all-to-all-start.2 = ((bf16[8,4,48,1408]{3,2,1,0:T(8,128)(2,1)}), bf16[8,4,48,1408]{3,2,1,0:T(8,128)(2,1)}, u32[]{:S(2)}, u32[]{:S(2)}) async-start(bf16[8,4,48,1408]{3,2,1,0:T(8,128)(2,1)} %copy.329), calls=%async_computation.2 | async-start | bytes 8650752 | tf_op jit(solution)/shard_map/all_to_all | solution.py:584
  126.0 152.2 %all-gather.10.cloned.1.call-start = ((), (), s32[]{:S(2)}) async-start(), calls=%async_computation.17 | async-start | bytes 2211840 | tf_op jit(solution)/shard_map/all_gather | solution.py:564
  126.5 27.7 %collective-permute-start.5 = (bf16[1,320,896]{2,1,0:T(8,128)(2,1)}, bf16[1,320,896]{2,1,0:T(8,128)(2,1)}, u32[]{:S(2)}, u32[]{:S(2)}) collective-permute-start(bf16[1,320,896]{2,1,0:T(8,128)(2,1)} %get-tuple-element.100), channel_id=1, source_target_pairs={{0,16},{8,24},{16,0},{24,8},{1,17},{9,25},{17,1},{25,9},{2,18},{10... | collective-permute-start | bytes 1720328 | tf_op jit(solution)/shard_map/ppermute | solution.py:521
  135.8 40.5 %copy-start.50 = (f32[3,40,896]{2,1,0:T(8,128)S(1)}, f32[3,40,896]{2,1,0:T(8,128)}, u32[]{:S(2)}) copy-start(f32[3,40,896]{2,1,0:T(8,128)} %param.27) | copy-start | bytes 1290244
  154.2 16.5 %collective-permute-start.6 = (bf16[1,128,1280]{2,1,0:T(8,128)(2,1)S(1)}, bf16[1,128,1280]{2,1,0:T(8,128)(2,1)S(1)}, u32[]{:S(2)}, u32[]{:S(2)}) collective-permute-start(bf16[1,128,1280]{2,1,0:T(8,128)(2,1)S(1)} %bitcast.307), channel_id=1, source_target_pairs={{0,16},{8,24},{16,0},{24,8},{1,17},{9,25},{17,1},{25,9},{2,18},{10... | collective-permute-start | bytes 983048 | tf_op jit(solution)/shard_map/ppermute | solution.py:464
  172.3 36.0 %collective-permute-start.7 = (bf16[2,128,1280]{2,1,0:T(8,128)(2,1)}, bf16[2,128,1280]{2,1,0:T(8,128)(2,1)}, u32[]{:S(2)}, u32[]{:S(2)}) collective-permute-start(bf16[2,128,1280]{2,1,0:T(8,128)(2,1)} %pad_maximum_fusion.3), channel_id=1, source_target_pairs={{0,8},{8,0},{16,24},{24,16},{1,9},{9,1},{17,25},{25,17},{2,10},{10... | collective-permute-start | bytes 1966088 | tf_op jit(solution)/shard_map/ppermute | solution.py:464
  175.6 35.0 %collective-permute-start.8 = (bf16[1,320,896]{2,1,0:T(8,128)(2,1)}, bf16[1,320,896]{2,1,0:T(8,128)(2,1)}, u32[]{:S(2)}, u32[]{:S(2)}) collective-permute-start(bf16[1,320,896]{2,1,0:T(8,128)(2,1)} %get-tuple-element.102), channel_id=1, source_target_pairs={{0,24},{8,16},{16,8},{24,0},{1,25},{9,17},{17,9},{25,1},{2,26},{10... | collective-permute-start | bytes 1720328 | tf_op jit(solution)/shard_map/ppermute | solution.py:521
  176.5 31.0 %collective-permute-start.17 = (bf16[3,40,224]{2,1,0:T(8,128)(2,1)S(1)}, bf16[3,40,224]{2,1,0:T(8,128)(2,1)S(1)}, u32[]{:S(2)}, u32[]{:S(2)}) collective-permute-start(bf16[3,40,224]{2,1,0:T(8,128)(2,1)S(1)} %get-tuple-element.334), channel_id=1, source_target_pairs={{0,24},{8,16},{16,8},{24,0},{1,25},{9,17},{17,9},{25,1},{2,26},{10... | collective-permute-start | bytes 161288 | tf_op jit(solution)/shard_map/ppermute | solution.py:451
  177.9 29.5 %collective-permute-start.16 = (bf16[3,40,224]{2,1,0:T(8,128)(2,1)S(1)}, bf16[3,40,224]{2,1,0:T(8,128)(2,1)S(1)}, u32[]{:S(2)}, u32[]{:S(2)}) collective-permute-start(bf16[3,40,224]{2,1,0:T(8,128)(2,1)S(1)} %get-tuple-element.335), channel_id=1, source_target_pairs={{0,16},{8,24},{16,0},{24,8},{1,17},{9,25},{17,1},{25,9},{2,18},{10... | collective-permute-start | bytes 161288 | tf_op jit(solution)/shard_map/ppermute | solution.py:451
  179.8 27.7 %collective-permute-start.15 = (bf16[3,40,224]{2,1,0:T(8,128)(2,1)S(1)}, bf16[3,40,224]{2,1,0:T(8,128)(2,1)S(1)}, u32[]{:S(2)}, u32[]{:S(2)}) collective-permute-start(bf16[3,40,224]{2,1,0:T(8,128)(2,1)S(1)} %get-tuple-element.336), channel_id=1, source_target_pairs={{0,8},{8,0},{16,24},{24,16},{1,9},{9,1},{17,25},{25,17},{2,10},{10... | collective-permute-start | bytes 161288 | tf_op jit(solution)/shard_map/ppermute | solution.py:451
  215.4 67.5 %all-to-all-start.3 = ((bf16[8,4,48,1280]{3,2,1,0:T(8,128)(2,1)}), bf16[8,4,48,1280]{3,2,1,0:T(8,128)(2,1)}, u32[]{:S(2)}, u32[]{:S(2)}) async-start(bf16[8,4,48,1280]{3,2,1,0:T(8,128)(2,1)} %copy.330), calls=%async_computation.3 | async-start | bytes 7864320 | tf_op jit(solution)/shard_map/all_to_all | solution.py:584
  223.2 52.6 %collective-permute-start.9 = (bf16[2,320,896]{2,1,0:T(8,128)(2,1)}, bf16[2,320,896]{2,1,0:T(8,128)(2,1)}, u32[]{:S(2)}, u32[]{:S(2)}) collective-permute-start(bf16[2,320,896]{2,1,0:T(8,128)(2,1)} %fusion.26), channel_id=1, source_target_pairs={{0,8},{8,0},{16,24},{24,16},{1,9},{9,1},{17,25},{25,17},{2,10},{10... | collective-permute-start | bytes 3440648 | tf_op jit(solution)/shard_map/ppermute | solution.py:521
  225.4 15.3 %collective-permute-start.10 = (bf16[1,320,896]{2,1,0:T(8,128)(2,1)}, bf16[1,320,896]{2,1,0:T(8,128)(2,1)S(1)}, u32[]{:S(2)}, u32[]{:S(2)}) collective-permute-start(bf16[1,320,896]{2,1,0:T(8,128)(2,1)} %get-tuple-element.105), channel_id=1, source_target_pairs={{0,24},{8,16},{16,8},{24,0},{1,25},{9,17},{17,9},{25,1},{2,26},{10... | collective-permute-start | bytes 1720328 | tf_op jit(solution)/shard_map/ppermute | solution.py:521
  240.6 31.0 %copy-start.25 = (bf16[1,320,896]{2,1,0:T(8,128)(2,1)}, bf16[1,320,896]{2,1,0:T(8,128)(2,1)S(1)}, u32[]{:S(2)}) copy-start(bf16[1,320,896]{2,1,0:T(8,128)(2,1)S(1)} %collective-permute-done.10.rest_7_) | copy-start | bytes 1720324
  240.6 73.1 %collective-permute-start.11 = (bf16[1,320,896]{2,1,0:T(8,128)(2,1)}, bf16[1,320,896]{2,1,0:T(8,128)(2,1)}, u32[]{:S(2)}, u32[]{:S(2)}) collective-permute-start(bf16[1,320,896]{2,1,0:T(8,128)(2,1)} %get-tuple-element.111), channel_id=1, source_target_pairs={{0,8},{8,0},{16,24},{24,16},{1,9},{9,1},{17,25},{25,17},{2,10},{10... | collective-permute-start | bytes 1720328 | tf_op jit(solution)/shard_map/ppermute | solution.py:521
  265.3 48.5 %collective-permute-start.12 = (bf16[1,320,896]{2,1,0:T(8,128)(2,1)}, bf16[1,320,896]{2,1,0:T(8,128)(2,1)}, u32[]{:S(2)}, u32[]{:S(2)}) collective-permute-start(bf16[1,320,896]{2,1,0:T(8,128)(2,1)} %get-tuple-element.112), channel_id=1, source_target_pairs={{0,16},{8,24},{16,0},{24,8},{1,17},{9,25},{17,1},{25,9},{2,18},{10... | collective-permute-start | bytes 1720328 | tf_op jit(solution)/shard_map/ppermute | solution.py:521
  266.1 50.5 %collective-permute-start.13 = (bf16[1,320,896]{2,1,0:T(8,128)(2,1)}, bf16[1,320,896]{2,1,0:T(8,128)(2,1)}, u32[]{:S(2)}, u32[]{:S(2)}) collective-permute-start(bf16[1,320,896]{2,1,0:T(8,128)(2,1)} %get-tuple-element.113), channel_id=1, source_target_pairs={{0,24},{8,16},{16,8},{24,0},{1,25},{9,17},{17,9},{25,1},{2,26},{10... | collective-permute-start | bytes 1720328 | tf_op jit(solution)/shard_map/ppermute | solution.py:521
  305.0 11.6 %copy-start.11 = (bf16[1,320,896]{2,1,0:T(8,128)(2,1)S(1)}, bf16[1,320,896]{2,1,0:T(8,128)(2,1)}, u32[]{:S(2)}) copy-start(bf16[1,320,896]{2,1,0:T(8,128)(2,1)} %get-tuple-element.296.rest_8_) | copy-start | bytes 1720324
  305.0 11.6 %copy-start.14 = (bf16[1,320,896]{2,1,0:T(8,128)(2,1)S(1)}, bf16[1,320,896]{2,1,0:T(8,128)(2,1)}, u32[]{:S(2)}) copy-start(bf16[1,320,896]{2,1,0:T(8,128)(2,1)} %get-tuple-element.299.rest_0_) | copy-start | bytes 1720324
  305.0 11.6 %copy-start.16 = (bf16[1,320,896]{2,1,0:T(8,128)(2,1)S(1)}, bf16[1,320,896]{2,1,0:T(8,128)(2,1)}, u32[]{:S(2)}) copy-start(bf16[1,320,896]{2,1,0:T(8,128)(2,1)} %get-tuple-element.316.rest_5_) | copy-start | bytes 1720324
  305.0 11.6 %copy-start.18 = (bf16[1,320,896]{2,1,0:T(8,128)(2,1)S(1)}, bf16[1,320,896]{2,1,0:T(8,128)(2,1)}, u32[]{:S(2)}) copy-start(bf16[1,320,896]{2,1,0:T(8,128)(2,1)} %get-tuple-element.317.rest_1_) | copy-start | bytes 1720324
  305.0 11.6 %copy-start.24 = (bf16[1,320,896]{2,1,0:T(8,128)(2,1)S(1)}, bf16[1,320,896]{2,1,0:T(8,128)(2,1)}, u32[]{:S(2)}) copy-start(bf16[1,320,896]{2,1,0:T(8,128)(2,1)} %copy-done.22) | copy-start | bytes 1720324
  305.0 11.6 %copy-start.27 = (bf16[1,320,896]{2,1,0:T(8,128)(2,1)S(1)}, bf16[1,320,896]{2,1,0:T(8,128)(2,1)}, u32[]{:S(2)}) copy-start(bf16[1,320,896]{2,1,0:T(8,128)(2,1)} %copy-done.25) | copy-start | bytes 1720324
  344.0 9.6 %all-to-all-start.6 = ((f32[8,8,192]{2,1,0:T(8,128)}), f32[8,8,192]{2,1,0:T(8,128)S(1)}, u32[]{:S(2)}, u32[]{:S(2)}) async-start(f32[8,8,192]{2,1,0:T(8,128)} %get-tuple-element.122), calls=%async_computation.6 | async-start | bytes 131072 | tf_op jit(solution)/shard_map/all_to_all | solution.py:633
  350.7 26.6 %collective-permute-start.14 = (bf16[1,320,896]{2,1,0:T(8,128)(2,1)}, bf16[1,320,896]{2,1,0:T(8,128)(2,1)}, u32[]{:S(2)}, u32[]{:S(2)}) collective-permute-start(bf16[1,320,896]{2,1,0:T(8,128)(2,1)} %get-tuple-element.310), channel_id=1, source_target_pairs={{0,16},{8,24},{16,0},{24,8},{1,17},{9,25},{17,1},{25,9},{2,18},{10... | collective-permute-start | bytes 1720328 | tf_op jit(solution)/shard_map/ppermute | solution.py:618
  353.7 55.7 %all-to-all-start.4 = ((bf16[8,4,48,1280]{3,2,1,0:T(8,128)(2,1)}), bf16[8,4,48,1280]{3,2,1,0:T(8,128)(2,1)}, u32[]{:S(2)}, u32[]{:S(2)}) async-start(bf16[8,4,48,1280]{3,2,1,0:T(8,128)(2,1)} %bitcast.335), calls=%async_computation.4 | async-start | bytes 7864320 | tf_op jit(solution)/shard_map/all_to_all | solution.py:658
  393.8 32.0 %collective-permute-start.18 = (bf16[1,320,896]{2,1,0:T(8,128)(2,1)}, bf16[1,320,896]{2,1,0:T(8,128)(2,1)}, u32[]{:S(2)}, u32[]{:S(2)}) collective-permute-start(bf16[1,320,896]{2,1,0:T(8,128)(2,1)} %get-tuple-element.123), channel_id=1, source_target_pairs={{0,24},{8,16},{16,8},{24,0},{1,25},{9,17},{17,9},{25,1},{2,26},{10... | collective-permute-start | bytes 1720328 | tf_op jit(solution)/shard_map/ppermute | solution.py:618
  409.4 88.5 %all-to-all-start.5 = ((bf16[8,4,48,1280]{3,2,1,0:T(8,128)(2,1)}), bf16[8,4,48,1280]{3,2,1,0:T(8,128)(2,1)}, u32[]{:S(2)}, u32[]{:S(2)}) async-start(bf16[8,4,48,1280]{3,2,1,0:T(8,128)(2,1)} %bitcast.334), calls=%async_computation.5 | async-start | bytes 7864320 | tf_op jit(solution)/shard_map/all_to_all | solution.py:658
  413.9 148.8 %reduce-scatter.8.cloned.1.call-start = ((), (), s32[]{:S(2)}) async-start(), calls=%async_computation.15 | async-start | bytes 2211840 | tf_op jit(solution)/shard_map/reduce_scatter | solution.py:745
  417.3 280.9 %reduce-scatter.6.cloned.1.call-start = ((), (), s32[]{:S(2)}) async-start(), calls=%async_computation.14 | async-start | bytes 4055040 | tf_op jit(solution)/shard_map/reduce_scatter | solution.py:679
  425.9 29.3 %collective-permute-start.19 = (bf16[2,128,1280]{2,1,0:T(8,128)(2,1)S(1)}, bf16[2,128,1280]{2,1,0:T(8,128)(2,1)S(1)}, u32[]{:S(2)}, u32[]{:S(2)}) collective-permute-start(bf16[2,128,1280]{2,1,0:T(8,128)(2,1)S(1)} %split.37), channel_id=1, source_target_pairs={{0,8},{8,0},{16,24},{24,16},{1,9},{9,1},{17,25},{25,17},{2,10},{10... | collective-permute-start | bytes 1966088 | tf_op jit(solution)/shard_map/ppermute | solution.py:471
  432.4 27.0 %copy-start.34 = (bf16[1280,512]{1,0:T(8,128)(2,1)S(1)}, bf16[1280,512]{1,0:T(8,128)(2,1)}, u32[]{:S(2)}) copy-start(bf16[1280,512]{1,0:T(8,128)(2,1)} %copy.345) | copy-start | bytes 3932164
  432.4 65.5 %collective-permute-start.21 = (bf16[2,320,896]{2,1,0:T(8,128)(2,1)}, bf16[2,320,896]{2,1,0:T(8,128)(2,1)}, u32[]{:S(2)}, u32[]{:S(2)}) collective-permute-start(bf16[2,320,896]{2,1,0:T(8,128)(2,1)} %get-tuple-element.125), channel_id=1, source_target_pairs={{0,16},{8,24},{16,0},{24,8},{1,17},{9,25},{17,1},{25,9},{2,18},{10... | collective-permute-start | bytes 3440648 | tf_op jit(solution)/shard_map/ppermute | solution.py:618
  456.2 40.5 %collective-permute-start.20 = (bf16[1,128,1280]{2,1,0:T(8,128)(2,1)S(1)}, bf16[1,128,1280]{2,1,0:T(8,128)(2,1)}, u32[]{:S(2)}, u32[]{:S(2)}) collective-permute-start(bf16[1,128,1280]{2,1,0:T(8,128)(2,1)S(1)} %split.49), channel_id=1, source_target_pairs={{0,16},{8,24},{16,0},{24,8},{1,17},{9,25},{17,1},{25,9},{2,18},{10... | collective-permute-start | bytes 983048 | tf_op jit(solution)/shard_map/ppermute | solution.py:471
  517.7 21.2 %copy-start.38 = (bf16[32,40,512]{2,1,0:T(8,128)(2,1)S(1)}, bf16[32,40,512]{2,1,0:T(8,128)(2,1)}, u32[]{:S(2)}) copy-start(bf16[32,40,512]{2,1,0:T(8,128)(2,1)} %copy-done.37) | copy-start | bytes 3932164
  517.7 183.6 %reduce-scatter.4.cloned.1.call-start = ((), (), s32[]{:S(2)}) async-start(), calls=%async_computation.13 | async-start | bytes 2949120 | tf_op jit(solution)/shard_map/reduce_scatter | solution.py:705
  547.7 125.1 %all-to-all-start.8 = ((bf16[32,40,512]{2,1,0:T(8,128)(2,1)}), bf16[32,40,512]{2,1,0:T(8,128)(2,1)S(1)}, u32[]{:S(2)}, u32[]{:S(2)}) async-start(bf16[32,40,512]{2,1,0:T(8,128)(2,1)} %bitcast.351), calls=%async_computation.9 | async-start | bytes 2621440 | tf_op jit(solution)/shard_map/all_to_all | solution.py:698
  558.9 33.3 %collective-permute-start.22 = (bf16[2,128,1280]{2,1,0:T(8,128)(2,1)S(1)}, bf16[2,128,1280]{2,1,0:T(8,128)(2,1)}, u32[]{:S(2)}, u32[]{:S(2)}) collective-permute-start(bf16[2,128,1280]{2,1,0:T(8,128)(2,1)S(1)} %split.41), channel_id=1, source_target_pairs={{0,8},{8,0},{16,24},{24,16},{1,9},{9,1},{17,25},{25,17},{2,10},{10... | collective-permute-start | bytes 1966088 | tf_op jit(solution)/shard_map/ppermute | solution.py:471
  560.5 75.0 %collective-permute-start.31 = (bf16[2,320,896]{2,1,0:T(8,128)(2,1)}, bf16[2,320,896]{2,1,0:T(8,128)(2,1)}, u32[]{:S(2)}, u32[]{:S(2)}) collective-permute-start(bf16[2,320,896]{2,1,0:T(8,128)(2,1)} %get-tuple-element.138), channel_id=1, source_target_pairs={{0,24},{8,16},{16,8},{24,0},{1,25},{9,17},{17,9},{25,1},{2,26},{10... | collective-permute-start | bytes 3440648 | tf_op jit(solution)/shard_map/ppermute | solution.py:618
  564.3 105.2 %collective-permute-start.28 = (bf16[3,40,224]{2,1,0:T(8,128)(2,1)S(1)}, bf16[3,40,224]{2,1,0:T(8,128)(2,1)S(1)}, u32[]{:S(2)}, u32[]{:S(2)}) collective-permute-start(bf16[3,40,224]{2,1,0:T(8,128)(2,1)S(1)} %get-tuple-element.329), channel_id=1, source_target_pairs={{0,24},{8,16},{16,8},{24,0},{1,25},{9,17},{17,9},{25,1},{2,26},{10... | collective-permute-start | bytes 161288 | tf_op jit(solution)/shard_map/ppermute | solution.py:451
  566.4 102.7 %collective-permute-start.27 = (bf16[3,40,224]{2,1,0:T(8,128)(2,1)S(1)}, bf16[3,40,224]{2,1,0:T(8,128)(2,1)S(1)}, u32[]{:S(2)}, u32[]{:S(2)}) collective-permute-start(bf16[3,40,224]{2,1,0:T(8,128)(2,1)S(1)} %get-tuple-element.330), channel_id=1, source_target_pairs={{0,16},{8,24},{16,0},{24,8},{1,17},{9,25},{17,1},{25,9},{2,18},{10... | collective-permute-start | bytes 161288 | tf_op jit(solution)/shard_map/ppermute | solution.py:451
  568.6 98.9 %collective-permute-start.26 = (bf16[3,40,224]{2,1,0:T(8,128)(2,1)}, bf16[3,40,224]{2,1,0:T(8,128)(2,1)}, u32[]{:S(2)}, u32[]{:S(2)}) collective-permute-start(bf16[3,40,224]{2,1,0:T(8,128)(2,1)} %get-tuple-element.331), channel_id=1, source_target_pairs={{0,8},{8,0},{16,24},{24,16},{1,9},{9,1},{17,25},{25,17},{2,10},{10... | collective-permute-start | bytes 161288 | tf_op jit(solution)/shard_map/ppermute | solution.py:451
  592.1 87.8 %collective-permute-start.29 = (bf16[2,320,896]{2,1,0:T(8,128)(2,1)}, bf16[2,320,896]{2,1,0:T(8,128)(2,1)}, u32[]{:S(2)}, u32[]{:S(2)}) collective-permute-start(bf16[2,320,896]{2,1,0:T(8,128)(2,1)} %get-tuple-element.134), channel_id=1, source_target_pairs={{0,8},{8,0},{16,24},{24,16},{1,9},{9,1},{17,25},{25,17},{2,10},{10... | collective-permute-start | bytes 3440648 | tf_op jit(solution)/shard_map/ppermute | solution.py:625
  635.5 40.7 %collective-permute-start.23 = (bf16[1,128,1280]{2,1,0:T(8,128)(2,1)}, bf16[1,128,1280]{2,1,0:T(8,128)(2,1)}, u32[]{:S(2)}, u32[]{:S(2)}) collective-permute-start(bf16[1,128,1280]{2,1,0:T(8,128)(2,1)} %split.51), channel_id=1, source_target_pairs={{0,16},{8,24},{16,0},{24,8},{1,17},{9,25},{17,1},{25,9},{2,18},{10... | collective-permute-start | bytes 983048 | tf_op jit(solution)/shard_map/ppermute | solution.py:471
  672.8 15.7 %collective-permute-start.30 = (bf16[1,320,896]{2,1,0:T(8,128)(2,1)}, bf16[1,320,896]{2,1,0:T(8,128)(2,1)}, u32[]{:S(2)}, u32[]{:S(2)}) collective-permute-start(bf16[1,320,896]{2,1,0:T(8,128)(2,1)} %get-tuple-element.136), channel_id=1, source_target_pairs={{0,8},{8,0},{16,24},{24,16},{1,9},{9,1},{17,25},{25,17},{2,10},{10... | collective-permute-start | bytes 1720328 | tf_op jit(solution)/shard_map/ppermute | solution.py:625
  699.5 12.2 %copy-start.61 = (f32[40,32]{1,0:T(8,128)S(1)}, f32[40,32]{1,0:T(8,128)}, u32[]{:S(2)}) copy-start(f32[40,32]{1,0:T(8,128)} %copy.352) | copy-start | bytes 15364
  699.5 12.2 %copy-start.62 = (f32[40,32]{1,0:T(8,128)S(1)}, f32[40,32]{1,0:T(8,128)}, u32[]{:S(2)}) copy-start(f32[40,32]{1,0:T(8,128)} %copy.351) | copy-start | bytes 15364
  699.5 12.2 %copy-start.63 = (f32[40,32]{1,0:T(8,128)S(1)}, f32[40,32]{1,0:T(8,128)}, u32[]{:S(2)}) copy-start(f32[40,32]{1,0:T(8,128)} %copy.354) | copy-start | bytes 15364
  699.5 6.0 collective-permute-start.24
  702.6 11.8 %copy-start.43 = (f32[4,40,1280]{2,1,0:T(8,128)S(1)}, f32[4,40,1280]{2,1,0:T(8,128)}, u32[]{:S(2)}) copy-start(f32[4,40,1280]{2,1,0:T(8,128)} %param.24) | copy-start | bytes 2457604
  702.6 11.8 %copy-start.78 = (f32[4]{0:T(128)S(1)}, f32[4]{0:T(128)}, u32[]{:S(2)}) copy-start(f32[4]{0:T(128)} %constant.188.clone) | copy-start | bytes 52
  705.7 5.8 collective-permute-start.25
  (64 other events, 223.0 us)
Sparse Core Ops, SparseCore 0:
  10.5 40.8 all-gather.5
  53.8 41.7 all-gather.7
  208.4 44.9 all-gather.9
  418.4 55.8 reduce-scatter.7
  517.8 56.1 reduce-scatter.5
  577.5 43.5 reduce-scatter.3
